TPU v7x, 32 devices: a whole 2x2x4 slice. The times are simulated.
32 devices in a mesh: dp: 8 (over z, x), tensor: 4 (over y, core).
Axes of the slice: x: 2, y: 2, z: 4, core: 2. Of those that a mesh axis runs over, the one named last changes fastest.
Arguments:
- hidden: bfloat16 [2048, 2, 8192], P('dp', None, 'tensor'), may hold values from -6 to 6
- key_value_weight: bfloat16 [8192, 2048], P('tensor'), may hold values from -0.0625 to 0.0625
- adapter_down_weight: bfloat16 [128, 8192, 64], P('dp', 'tensor'), may hold values from -0.0625 to 0.0625
- adapter_up_weight: bfloat16 [128, 64, 2048], P('dp', None, 'tensor'), may hold values from -0.75 to 0.75
- attempt_adapter_slot: int32 [2048, 1], P('dp'), may hold values from 0 to 7; in each aligned block of 256 rows (0 to 255, 256 to 511, ...) at most 128 rows name the same one
- group_slot_task: int32 [8, 8], replicated, may hold values from 0 to 127, as said below
- task_row_position: int32 [128], replicated, may hold values from 0 to 127, as said below
- scores: int32 [2048], P('dp'), may hold values 0 or 1
- cotangent: bfloat16 [2048, 2, 2048], P('dp', None, 'tensor'), may hold values from -6 to 6
Outputs:
- kv_new: bfloat16 [2048, 2, 2048], P('dp', None, 'tensor')
- grad_down: bfloat16 [128, 8192, 64], P('dp', 'tensor')
- grad_up: bfloat16 [128, 64, 2048], P('dp', None, 'tensor')
Inputs may be any that keep to these rules, and one draw needn't show every extreme that they name: `attempt_adapter_slot`: among the 256 attempts of one group (aligned blocks of 256 rows), at most 128 name the same slot, and exactly 128 do in some block. `task_row_position`: every row is named once; rows o * 16 to (o + 1) * 16 - 1 belong to group o. group_slot_task[g, o] is a task t with task_row_position[t] between o * 16 and (o + 1) * 16 - 1.
All inputs are finite; a program needn't handle non-finite values. No bound on the sum of `scores` on one device may be relied on, other than what follows from the above.
Results may differ from a plain program's by a relative error of at most 0.0057.
Values may be sent and summed in bfloat16 or wider, within the bound.
No kernel may reach another device: no remote copies, remote signals or barrier semaphores. Data moves between devices by JAX's collectives and lax.ppermute only.
A program may use at most 64 MiB of HBM per device.

v0:
```python
import jax
import jax.numpy as jnp
from jax import lax
from jax.sharding import PartitionSpec as P

adapter_output_scale = 0.25
precise = lax.Precision.HIGHEST


def rank_totals(down_part, back_part):
    return lax.psum((down_part, back_part), "tensor")


def body(
    hidden,
    key_value_weight,
    adapter_down_weight,
    adapter_up_weight,
    attempt_adapter_slot,
    group_slot_task,
    task_row_position,
    scores,
    cotangent,
):
    group_total = lax.axis_size("dp")
    my_group = lax.axis_index("dp")
    att_rows, step_count, width_part = hidden.shape
    task_on_device = adapter_down_weight.shape[0]
    tasks_all = task_row_position.shape[0]
    kv_part = cotangent.shape[2]
    row_count = att_rows * step_count
    slot_ids = jnp.arange(group_total, dtype=jnp.int32)
    slot_of = attempt_adapter_slot[:, 0]
    slot_hot = slot_of[:, None] == slot_ids[None, :]
    my_tasks = lax.dynamic_index_in_dim(group_slot_task, my_group, 0, keepdims=False)
    task_of = jnp.sum(jnp.where(slot_hot, my_tasks[None, :], 0), axis=1)
    task_ids = jnp.arange(tasks_all, dtype=jnp.int32)
    task_hot = (task_of[:, None] == task_ids[None, :]).astype(jnp.float32)
    score_f = scores.astype(jnp.float32)
    sums_local = jnp.dot(score_f, task_hot, precision=precise)
    counts_local = jnp.sum(task_hot, axis=0)
    score_sums, task_counts = lax.psum((sums_local, counts_local), "dp")
    task_means = score_sums / jnp.maximum(task_counts, 1.0)
    advantage = score_f - jnp.dot(task_hot, task_means, precision=precise)
    weighted = (advantage[:, None, None] * cotangent.astype(jnp.float32)).astype(jnp.bfloat16)
    served = lax.dynamic_index_in_dim(group_slot_task, my_group, 1, keepdims=False)
    stored = jnp.sum(
        jnp.where(served[:, None] == task_ids[None, :], task_row_position[None, :], 0), axis=1
    )
    slot_on_device = stored % task_on_device
    picker = (
        slot_on_device[:, None] == jnp.arange(task_on_device, dtype=jnp.int32)[None, :]
    ).astype(jnp.float32)
    flat_rows = hidden.reshape(row_count, width_part)
    base_terms = jnp.dot(flat_rows, key_value_weight, preferred_element_type=jnp.float32)
    base_rows = lax.psum_scatter(base_terms, "tensor", scatter_dimension=1, tiled=True)
    weighted_rows = weighted.reshape(row_count, kv_part)
    outgoing_down_weight = jnp.take(adapter_down_weight, slot_on_device, axis=0)
    outgoing_up_weight = jnp.take(adapter_up_weight, slot_on_device, axis=0)
    got_down, got_up = (
        lax.all_to_all(outgoing_down_weight, "dp", split_axis=0, concat_axis=0, tiled=True),
        lax.all_to_all(outgoing_up_weight, "dp", split_axis=0, concat_axis=0, tiled=True),
    )
    row_hot = jnp.repeat(slot_hot, step_count, axis=0)
    row_mask = row_hot.astype(jnp.float32)
    down_all = jnp.einsum("nd,sdr->nsr", flat_rows, got_down, preferred_element_type=jnp.float32)
    back_all = jnp.einsum("nk,srk->nsr", weighted_rows, got_up, preferred_element_type=jnp.float32)
    down_part = jnp.sum(down_all * row_mask[:, :, None], axis=1)
    back_part = jnp.sum(back_all * row_mask[:, :, None], axis=1)
    down_total, back_total = rank_totals(down_part, back_part)
    zero_bf = jnp.zeros((), jnp.bfloat16)
    down_spread = jnp.where(
        row_hot[:, :, None], down_total.astype(jnp.bfloat16)[:, None, :], zero_bf
    )
    back_spread = jnp.where(
        row_hot[:, :, None], back_total.astype(jnp.bfloat16)[:, None, :], zero_bf
    )
    adapter_delta_rows = (
        adapter_output_scale
        * jnp.einsum("nsr,srk->nk", down_spread, got_up, preferred_element_type=jnp.float32)
    ).astype(jnp.bfloat16)
    down_gradient_sender = adapter_output_scale * jnp.einsum(
        "nd,nsr->sdr", flat_rows, back_spread, preferred_element_type=jnp.float32
    )
    up_gradient_sender = adapter_output_scale * jnp.einsum(
        "nsr,nk->srk", down_spread, weighted_rows, preferred_element_type=jnp.float32
    )
    got_grad_down, got_grad_up = (
        lax.all_to_all(down_gradient_sender, "dp", split_axis=0, concat_axis=0, tiled=True),
        lax.all_to_all(up_gradient_sender, "dp", split_axis=0, concat_axis=0, tiled=True),
    )
    kv_new = (base_rows + adapter_delta_rows.astype(jnp.float32)).astype(jnp.bfloat16)
    kv_new = kv_new.reshape(att_rows, step_count, kv_part)
    grad_down = jnp.einsum("st,sdr->tdr", picker, got_grad_down, precision=precise).astype(
        jnp.bfloat16
    )
    grad_up = jnp.einsum("st,srk->trk", picker, got_grad_up, precision=precise).astype(jnp.bfloat16)
    return (kv_new, grad_down, grad_up)


def solution(mesh):
    in_specs = (
        P("dp", None, "tensor"),
        P("tensor", None),
        P("dp", "tensor", None),
        P("dp", None, "tensor"),
        P("dp", None),
        P(),
        P(),
        P("dp"),
        P("dp", None, "tensor"),
    )
    out_specs = (P("dp", None, "tensor"), P("dp", "tensor", None), P("dp", None, "tensor"))
    return jax.shard_map(body, mesh=mesh, in_specs=in_specs, out_specs=out_specs, check_vma=False)
```

profile of v0, /device:TPU:0, one launch (start us, length us, event | category | flops | bytes accessed | tf_op | source)
XLA Modules:
  0.0 266.5 jit_solution(2627566661466499699)
XLA Ops:
  7.2 1.0 dynamic-slice_reduce_fusion
  8.1 0.8 select_reduce_fusion.1
  9.6 0.9 broadcast_select_fusion.1
  10.5 7.3 %all-to-all-start.1 = ((bf16[8,64,512]{2,1,0:T(8,128)(2,1)}), bf16[8,64,512]{2,1,0:T(8,128)(2,1)}, u32[]{:S(2)}, u32[]{:S(2)}) async-start(bf16[8,64,512]{2,1,0:T(8,128)(2,1)} %broadcast_select_fusion.1), calls=%async_computation.2 | async-start | bytes 1048576 | tf_op jit(solution)/shard_map/all_to_all | solution.py:62
  17.8 2.9 %gather_fusion = bf16[8,2048,64]{1,2,0:T(8,128)(2,1)S(1)} fusion(bf16[16,2048,64]{1,2,0:T(8,128)(2,1)} %param.11, s32[1024]{0:T(1024)S(1)} %pad_clamp_fusion), kind=kCustom, calls=%fused_computation | custom fusion | bytes 4194336 | tf_op jit(solution)/shard_map/jit(_take)/gather | solution.py:58
  20.7 1.6 broadcast_select_fusion
  22.2 10.2 %all-to-all-done.1 = bf16[8,64,512]{2,1,0:T(8,128)(2,1)} async-done(((bf16[8,64,512]{2,1,0:T(8,128)(2,1)}), bf16[8,64,512]{2,1,0:T(8,128)(2,1)}, u32[]{:S(2)}, u32[]{:S(2)}) %all-to-all-start.1) | async-done | bytes 524320 | tf_op jit(solution)/shard_map/all_to_all | solution.py:62
  32.4 4.3 %all-to-all-start = ((bf16[8,2048,64]{1,2,0:T(8,128)(2,1)}), bf16[8,2048,64]{1,2,0:T(8,128)(2,1)}, u32[]{:S(2)}, u32[]{:S(2)}) async-start(bf16[8,2048,64]{1,2,0:T(8,128)(2,1)} %broadcast_select_fusion), calls=%async_computation.1 | async-start | bytes 4194304 | tf_op jit(solution)/shard_map/all_to_all | solution.py:61
  36.8 2.2 reshape.80
  39.0 10.5 %fusion.44 = f32[512,2048]{1,0:T(8,128)} fusion(bf16[512,2048]{1,0:T(8,128)(2,1)} %reshape.80, bf16[2048,2048]{1,0:T(8,128)(2,1)} %param.10), kind=kOutput, calls=%fused_computation.73 | convolution fusion | flops 4294967296 | bytes 14680064 | tf_op jit(solution)/shard_map/dot_general | solution.py:55
  49.6 2.2 reshape.99
  52.5 0.7 dynamic-slice_bitcast_fusion
  53.7 32.0 %all-reduce = (f32[128]{0:T(128)S(1)}, f32[128]{0:T(128)S(1)}) all-reduce(f32[128]{0:T(128)S(1)} %convolution_bitcast_fusion.2, f32[128]{0:T(128)S(1)} %convert_reduce_fusion), channel_id=1, replica_groups=mesh['dp'=8,'tensor'=4] {'dp'}, use_global_device_ids=true, to_apply=%region_5.6 | all-reduce | flops 256 | bytes 2048 | tf_op jit(solution)/shard_map/psum | solution.py:42
  86.0 2.4 multiply_convert_fusion
  88.3 2.0 reshape.105
  90.4 1.7 fusion.12
  92.1 2.9 %fusion.11 = f32[512,64]{0,1:T(8,128)S(1)} fusion(bf16[8,2048,64]{1,2,0:T(8,128)(2,1)} %all-to-all-done, bf16[512,2048,1]{1,0,2:T(8,128)(2,1)S(1)} %copy-done.2, f32[512,8]{0,1:T(8,128)S(1)} %copy.47), kind=kOutput, calls=%fused_computation.18 | convolution fusion | flops 1074233344 | bytes 4341760 | tf_op jit(solution)/shard_map/nd,sdr->nsr/dot_general | solution.py:66
  95.0 13.0 %all-reduce.3 = (bf16[512,64]{0,1:T(8,128)(2,1)S(1)}, bf16[512,64]{0,1:T(8,128)(2,1)S(1)}) all-reduce(f32[512,64]{0,1:T(8,128)S(1)} %fusion.11, f32[512,64]{0,1:T(8,128)S(1)} %fusion.12), channel_id=1, replica_groups=mesh['dp'=8,'tensor'=4] {'tensor'}, use_global_device_ids=true, to_apply=%region_3.4 | all-reduce | flops 65536 | bytes 393216 | tf_op jit(solution)/shard_map/psum | solution.py:11
  108.0 1.5 convolution_multiply_fusion
  109.5 1.6 copy.51
  111.1 10.7 %all-to-all-start.3 = ((f32[8,64,512]{2,1,0:T(8,128)}), f32[8,64,512]{2,1,0:T(8,128)}, u32[]{:S(2)}, u32[]{:S(2)}) async-start(f32[8,64,512]{2,1,0:T(8,128)} %copy.51), calls=%async_computation.4 | async-start | bytes 2097152 | tf_op jit(solution)/shard_map/all_to_all | solution.py:90
  121.8 1.3 multiply_bitcast_fusion
  123.1 4.4 %copy.49 = f32[8,2048,64]{1,2,0:T(8,128)} copy(f32[8,2048,64]{1,0,2:T(8,128)S(1)} %multiply_bitcast_fusion) | data formatting | bytes 8388608 | tf_op jit(solution)/shard_map/mul | solution.py:82
  127.5 21.9 %all-to-all-done.3 = f32[8,64,512]{2,1,0:T(8,128)} async-done(((f32[8,64,512]{2,1,0:T(8,128)}), f32[8,64,512]{2,1,0:T(8,128)}, u32[]{:S(2)}, u32[]{:S(2)}) %all-to-all-start.3) | async-done | bytes 1048608 | tf_op jit(solution)/shard_map/all_to_all | solution.py:90
  149.4 4.5 %all-to-all-start.2 = ((f32[8,2048,64]{1,2,0:T(8,128)}), f32[8,2048,64]{1,2,0:T(8,128)}, u32[]{:S(2)}, u32[]{:S(2)}) async-start(f32[8,2048,64]{1,2,0:T(8,128)} %copy.49), calls=%async_computation.3 | async-start | bytes 8388608 | tf_op jit(solution)/shard_map/all_to_all | solution.py:89
  154.0 2.7 %convolution_convert_fusion = bf16[16,64,512]{2,0,1:T(8,128)(2,1)S(1)} fusion(f32[8,64,512]{2,1,0:T(8,128)} %all-to-all-done.3, s32[8]{0:T(128)S(1)} %get-tuple-element.26), kind=kOutput, calls=%fused_computation.7 | convolution fusion | flops 50856064 | bytes 2097184 | tf_op jit(solution)/shard_map/st,srk->trk/dot_general | solution.py:97
  156.7 1.5 copy.54
  158.2 2.0 fusion.10
  160.2 1.0 reshape.81
  161.2 86.4 %all-to-all-done.2 = f32[8,2048,64]{1,2,0:T(8,128)} async-done(((f32[8,2048,64]{1,2,0:T(8,128)}), f32[8,2048,64]{1,2,0:T(8,128)}, u32[]{:S(2)}, u32[]{:S(2)}) %all-to-all-start.2) | async-done | bytes 4194336 | tf_op jit(solution)/shard_map/all_to_all | solution.py:89
  247.6 7.7 %fusion.2 = bf16[16,2048,64]{1,0,2:T(8,128)(2,1)S(1)} fusion(f32[8,2048,64]{1,2,0:T(8,128)} %all-to-all-done.2, s32[8]{0:T(128)S(1)} %get-tuple-element.26), kind=kOutput, calls=%fused_computation.5 | convolution fusion | flops 203423872 | bytes 8388640 | tf_op jit(solution)/shard_map/st,sdr->tdr/dot_general | solution.py:94
  255.3 4.3 %copy.53 = bf16[16,2048,64]{1,2,0:T(8,128)(2,1)} copy(bf16[16,2048,64]{1,0,2:T(8,128)(2,1)S(1)} %fusion.2) | data formatting | bytes 8388608
  (30 shorter events, 2.1 us)
Async XLA Ops:
  7.2 1.9 copy-start
  10.5 21.8 %all-to-all-start.1 = ((bf16[8,64,512]{2,1,0:T(8,128)(2,1)}), bf16[8,64,512]{2,1,0:T(8,128)(2,1)}, u32[]{:S(2)}, u32[]{:S(2)}) async-start(bf16[8,64,512]{2,1,0:T(8,128)(2,1)} %broadcast_select_fusion.1), calls=%async_computation.2 | async-start | bytes 1048576 | tf_op jit(solution)/shard_map/all_to_all | solution.py:62
  22.2 14.6 %copy-start.1 = (bf16[256,2,2048]{2,1,0:T(2,128)(2,1)S(1)}, bf16[256,2,2048]{2,1,0:T(2,128)(2,1)}, u32[]{:S(2)}) copy-start(bf16[256,2,2048]{2,1,0:T(2,128)(2,1)} %param.9) | copy-start | bytes 6291460
  32.4 59.7 %all-to-all-start = ((bf16[8,2048,64]{1,2,0:T(8,128)(2,1)}), bf16[8,2048,64]{1,2,0:T(8,128)(2,1)}, u32[]{:S(2)}, u32[]{:S(2)}) async-start(bf16[8,2048,64]{1,2,0:T(8,128)(2,1)} %broadcast_select_fusion), calls=%async_computation.1 | async-start | bytes 4194304 | tf_op jit(solution)/shard_map/all_to_all | solution.py:61
  36.7 121.5 %reduce-scatter.2.cloned.1.call-start = ((), (), s32[]{:S(2)}) async-start(), calls=%async_computation.5 | async-start | bytes 5242880 | tf_op jit(solution)/shard_map/reduce_scatter | solution.py:56
  49.6 2.3 copy-start.3
  49.6 2.9 %copy-start.4 = (s32[256]{0:T(256)S(1)}, s32[256]{0:T(256)}, u32[]{:S(2)}) copy-start(s32[256]{0:T(256)} %param.16) | copy-start | bytes 3076
  51.8 40.2 %copy-start.2 = (bf16[512,2048,1]{1,0,2:T(8,128)(2,1)S(1)}, bf16[512,2048,1]{1,0,2:T(8,128)(2,1)}, u32[]{:S(2)}) copy-start(bf16[512,2048,1]{1,0,2:T(8,128)(2,1)} %reshape.99) | copy-start | bytes 6291460
  111.1 38.3 %all-to-all-start.3 = ((f32[8,64,512]{2,1,0:T(8,128)}), f32[8,64,512]{2,1,0:T(8,128)}, u32[]{:S(2)}, u32[]{:S(2)}) async-start(f32[8,64,512]{2,1,0:T(8,128)} %copy.51), calls=%async_computation.4 | async-start | bytes 2097152 | tf_op jit(solution)/shard_map/all_to_all | solution.py:90
  149.4 98.2 %all-to-all-start.2 = ((f32[8,2048,64]{1,2,0:T(8,128)}), f32[8,2048,64]{1,2,0:T(8,128)}, u32[]{:S(2)}, u32[]{:S(2)}) async-start(f32[8,2048,64]{1,2,0:T(8,128)} %copy.49), calls=%async_computation.3 | async-start | bytes 8388608 | tf_op jit(solution)/shard_map/all_to_all | solution.py:89
Sparse Core Ops, SparseCore 0:
  49.7 45.8 reduce-scatter.1
where the time goes:
time: 267 us; the launch traced here: 266 us
  waiting for transfers between devices  118 us (44%)
  blocking collectives  45.1 us (17%)
  matrix products  30.7 us (11%)
  starting transfers between devices  26.9 us (10%)
  local copies, waits for them, and re-layouts  25 us (9%)
  between operations  14.2 us (5%)
  other arithmetic  6.16 us (2%)
    all_to_all x1, waiting for transfers between devices, body(): lax.all_to_all(down_gradient_sender, 'dp', split_axis=0, concat_axis=0, t...  86.4 us
    psum x1, blocking collectives, body(): score_sums, task_counts = lax.psum((sums_local, counts_local), 'dp')  32 us
    all_to_all x1, waiting for transfers between devices, body(): lax.all_to_all(up_gradient_sender, 'dp', split_axis=0, concat_axis=0, til...  21.9 us
    psum x1, blocking collectives, rank_totals(): return lax.psum((down_part, back_part), 'tensor')  13 us
    all_to_all x1, starting transfers between devices, body(): lax.all_to_all(up_gradient_sender, 'dp', split_axis=0, concat_axis=0, til...  10.7 us
    dot_general x1, matrix products, body(): jnp.dot(flat_rows, key_value_weight, preferred_element_type=jnp.float32)  10.5 us
    all_to_all x1, waiting for transfers between devices, body(): lax.all_to_all(outgoing_up_weight, 'dp', split_axis=0, concat_axis=0, til...  10.2 us
    dot_general x1, matrix products, body(): jnp.einsum('st,sdr->tdr', picker, got_grad_down, precision=precise)  7.72 us
  transfers between devices with their start and end apart: 5, of which 3 were waited for; matrix products, arithmetic and copies ran while one was open for 17% of the time, Pallas kernels for 0%

commit v1 on v0

v1 whole, which is shorter than its diff:
```python
import functools

import jax
import jax.numpy as jnp
from jax import lax
from jax.experimental import pallas as pl
from jax.experimental.pallas import tpu as pltpu
from jax.sharding import PartitionSpec as P

scale = 0.25
bf = jnp.bfloat16
f32 = jnp.float32
big = 48 * 1024 * 1024

ANY = pl.BlockSpec(memory_space=pl.ANY)
SMEM = pl.BlockSpec(memory_space=pltpu.SMEM)
VMEM = pl.BlockSpec(memory_space=pltpu.VMEM)


def params():
    return pltpu.CompilerParams(vmem_limit_bytes=big)


def cost(flops, nbytes):
    return pl.CostEstimate(flops=flops, bytes_accessed=nbytes, transcendentals=0)


def nbytes(*arrays):
    return sum(a.size * a.dtype.itemsize for a in arrays)


def swap(x, k, axis):
    n = lax.axis_size(axis)
    return lax.ppermute(x, axis, [(i, i ^ k) for i in range(n)])


def total(x, axis, wire=None):
    k = 1
    while k < lax.axis_size(axis):
        x = x + swap(x if wire is None else x.astype(wire), k, axis).astype(x.dtype)
        k *= 2
    return x


def pack_kernel(groups, tasks, gst, trp, stored, *rest):
    outs, sem = rest[:groups], rest[groups]
    me = lax.axis_index("dp")
    copies = []
    for k in reversed(range(groups)):
        row = lax.rem(trp[gst[me ^ k, me]], tasks)
        copies.append(pltpu.make_async_copy(stored.at[row], outs[k], sem.at[k]))
        copies[-1].start()
    for c in copies:
        c.wait()


def pack(gst, trp, stored):
    groups, tasks = gst.shape[0], stored.shape[0]
    shape = jax.ShapeDtypeStruct(stored.shape[1:], stored.dtype)
    return pl.pallas_call(
        functools.partial(pack_kernel, groups, tasks),
        out_shape=[shape] * groups,
        in_specs=[SMEM, SMEM, ANY],
        out_specs=[ANY] * groups,
        scratch_shapes=[pltpu.SemaphoreType.DMA((groups,))],
        compiler_params=params(),
        cost_estimate=cost(0, 2 * groups * stored.size // tasks * 2),
    )(gst, trp, stored)


def score_kernel(slots, gst, slot, score, out):
    me = lax.axis_index("dp")
    hot = slot[...] == lax.broadcasted_iota(jnp.int32, (slots, slot.shape[1]), 0)
    sums = jnp.sum(jnp.where(hot, score[...].astype(f32), 0.0), axis=1, keepdims=True)
    counts = jnp.sum(jnp.where(hot, 1.0, 0.0), axis=1, keepdims=True)
    lane = lax.broadcasted_iota(jnp.int32, (1, out.shape[1]), 1)
    a = jnp.zeros((1, out.shape[1]), f32)
    b = jnp.zeros((1, out.shape[1]), f32)
    for s in range(slots):
        mine = lane == gst[me, s]
        a += jnp.where(mine, sums[s : s + 1, :], 0.0)
        b += jnp.where(mine, counts[s : s + 1, :], 0.0)
    out[0:1, :] = a
    out[1:2, :] = b


def advantage_kernel(slots, gst, totals, slot, score, out):
    me = lax.axis_index("dp")
    means = totals[0:1, :] / jnp.maximum(totals[1:2, :], 1.0)
    lane = lax.broadcasted_iota(jnp.int32, means.shape, 1)
    mean_of = jnp.zeros(slot.shape, f32)
    for s in range(slots):
        m = jnp.sum(jnp.where(lane == gst[me, s], means, 0.0), axis=1, keepdims=True)
        mean_of += jnp.where(slot[...] == s, m, 0.0)
    out[...] = score[...].astype(f32) - mean_of


def base_kernel(mine, hidden, weight, out):
    out[0] = jnp.dot(hidden[...], weight[...], preferred_element_type=f32).astype(bf)


def base_parts(rows, weight, parts):
    n, width = rows.shape
    cols = weight.shape[1] // parts
    mine = lax.axis_index("tensor").astype(jnp.int32).reshape(1)
    return pl.pallas_call(
        base_kernel,
        out_shape=jax.ShapeDtypeStruct((parts, n, cols), bf),
        grid_spec=pltpu.PrefetchScalarGridSpec(
            num_scalar_prefetch=1,
            grid=(parts,),
            in_specs=[
                pl.BlockSpec((n, width), lambda i, m: (0, 0)),
                pl.BlockSpec((width, cols), lambda i, m: (0, m[0] ^ i)),
            ],
            out_specs=pl.BlockSpec((1, n, cols), lambda i, m: (i, 0, 0)),
        ),
        compiler_params=params(),
        cost_estimate=cost(2 * n * width * weight.shape[1], nbytes(rows, weight)),
    )(mine, rows, weight)


def inner_kernel(groups, place, rows, *rest):
    blocks, out = rest[:groups], rest[groups]
    acc = jnp.zeros(out.shape, f32)
    for k in range(groups):
        part = lax.dot_general(
            blocks[k][...], rows[...], (((1,), (1,)), ((), ())), preferred_element_type=f32
        )
        acc = jnp.where(place[...] == k, part, acc)
    out[...] = acc


def inner(place, rows, blocks):
    rank = blocks[0].shape[0]
    n = rows.shape[0]
    return pl.pallas_call(
        functools.partial(inner_kernel, len(blocks)),
        out_shape=jax.ShapeDtypeStruct((rank, n), f32),
        in_specs=[VMEM] * (2 + len(blocks)),
        out_specs=VMEM,
        compiler_params=params(),
        cost_estimate=cost(2 * n * rows.shape[1] * rank * len(blocks), nbytes(rows, *blocks)),
    )(place, rows, *blocks)


def grad_kernel(groups, place, adv, inner_t, rows, *outs):
    t = (adv[...] * inner_t[...]).astype(bf)
    zero = jnp.zeros((), bf)
    for k in range(groups):
        part = jnp.where(place[...] == k, t, zero)
        outs[k][...] = (
            scale * jnp.dot(part, rows[...], preferred_element_type=f32)
        ).astype(bf)


def grads(place, adv, inner_t, rows, groups):
    rank = inner_t.shape[0]
    n, width = rows.shape
    shape = jax.ShapeDtypeStruct((rank, width), bf)
    return pl.pallas_call(
        functools.partial(grad_kernel, groups),
        out_shape=[shape] * groups,
        in_specs=[VMEM] * 4,
        out_specs=[VMEM] * groups,
        compiler_params=params(),
        cost_estimate=cost(2 * n * width * rank * groups, nbytes(rows) + groups * rank * width * 2),
    )(place, adv, inner_t, rows)


def delta_kernel(groups, place, inner_t, base_mine, base_got, *rest):
    blocks, out = rest[:groups], rest[groups]
    t = inner_t[...].astype(bf)
    zero = jnp.zeros((), bf)
    spread = jnp.concatenate([jnp.where(place[...] == k, t, zero) for k in range(groups)], axis=0)
    ups = jnp.concatenate([b[...] for b in blocks], axis=0)
    delta = lax.dot_general(spread, ups, (((0,), (0,)), ((), ())), preferred_element_type=f32)
    delta = (scale * delta).astype(bf).astype(f32)
    out[...] = (base_mine[...].astype(f32) + base_got[...].astype(f32) + delta).astype(bf)


def adapted(place, inner_t, base_mine, base_got, blocks):
    n, cols = base_got.shape
    groups = len(blocks)
    return pl.pallas_call(
        functools.partial(delta_kernel, groups),
        out_shape=jax.ShapeDtypeStruct((n, cols), bf),
        in_specs=[VMEM] * (4 + groups),
        out_specs=VMEM,
        compiler_params=params(),
        cost_estimate=cost(2 * n * cols * groups * inner_t.shape[0], nbytes(*blocks) + 3 * n * cols * 2),
    )(place, inner_t, base_mine, base_got, *blocks)


def combine_kernel(groups, tasks, gst, trp, *rest):
    blocks, out = rest[:groups], rest[groups]
    me = lax.axis_index("dp")
    here = pl.program_id(0)
    rows = [lax.rem(trp[gst[me ^ k, me]], tasks) for k in range(groups)]
    acc = jnp.zeros(out.shape[1:], f32)
    for k in range(groups):
        acc += jnp.where(rows[k] == here, blocks[k][...].astype(f32), 0.0)
    out[0] = acc.astype(bf)


def combine(gst, trp, blocks, tasks):
    groups = len(blocks)
    rank, width = blocks[0].shape
    return pl.pallas_call(
        functools.partial(combine_kernel, groups, tasks),
        out_shape=jax.ShapeDtypeStruct((tasks, rank, width), bf),
        grid=(tasks,),
        in_specs=[SMEM, SMEM] + [VMEM] * groups,
        out_specs=pl.BlockSpec((1, rank, width), lambda t: (t, 0, 0)),
        compiler_params=params(),
        cost_estimate=cost(0, (groups + tasks) * rank * width * 2),
    )(gst, trp, *blocks)


def body(hidden, weight, down, up, slot, gst, trp, scores, cotangent):
    groups, parts = lax.axis_size("dp"), lax.axis_size("tensor")
    me = lax.axis_index("dp")
    att, steps, width = hidden.shape
    cols = cotangent.shape[2]
    n = att * steps
    tasks = down.shape[0]

    up_out = pack(gst, trp, up)
    down_out = pack(gst, trp, jnp.swapaxes(down, 1, 2))
    order = list(reversed(range(1, groups)))
    up_in = [up_out[0]] + [None] * (groups - 1)
    down_in = [down_out[0]] + [None] * (groups - 1)
    for k in order:
        up_in[k] = swap(up_out[k], k, "dp")
    for k in order:
        down_in[k] = swap(down_out[k], k, "dp")

    slot_row = slot.reshape(1, att)
    score_row = scores.reshape(1, att)
    local = pl.pallas_call(
        functools.partial(score_kernel, groups),
        out_shape=jax.ShapeDtypeStruct((2, trp.shape[0]), f32),
        in_specs=[SMEM, VMEM, VMEM],
        out_specs=VMEM,
    )(gst, slot_row, score_row)
    totals = total(local, "dp")
    slot_rows = jnp.repeat(slot_row, steps, axis=1)
    score_rows = jnp.repeat(score_row, steps, axis=1)
    place = slot_rows ^ me
    adv = pl.pallas_call(
        functools.partial(advantage_kernel, groups),
        out_shape=jax.ShapeDtypeStruct((1, n), f32),
        in_specs=[SMEM, VMEM, VMEM, VMEM],
        out_specs=VMEM,
    )(gst, totals, slot_rows, score_rows)

    cot = cotangent.reshape(n, cols)
    rows = hidden.reshape(n, width)

    base = base_parts(rows, weight, parts)
    held = [base[i] for i in range(parts)]
    k = 1
    while 2 * k < parts:
        got = swap(jnp.stack(held[1::2]), k, "tensor")
        held = [
            (a.astype(f32) + got[i].astype(f32)).astype(bf) for i, a in enumerate(held[0::2])
        ]
        k *= 2
    base_mine, base_got = held[0], swap(held[1], k, "tensor")

    back = total(inner(place, cot, up_in), "tensor")
    grad_down_out = grads(place, adv, back, rows, groups)
    grad_down_in = [grad_down_out[0]] + [None] * (groups - 1)
    for k in order:
        grad_down_in[k] = swap(grad_down_out[k], k, "dp")

    ahead = total(inner(place, rows, down_in), "tensor")
    grad_up_out = grads(place, adv, ahead, cot, groups)
    grad_up_in = [grad_up_out[0]] + [None] * (groups - 1)
    for k in order:
        grad_up_in[k] = swap(grad_up_out[k], k, "dp")
    kv_new = adapted(place, ahead, base_mine, base_got, up_in).reshape(att, steps, cols)

    grad_down = jnp.swapaxes(combine(gst, trp, grad_down_in, tasks), 1, 2)
    grad_up = combine(gst, trp, grad_up_in, tasks)
    return (kv_new, grad_down, grad_up)


def solution(mesh):
    in_specs = (
        P("dp", None, "tensor"),
        P("tensor", None),
        P("dp", "tensor", None),
        P("dp", None, "tensor"),
        P("dp", None),
        P(),
        P(),
        P("dp"),
        P("dp", None, "tensor"),
    )
    out_specs = (P("dp", None, "tensor"), P("dp", "tensor", None), P("dp", None, "tensor"))
    return jax.shard_map(body, mesh=mesh, in_specs=in_specs, out_specs=out_specs, check_vma=False)
```

time: 267 us -> 229 us (0.86)
  Pallas kernels: 0 us -> 66.4 us
  starting transfers between devices: 26.9 us -> 73.6 us
  waiting for transfers between devices: 118 us -> 71.4 us
  blocking collectives: 45.1 us -> 0 us
  matrix products: 30.7 us -> 0 us
  local copies, waits for them, and re-layouts: 25 us -> 10.1 us
  between operations: 14.2 us -> 0.9 us
    all_to_all x4 -> x0, waiting for transfers between devices: 118 us -> none  [the longest x1 86.4 us: body(): lax.all_to_all(down_gradient_sender, 'dp', split_axis=0, concat_axis=0, t...]
    ppermute x0 -> x37, starting transfers between devices: none -> 73.6 us  [swap(): return lax.ppermute(x, axis, [(i, i ^ k) for i in range(n)])]
    ppermute x0 -> x37, waiting for transfers between devices: none -> 71.4 us  [swap(): return lax.ppermute(x, axis, [(i, i ^ k) for i in range(n)])]
    pallas_call x0 -> x12, Pallas kernels: none -> 66.4 us  [the longest x2 27.2 us: pack(): pl.pallas_call(functools.partial(pack_kernel, groups, tasks), out_shape=[...]
    psum x2 -> x0, blocking collectives: 45.1 us -> none  [the longest x1 32 us: body(): score_sums, task_counts = lax.psum((sums_local, counts_local), 'dp')]
    dot_general x10 -> x0, matrix products: 30.7 us -> none  [the longest x1 10.5 us: body(): jnp.dot(flat_rows, key_value_weight, preferred_element_type=jnp.float32)]
    all_to_all x4 -> x0, starting transfers between devices: 26.9 us -> none  [the longest x1 10.7 us: body(): lax.all_to_all(up_gradient_sender, 'dp', split_axis=0, concat_axis=0, til...]
    mul x2 -> x0, local copies, waits for them, and re-layouts: 5.98 us -> none  [the longest x1 4.4 us: body(): adapter_output_scale * jnp.einsum('nd,nsr->sdr', flat_rows, back_spread,...]
  transfers between devices with their start and end apart: 5 -> 37, of which waited for: 3 -> 11; matrix products, arithmetic and copies ran while one was open for 17% -> 3% of each run, Pallas kernels for 0% -> 26%
where the time goes in v1:
time: 229 us
  starting transfers between devices  73.6 us (32%)
  waiting for transfers between devices  71.4 us (31%)
  Pallas kernels  66.4 us (29%)
  local copies, waits for them, and re-layouts  10.1 us (4%)
  other arithmetic  6.41 us (3%)
    ppermute x37, starting transfers between devices, swap(): return lax.ppermute(x, axis, [(i, i ^ k) for i in range(n)])  73.6 us
    ppermute x37, waiting for transfers between devices, swap(): return lax.ppermute(x, axis, [(i, i ^ k) for i in range(n)])  71.4 us
    pallas_call x2, Pallas kernels, pack(): pl.pallas_call(functools.partial(pack_kernel, groups, tasks), out_shape=[...  27.2 us
    pallas_call x2, Pallas kernels, combine(): pl.pallas_call(functools.partial(combine_kernel, groups, tasks), out_shap...  17.2 us
    pallas_call x2, Pallas kernels, inner(): pl.pallas_call(functools.partial(inner_kernel, len(blocks)), out_shape=ja...  7.65 us
    pallas_call x1, Pallas kernels, base_parts(): pl.pallas_call(base_kernel, out_shape=jax.ShapeDtypeStruct((parts, n, col...  7.05 us
  transfers between devices with their start and end apart: 37, of which 11 were waited for; matrix products, arithmetic and copies ran while one was open for 3% of the time, Pallas kernels for 26%

profile of v1, /device:TPU:0, one launch (start us, length us, event | category | flops | bytes accessed | tf_op | source)
XLA Modules:
  0.0 228.8 jit_solution(13073427968337237628)
XLA Ops:
  0.6 2.7 %reshape.60.rows.hidden = bf16[512,2048]{1,0:T(8,128)(2,1)S(1)} reshape(bf16[256,2,2048]{2,1,0:T(2,128)(2,1)} %param.9) | data formatting | bytes 4194304 | tf_op jit(solution)/shard_map/reshape | solution.py:258
  3.4 7.0 %shard_map.114 = bf16[4,512,512]{2,1,0:T(8,128)(2,1)S(1)} custom-call(s32[1]{0:T(128)} %bitcast.2.mine, bf16[512,2048]{1,0:T(8,128)(2,1)S(1)} %reshape.60.rows.hidden, bf16[2048,2048]{1,0:T(8,128)(2,1)} %weight.1), custom_call_target="tpu_custom_call" | custom-call | flops 4294967296 | bytes 10485760 | tf_op jit(solution)/shard_map/pallas_call | solution.py:106
  14.1 2.9 %collective-permute-start.11 = (bf16[64,512]{1,0:T(8,128)(2,1)S(1)}, bf16[64,512]{1,0:T(8,128)(2,1)S(1)}, u32[]{:S(2)}, u32[]{:S(2)}) collective-permute-start(bf16[64,512]{1,0:T(8,128)(2,1)S(1)} %get-tuple-element.44), channel_id=1, source_target_pairs={{0,4},{4,0},{8,12},{12,8},{16,20},{20,16},{24,28},{28,24},{1,5},{5... | collective-permute-start | bytes 196616 | tf_op jit(solution)/shard_map/ppermute | solution.py:34
  18.6 3.0 %collective-permute-start.14 = (bf16[64,512]{1,0:T(8,128)(2,1)}, bf16[64,512]{1,0:T(8,128)(2,1)S(1)}, u32[]{:S(2)}, u32[]{:S(2)}) collective-permute-start(bf16[64,512]{1,0:T(8,128)(2,1)} %get-tuple-element.47), channel_id=1, source_target_pairs={{0,16},{4,20},{8,24},{12,28},{16,0},{20,4},{24,8},{28,12},{1,17},{... | collective-permute-start | bytes 196616 | tf_op jit(solution)/shard_map/ppermute | solution.py:34
  21.6 1.7 collective-permute-start.15
  23.3 3.2 %collective-permute-start.16 = (bf16[64,512]{1,0:T(8,128)(2,1)S(1)}, bf16[64,512]{1,0:T(8,128)(2,1)S(1)}, u32[]{:S(2)}, u32[]{:S(2)}) collective-permute-start(bf16[64,512]{1,0:T(8,128)(2,1)S(1)} %get-tuple-element.49), channel_id=1, source_target_pairs={{0,24},{4,28},{8,16},{12,20},{16,8},{20,12},{24,0},{28,4},{1,25},{... | collective-permute-start | bytes 196616 | tf_op jit(solution)/shard_map/ppermute | solution.py:34
  26.8 25.6 %shard_map.112 = (bf16[64,2048]{1,0:T(8,128)(2,1)S(1)}, bf16[64,2048]{1,0:T(8,128)(2,1)}, bf16[64,2048]{1,0:T(8,128)(2,1)}, bf16[64,2048]{1,0:T(8,128)(2,1)}, bf...) custom-call(s32[8,8]{1,0:T(8,128)S(1)} %copy-done.3, ...), custom_call_target="tpu_custom_call" | custom-call | bytes 4194304 | tf_op jit(solution)/shard_map/pallas_call | solution.py:60
  55.8 2.9 %collective-permute-start.2 = (bf16[64,2048]{1,0:T(8,128)(2,1)}, bf16[64,2048]{1,0:T(8,128)(2,1)}, u32[]{:S(2)}, u32[]{:S(2)}) collective-permute-start(bf16[64,2048]{1,0:T(8,128)(2,1)} %get-tuple-element.38), channel_id=1, source_target_pairs={{0,12},{4,8},{8,4},{12,0},{16,28},{20,24},{24,20},{28,16},{1,13},{... | collective-permute-start | bytes 786440 | tf_op jit(solution)/shard_map/ppermute | solution.py:34
  60.6 9.1 %collective-permute-done.17.rest_7_ = bf16[64,512]{1,0:T(8,128)(2,1)S(1)} collective-permute-done((bf16[64,512]{1,0:T(8,128)(2,1)S(1)}, bf16[64,512]{1,0:T(8,128)(2,1)S(1)}, u32[]{:S(2)}, u32[]{:S(2)}) %collective-permute-start.17) | collective-permute-done | bytes 65568 | tf_op jit(solution)/shard_map/ppermute | solution.py:34
  72.5 2.9 %collective-permute-start.4 = (bf16[64,2048]{1,0:T(8,128)(2,1)}, bf16[64,2048]{1,0:T(8,128)(2,1)S(1)}, u32[]{:S(2)}, u32[]{:S(2)}) collective-permute-start(bf16[64,2048]{1,0:T(8,128)(2,1)} %copy-done.9), channel_id=1, source_target_pairs={{0,20},{4,16},{8,28},{12,24},{16,4},{20,0},{24,12},{28,8},{1,21},{... | collective-permute-start | bytes 786440 | tf_op jit(solution)/shard_map/ppermute | solution.py:34
  75.4 2.7 %collective-permute-start.5 = (bf16[64,2048]{1,0:T(8,128)(2,1)}, bf16[64,2048]{1,0:T(8,128)(2,1)S(1)}, u32[]{:S(2)}, u32[]{:S(2)}) collective-permute-start(bf16[64,2048]{1,0:T(8,128)(2,1)} %copy-done.8), channel_id=1, source_target_pairs={{0,24},{4,28},{8,16},{12,20},{16,8},{20,12},{24,0},{28,4},{1,25},{... | collective-permute-start | bytes 786440 | tf_op jit(solution)/shard_map/ppermute | solution.py:34
  78.1 2.0 collective-permute-start.6
  80.8 23.8 %collective-permute-done.3.rest_4_ = bf16[64,2048]{1,0:T(8,128)(2,1)S(1)} collective-permute-done((bf16[64,2048]{1,0:T(8,128)(2,1)}, bf16[64,2048]{1,0:T(8,128)(2,1)S(1)}, u32[]{:S(2)}, u32[]{:S(2)}) %collective-permute-start.3) | collective-permute-done | bytes 262176 | tf_op jit(solution)/shard_map/ppermute | solution.py:34
  106.1 4.1 %collective-permute-done.4.rest_5_ = bf16[64,2048]{1,0:T(8,128)(2,1)S(1)} collective-permute-done((bf16[64,2048]{1,0:T(8,128)(2,1)}, bf16[64,2048]{1,0:T(8,128)(2,1)S(1)}, u32[]{:S(2)}, u32[]{:S(2)}) %collective-permute-start.4) | collective-permute-done | bytes 262176 | tf_op jit(solution)/shard_map/ppermute | solution.py:34
  110.2 6.3 %shard_map.113 = f32[64,512]{1,0:T(8,128)S(1)} custom-call(s32[1,512]{1,0:T(1,128)S(1)} %broadcast_xor_fusion.place, bf16[512,2048]{1,0:T(8,128)(2,1)S(1)} %reshape.60.rows.hidden, bf16[64,2048]{1,0:T(8,128)(2,1)S(1)} %get-tuple-element.35.rest_0_, bf16[64,2048]{1,0:T(8,128)(2,1)} %collective-permute-done.rest_1_, ...), custom_call_target="tpu_custom_call" | custom-call | flops 1073741824 | bytes 4194304 | tf_op jit(solution)/shard_map/pallas_call | solution.py:137
  119.4 2.1 collective-permute-done.18
  122.3 11.6 %collective-permute-start.19 = (f32[2,128]{1,0:T(2,128)S(1)}, f32[2,128]{1,0:T(2,128)S(1)}, u32[]{:S(2)}, u32[]{:S(2)}) collective-permute-start(f32[2,128]{1,0:T(2,128)S(1)} %add.33), channel_id=1, source_target_pairs={{0,8},{4,12},{8,0},{12,4},{16,24},{20,28},{24,16},{28,20},{1,9},{5... | collective-permute-start | bytes 3080 | tf_op jit(solution)/shard_map/ppermute | solution.py:34
  135.4 1.8 collective-permute-start.20
  138.0 1.9 collective-permute-done.20
  143.6 3.0 %shard_map.120 = (bf16[64,2048]{1,0:T(8,128)(2,1)S(1)}, bf16[64,2048]{1,0:T(8,128)(2,1)S(1)}, bf16[64,2048]{1,0:T(8,128)(2,1)S(1)}, bf16[64,2048]{1,0:T(8,128)(2...) custom-call(s32[1,512]{1,0:T(1,128)S(1)} %broadcast_xor_fusion.place, ...), custom_call_target="tpu_custom_call" | custom-call | flops 1073741824 | bytes 4194304 | tf_op jit(solution)/shard_map/pallas_call | solution.py:161
  148.2 2.0 collective-permute-start.24
  154.9 2.8 %collective-permute-done.8 = f32[64,512]{1,0:T(8,128)S(1)} collective-permute-done((f32[64,512]{1,0:T(8,128)S(1)}, f32[64,512]{1,0:T(8,128)S(1)}, u32[]{:S(2)}, u32[]{:S(2)}) %collective-permute-start.8) | collective-permute-done | bytes 131104 | tf_op jit(solution)/shard_map/ppermute | solution.py:34
  157.7 1.7 collective-permute-start.26
  159.4 2.1 collective-permute-start.27
  163.1 4.1 %collective-permute-start.29 = (bf16[64,2048]{1,0:T(8,128)(2,1)S(1)}, bf16[64,2048]{1,0:T(8,128)(2,1)S(1)}, u32[]{:S(2)}, u32[]{:S(2)}) collective-permute-start(bf16[64,2048]{1,0:T(8,128)(2,1)S(1)} %get-tuple-element.58), channel_id=1, source_target_pairs={{0,28},{4,24},{8,20},{12,16},{16,12},{20,8},{24,4},{28,0},{1,29},{... | collective-permute-start | bytes 786440 | tf_op jit(solution)/shard_map/ppermute | solution.py:34
  168.1 19.5 %collective-permute-done.26.rest_4_ = bf16[64,2048]{1,0:T(8,128)(2,1)S(1)} collective-permute-done((bf16[64,2048]{1,0:T(8,128)(2,1)S(1)}, bf16[64,2048]{1,0:T(8,128)(2,1)S(1)}, u32[]{:S(2)}, u32[]{:S(2)}) %collective-permute-start.26) | collective-permute-done | bytes 262176 | tf_op jit(solution)/shard_map/ppermute | solution.py:34
  189.0 5.1 %collective-permute-done.27.rest_5_ = bf16[64,2048]{1,0:T(8,128)(2,1)S(1)} collective-permute-done((bf16[64,2048]{1,0:T(8,128)(2,1)S(1)}, bf16[64,2048]{1,0:T(8,128)(2,1)S(1)}, u32[]{:S(2)}, u32[]{:S(2)}) %collective-permute-start.27) | collective-permute-done | bytes 262176 | tf_op jit(solution)/shard_map/ppermute | solution.py:34
  194.0 5.3 %collective-permute-start.32 = (bf16[64,512]{1,0:T(8,128)(2,1)S(1)}, bf16[64,512]{1,0:T(8,128)(2,1)S(1)}, u32[]{:S(2)}, u32[]{:S(2)}) collective-permute-start(bf16[64,512]{1,0:T(8,128)(2,1)S(1)} %get-tuple-element.62), channel_id=1, source_target_pairs={{0,12},{4,8},{8,4},{12,0},{16,28},{20,24},{24,20},{28,16},{1,13},{... | collective-permute-start | bytes 196616 | tf_op jit(solution)/shard_map/ppermute | solution.py:34
  199.3 5.9 %collective-permute-start.33 = (bf16[64,512]{1,0:T(8,128)(2,1)S(1)}, bf16[64,512]{1,0:T(8,128)(2,1)S(1)}, u32[]{:S(2)}, u32[]{:S(2)}) collective-permute-start(bf16[64,512]{1,0:T(8,128)(2,1)S(1)} %get-tuple-element.63), channel_id=1, source_target_pairs={{0,16},{4,20},{8,24},{12,28},{16,0},{20,4},{24,8},{28,12},{1,17},{... | collective-permute-start | bytes 196616 | tf_op jit(solution)/shard_map/ppermute | solution.py:34
  205.2 3.6 %collective-permute-start.35 = (bf16[64,512]{1,0:T(8,128)(2,1)S(1)}, bf16[64,512]{1,0:T(8,128)(2,1)S(1)}, u32[]{:S(2)}, u32[]{:S(2)}) collective-permute-start(bf16[64,512]{1,0:T(8,128)(2,1)S(1)} %get-tuple-element.65), channel_id=1, source_target_pairs={{0,24},{4,28},{8,16},{12,20},{16,8},{20,12},{24,0},{28,4},{1,25},{... | collective-permute-start | bytes 196616 | tf_op jit(solution)/shard_map/ppermute | solution.py:34
  210.0 10.2 %shard_map.121 = bf16[16,64,2048]{2,1,0:T(8,128)(2,1)} custom-call(s32[8,8]{1,0:T(8,128)S(1)} %copy-done.4, s32[128]{0:T(128)S(1)} %copy-done.5, bf16[64,2048]{1,0:T(8,128)(2,1)S(1)} %get-tuple-element.51.rest_0_, bf16[64,2048]{1,0:T(8,128)(2,1)S(1)} %collective-permute-done.23.rest_1_, bf16[64,2048]{1,0:T(8,128)(2,1)S(1)} %collective-permute-done.24.rest_2_, ...), custom_call_target="tpu_custom_call" | custom-call | bytes 6291456 | tf_op jit(solution)/shard_map/pallas_call | solution.py:209
  220.2 7.0 %shard_map.123 = bf16[16,64,512]{2,1,0:T(8,128)(2,1)} custom-call(s32[8,8]{1,0:T(8,128)S(1)} %copy-done.4, s32[128]{0:T(128)S(1)} %copy-done.5, bf16[64,512]{1,0:T(8,128)(2,1)S(1)} %get-tuple-element.59.rest_0_, bf16[64,512]{1,0:T(8,128)(2,1)S(1)} %collective-permute-done.30.rest_1_, bf16[64,512]{1,0:T(8,128)(2,1)S(1)} %collective-permute-done.31.rest_2_, ...), custom_call_target="tpu_custom_call" | custom-call | bytes 1572864 | tf_op jit(solution)/shard_map/pallas_call | solution.py:209
  (100 shorter events, 38.1 us)
Async XLA Ops:
  12.1 140.7 %collective-permute-start.9 = (bf16[2,512,512]{2,1,0:T(8,128)(2,1)}, bf16[2,512,512]{2,1,0:T(8,128)(2,1)}, u32[]{:S(2)}, u32[]{:S(2)}) collective-permute-start(bf16[2,512,512]{2,1,0:T(8,128)(2,1)} %pad_maximum_fusion), channel_id=1, source_target_pairs={{0,1},{1,0},{2,3},{3,2},{4,5},{5,4},{6,7},{7,6},{8,9},{9,8},{10,11... | collective-permute-start | bytes 3145736 | tf_op jit(solution)/shard_map/ppermute | solution.py:34
  14.1 7.5 %collective-permute-start.11 = (bf16[64,512]{1,0:T(8,128)(2,1)S(1)}, bf16[64,512]{1,0:T(8,128)(2,1)S(1)}, u32[]{:S(2)}, u32[]{:S(2)}) collective-permute-start(bf16[64,512]{1,0:T(8,128)(2,1)S(1)} %get-tuple-element.44), channel_id=1, source_target_pairs={{0,4},{4,0},{8,12},{12,8},{16,20},{20,16},{24,28},{28,24},{1,5},{5... | collective-permute-start | bytes 196616 | tf_op jit(solution)/shard_map/ppermute | solution.py:34
  18.6 36.6 %collective-permute-start.13 = (bf16[64,512]{1,0:T(8,128)(2,1)}, bf16[64,512]{1,0:T(8,128)(2,1)S(1)}, u32[]{:S(2)}, u32[]{:S(2)}) collective-permute-start(bf16[64,512]{1,0:T(8,128)(2,1)} %get-tuple-element.46), channel_id=1, source_target_pairs={{0,12},{4,8},{8,4},{12,0},{16,28},{20,24},{24,20},{28,16},{1,13},{... | collective-permute-start | bytes 196616 | tf_op jit(solution)/shard_map/ppermute | solution.py:34
  18.6 37.1 %collective-permute-start.14 = (bf16[64,512]{1,0:T(8,128)(2,1)}, bf16[64,512]{1,0:T(8,128)(2,1)S(1)}, u32[]{:S(2)}, u32[]{:S(2)}) collective-permute-start(bf16[64,512]{1,0:T(8,128)(2,1)} %get-tuple-element.47), channel_id=1, source_target_pairs={{0,16},{4,20},{8,24},{12,28},{16,0},{20,4},{24,8},{28,12},{1,17},{... | collective-permute-start | bytes 196616 | tf_op jit(solution)/shard_map/ppermute | solution.py:34
  21.6 34.1 %collective-permute-start.15 = (bf16[64,512]{1,0:T(8,128)(2,1)}, bf16[64,512]{1,0:T(8,128)(2,1)S(1)}, u32[]{:S(2)}, u32[]{:S(2)}) collective-permute-start(bf16[64,512]{1,0:T(8,128)(2,1)} %get-tuple-element.48), channel_id=1, source_target_pairs={{0,20},{4,16},{8,28},{12,24},{16,4},{20,0},{24,12},{28,8},{1,21},{... | collective-permute-start | bytes 196616 | tf_op jit(solution)/shard_map/ppermute | solution.py:34
  23.3 35.4 %collective-permute-start.16 = (bf16[64,512]{1,0:T(8,128)(2,1)S(1)}, bf16[64,512]{1,0:T(8,128)(2,1)S(1)}, u32[]{:S(2)}, u32[]{:S(2)}) collective-permute-start(bf16[64,512]{1,0:T(8,128)(2,1)S(1)} %get-tuple-element.49), channel_id=1, source_target_pairs={{0,24},{4,28},{8,16},{12,20},{16,8},{20,12},{24,0},{28,4},{1,25},{... | collective-permute-start | bytes 196616 | tf_op jit(solution)/shard_map/ppermute | solution.py:34
  55.2 17.3 %collective-permute-start = (bf16[64,2048]{1,0:T(8,128)(2,1)}, bf16[64,2048]{1,0:T(8,128)(2,1)}, u32[]{:S(2)}, u32[]{:S(2)}) collective-permute-start(bf16[64,2048]{1,0:T(8,128)(2,1)} %get-tuple-element.36), channel_id=1, source_target_pairs={{0,4},{4,0},{8,12},{12,8},{16,20},{20,16},{24,28},{28,24},{1,5},{5... | collective-permute-start | bytes 786440 | tf_op jit(solution)/shard_map/ppermute | solution.py:34
  55.8 19.6 %collective-permute-start.1 = (bf16[64,2048]{1,0:T(8,128)(2,1)}, bf16[64,2048]{1,0:T(8,128)(2,1)}, u32[]{:S(2)}, u32[]{:S(2)}) collective-permute-start(bf16[64,2048]{1,0:T(8,128)(2,1)} %get-tuple-element.37), channel_id=1, source_target_pairs={{0,8},{4,12},{8,0},{12,4},{16,24},{20,28},{24,16},{28,20},{1,9},{5... | collective-permute-start | bytes 786440 | tf_op jit(solution)/shard_map/ppermute | solution.py:34
  55.8 22.3 %collective-permute-start.2 = (bf16[64,2048]{1,0:T(8,128)(2,1)}, bf16[64,2048]{1,0:T(8,128)(2,1)}, u32[]{:S(2)}, u32[]{:S(2)}) collective-permute-start(bf16[64,2048]{1,0:T(8,128)(2,1)} %get-tuple-element.38), channel_id=1, source_target_pairs={{0,12},{4,8},{8,4},{12,0},{16,28},{20,24},{24,20},{28,16},{1,13},{... | collective-permute-start | bytes 786440 | tf_op jit(solution)/shard_map/ppermute | solution.py:34
  58.7 11.0 %collective-permute-start.17 = (bf16[64,512]{1,0:T(8,128)(2,1)S(1)}, bf16[64,512]{1,0:T(8,128)(2,1)S(1)}, u32[]{:S(2)}, u32[]{:S(2)}) collective-permute-start(bf16[64,512]{1,0:T(8,128)(2,1)S(1)} %get-tuple-element.50), channel_id=1, source_target_pairs={{0,28},{4,24},{8,20},{12,16},{16,12},{20,8},{24,4},{28,0},{1,29},{... | collective-permute-start | bytes 196616 | tf_op jit(solution)/shard_map/ppermute | solution.py:34
  72.5 32.1 %collective-permute-start.3 = (bf16[64,2048]{1,0:T(8,128)(2,1)}, bf16[64,2048]{1,0:T(8,128)(2,1)S(1)}, u32[]{:S(2)}, u32[]{:S(2)}) collective-permute-start(bf16[64,2048]{1,0:T(8,128)(2,1)} %copy-done.10), channel_id=1, source_target_pairs={{0,16},{4,20},{8,24},{12,28},{16,0},{20,4},{24,8},{28,12},{1,17},{... | collective-permute-start | bytes 786440 | tf_op jit(solution)/shard_map/ppermute | solution.py:34
  72.5 37.7 %collective-permute-start.4 = (bf16[64,2048]{1,0:T(8,128)(2,1)}, bf16[64,2048]{1,0:T(8,128)(2,1)S(1)}, u32[]{:S(2)}, u32[]{:S(2)}) collective-permute-start(bf16[64,2048]{1,0:T(8,128)(2,1)} %copy-done.9), channel_id=1, source_target_pairs={{0,20},{4,16},{8,28},{12,24},{16,4},{20,0},{24,12},{28,8},{1,21},{... | collective-permute-start | bytes 786440 | tf_op jit(solution)/shard_map/ppermute | solution.py:34
  75.4 34.8 %collective-permute-start.5 = (bf16[64,2048]{1,0:T(8,128)(2,1)}, bf16[64,2048]{1,0:T(8,128)(2,1)S(1)}, u32[]{:S(2)}, u32[]{:S(2)}) collective-permute-start(bf16[64,2048]{1,0:T(8,128)(2,1)} %copy-done.8), channel_id=1, source_target_pairs={{0,24},{4,28},{8,16},{12,20},{16,8},{20,12},{24,0},{28,4},{1,25},{... | collective-permute-start | bytes 786440 | tf_op jit(solution)/shard_map/ppermute | solution.py:34
  78.1 32.1 %collective-permute-start.6 = (bf16[64,2048]{1,0:T(8,128)(2,1)}, bf16[64,2048]{1,0:T(8,128)(2,1)S(1)}, u32[]{:S(2)}, u32[]{:S(2)}) collective-permute-start(bf16[64,2048]{1,0:T(8,128)(2,1)} %copy-done.7), channel_id=1, source_target_pairs={{0,28},{4,24},{8,20},{12,16},{16,12},{20,8},{24,4},{28,0},{1,29},{... | collective-permute-start | bytes 786440 | tf_op jit(solution)/shard_map/ppermute | solution.py:34
  104.6 37.4 %collective-permute-start.22 = (f32[64,512]{1,0:T(8,128)}, f32[64,512]{1,0:T(8,128)}, u32[]{:S(2)}, u32[]{:S(2)}) collective-permute-start(f32[64,512]{1,0:T(8,128)} %add.36), channel_id=1, source_target_pairs={{0,2},{1,3},{2,0},{3,1},{4,6},{5,7},{6,4},{7,5},{8,10},{9,11},{10,... | collective-permute-start | bytes 393224 | tf_op jit(solution)/shard_map/ppermute | solution.py:34
  116.5 33.8 %collective-permute-start.7 = (f32[64,512]{1,0:T(8,128)S(1)}, f32[64,512]{1,0:T(8,128)}, u32[]{:S(2)}, u32[]{:S(2)}) collective-permute-start(f32[64,512]{1,0:T(8,128)S(1)} %shard_map.113), channel_id=1, source_target_pairs={{0,1},{1,0},{2,3},{3,2},{4,5},{5,4},{6,7},{7,6},{8,9},{9,8},{10,11... | collective-permute-start | bytes 393224 | tf_op jit(solution)/shard_map/ppermute | solution.py:34
  122.3 13.2 %collective-permute-start.19 = (f32[2,128]{1,0:T(2,128)S(1)}, f32[2,128]{1,0:T(2,128)S(1)}, u32[]{:S(2)}, u32[]{:S(2)}) collective-permute-start(f32[2,128]{1,0:T(2,128)S(1)} %add.33), channel_id=1, source_target_pairs={{0,8},{4,12},{8,0},{12,4},{16,24},{20,28},{24,16},{28,20},{1,9},{5... | collective-permute-start | bytes 3080 | tf_op jit(solution)/shard_map/ppermute | solution.py:34
  146.7 12.8 %collective-permute-start.23 = (bf16[64,2048]{1,0:T(8,128)(2,1)S(1)}, bf16[64,2048]{1,0:T(8,128)(2,1)S(1)}, u32[]{:S(2)}, u32[]{:S(2)}) collective-permute-start(bf16[64,2048]{1,0:T(8,128)(2,1)S(1)} %get-tuple-element.52), channel_id=1, source_target_pairs={{0,4},{4,0},{8,12},{12,8},{16,20},{20,16},{24,28},{28,24},{1,5},{5... | collective-permute-start | bytes 786440 | tf_op jit(solution)/shard_map/ppermute | solution.py:34
  148.2 13.3 %collective-permute-start.24 = (bf16[64,2048]{1,0:T(8,128)(2,1)S(1)}, bf16[64,2048]{1,0:T(8,128)(2,1)S(1)}, u32[]{:S(2)}, u32[]{:S(2)}) collective-permute-start(bf16[64,2048]{1,0:T(8,128)(2,1)S(1)} %get-tuple-element.53), channel_id=1, source_target_pairs={{0,8},{4,12},{8,0},{12,4},{16,24},{20,28},{24,16},{28,20},{1,9},{5... | collective-permute-start | bytes 786440 | tf_op jit(solution)/shard_map/ppermute | solution.py:34
  150.2 12.9 %collective-permute-start.25 = (bf16[64,2048]{1,0:T(8,128)(2,1)S(1)}, bf16[64,2048]{1,0:T(8,128)(2,1)S(1)}, u32[]{:S(2)}, u32[]{:S(2)}) collective-permute-start(bf16[64,2048]{1,0:T(8,128)(2,1)S(1)} %get-tuple-element.54), channel_id=1, source_target_pairs={{0,12},{4,8},{8,4},{12,0},{16,28},{20,24},{24,20},{28,16},{1,13},{... | collective-permute-start | bytes 786440 | tf_op jit(solution)/shard_map/ppermute | solution.py:34
  154.3 72.9 %collective-permute-start.10 = (bf16[512,512]{1,0:T(8,128)(2,1)S(1)}, bf16[512,512]{1,0:T(8,128)(2,1)S(1)}, u32[]{:S(2)}, u32[]{:S(2)}) collective-permute-start(bf16[512,512]{1,0:T(8,128)(2,1)S(1)} %get-tuple-element.67), channel_id=1, source_target_pairs={{0,2},{1,3},{2,0},{3,1},{4,6},{5,7},{6,4},{7,5},{8,10},{9,11},{10,... | collective-permute-start | bytes 1572872 | tf_op jit(solution)/shard_map/ppermute | solution.py:34
  157.7 29.9 %collective-permute-start.26 = (bf16[64,2048]{1,0:T(8,128)(2,1)S(1)}, bf16[64,2048]{1,0:T(8,128)(2,1)S(1)}, u32[]{:S(2)}, u32[]{:S(2)}) collective-permute-start(bf16[64,2048]{1,0:T(8,128)(2,1)S(1)} %get-tuple-element.55), channel_id=1, source_target_pairs={{0,16},{4,20},{8,24},{12,28},{16,0},{20,4},{24,8},{28,12},{1,17},{... | collective-permute-start | bytes 786440 | tf_op jit(solution)/shard_map/ppermute | solution.py:34
  159.4 34.6 %collective-permute-start.27 = (bf16[64,2048]{1,0:T(8,128)(2,1)S(1)}, bf16[64,2048]{1,0:T(8,128)(2,1)S(1)}, u32[]{:S(2)}, u32[]{:S(2)}) collective-permute-start(bf16[64,2048]{1,0:T(8,128)(2,1)S(1)} %get-tuple-element.56), channel_id=1, source_target_pairs={{0,20},{4,16},{8,28},{12,24},{16,4},{20,0},{24,12},{28,8},{1,21},{... | collective-permute-start | bytes 786440 | tf_op jit(solution)/shard_map/ppermute | solution.py:34
  161.5 32.5 %collective-permute-start.28 = (bf16[64,2048]{1,0:T(8,128)(2,1)S(1)}, bf16[64,2048]{1,0:T(8,128)(2,1)S(1)}, u32[]{:S(2)}, u32[]{:S(2)}) collective-permute-start(bf16[64,2048]{1,0:T(8,128)(2,1)S(1)} %get-tuple-element.57), channel_id=1, source_target_pairs={{0,24},{4,28},{8,16},{12,20},{16,8},{20,12},{24,0},{28,4},{1,25},{... | collective-permute-start | bytes 786440 | tf_op jit(solution)/shard_map/ppermute | solution.py:34
  163.1 36.2 %collective-permute-start.29 = (bf16[64,2048]{1,0:T(8,128)(2,1)S(1)}, bf16[64,2048]{1,0:T(8,128)(2,1)S(1)}, u32[]{:S(2)}, u32[]{:S(2)}) collective-permute-start(bf16[64,2048]{1,0:T(8,128)(2,1)S(1)} %get-tuple-element.58), channel_id=1, source_target_pairs={{0,28},{4,24},{8,20},{12,16},{16,12},{20,8},{24,4},{28,0},{1,29},{... | collective-permute-start | bytes 786440 | tf_op jit(solution)/shard_map/ppermute | solution.py:34
  187.6 17.7 %collective-permute-start.30 = (bf16[64,512]{1,0:T(8,128)(2,1)S(1)}, bf16[64,512]{1,0:T(8,128)(2,1)S(1)}, u32[]{:S(2)}, u32[]{:S(2)}) collective-permute-start(bf16[64,512]{1,0:T(8,128)(2,1)S(1)} %get-tuple-element.60), channel_id=1, source_target_pairs={{0,4},{4,0},{8,12},{12,8},{16,20},{20,16},{24,28},{28,24},{1,5},{5... | collective-permute-start | bytes 196616 | tf_op jit(solution)/shard_map/ppermute | solution.py:34
  194.0 11.2 %collective-permute-start.31 = (bf16[64,512]{1,0:T(8,128)(2,1)S(1)}, bf16[64,512]{1,0:T(8,128)(2,1)S(1)}, u32[]{:S(2)}, u32[]{:S(2)}) collective-permute-start(bf16[64,512]{1,0:T(8,128)(2,1)S(1)} %get-tuple-element.61), channel_id=1, source_target_pairs={{0,8},{4,12},{8,0},{12,4},{16,24},{20,28},{24,16},{28,20},{1,9},{5... | collective-permute-start | bytes 196616 | tf_op jit(solution)/shard_map/ppermute | solution.py:34
  194.0 14.9 %collective-permute-start.32 = (bf16[64,512]{1,0:T(8,128)(2,1)S(1)}, bf16[64,512]{1,0:T(8,128)(2,1)S(1)}, u32[]{:S(2)}, u32[]{:S(2)}) collective-permute-start(bf16[64,512]{1,0:T(8,128)(2,1)S(1)} %get-tuple-element.62), channel_id=1, source_target_pairs={{0,12},{4,8},{8,4},{12,0},{16,28},{20,24},{24,20},{28,16},{1,13},{... | collective-permute-start | bytes 196616 | tf_op jit(solution)/shard_map/ppermute | solution.py:34
  199.3 20.9 %collective-permute-start.33 = (bf16[64,512]{1,0:T(8,128)(2,1)S(1)}, bf16[64,512]{1,0:T(8,128)(2,1)S(1)}, u32[]{:S(2)}, u32[]{:S(2)}) collective-permute-start(bf16[64,512]{1,0:T(8,128)(2,1)S(1)} %get-tuple-element.63), channel_id=1, source_target_pairs={{0,16},{4,20},{8,24},{12,28},{16,0},{20,4},{24,8},{28,12},{1,17},{... | collective-permute-start | bytes 196616 | tf_op jit(solution)/shard_map/ppermute | solution.py:34
  205.2 15.0 %collective-permute-start.34 = (bf16[64,512]{1,0:T(8,128)(2,1)S(1)}, bf16[64,512]{1,0:T(8,128)(2,1)S(1)}, u32[]{:S(2)}, u32[]{:S(2)}) collective-permute-start(bf16[64,512]{1,0:T(8,128)(2,1)S(1)} %get-tuple-element.64), channel_id=1, source_target_pairs={{0,20},{4,16},{8,28},{12,24},{16,4},{20,0},{24,12},{28,8},{1,21},{... | collective-permute-start | bytes 196616 | tf_op jit(solution)/shard_map/ppermute | solution.py:34
  205.2 15.0 %collective-permute-start.35 = (bf16[64,512]{1,0:T(8,128)(2,1)S(1)}, bf16[64,512]{1,0:T(8,128)(2,1)S(1)}, u32[]{:S(2)}, u32[]{:S(2)}) collective-permute-start(bf16[64,512]{1,0:T(8,128)(2,1)S(1)} %get-tuple-element.65), channel_id=1, source_target_pairs={{0,24},{4,28},{8,16},{12,20},{16,8},{20,12},{24,0},{28,4},{1,25},{... | collective-permute-start | bytes 196616 | tf_op jit(solution)/shard_map/ppermute | solution.py:34
  208.9 11.3 %collective-permute-start.36 = (bf16[64,512]{1,0:T(8,128)(2,1)S(1)}, bf16[64,512]{1,0:T(8,128)(2,1)S(1)}, u32[]{:S(2)}, u32[]{:S(2)}) collective-permute-start(bf16[64,512]{1,0:T(8,128)(2,1)S(1)} %get-tuple-element.66), channel_id=1, source_target_pairs={{0,28},{4,24},{8,20},{12,16},{16,12},{20,8},{24,4},{28,0},{1,29},{... | collective-permute-start | bytes 196616 | tf_op jit(solution)/shard_map/ppermute | solution.py:34
  (19 other events, 177.3 us)

commit v2 on v0

v2 whole, which is shorter than its diff:
```python
import functools

import jax
import jax.numpy as jnp
from jax import lax
from jax.experimental import pallas as pl
from jax.experimental.pallas import tpu as pltpu
from jax.sharding import PartitionSpec as P

scale = 0.25
bf = jnp.bfloat16
f32 = jnp.float32
big = 63 * 1024 * 1024
spare = 16

ANY = pl.BlockSpec(memory_space=pl.ANY)
SMEM = pl.BlockSpec(memory_space=pltpu.SMEM)
VMEM = pl.BlockSpec(memory_space=pltpu.VMEM)


def shaped(shape, dtype):
    return jax.ShapeDtypeStruct(shape, dtype)


def call(kernel, outs, operands, specs, flops=0, scratch=(), after=(), vmem_outs=True):
    moved = sum(a.size * a.dtype.itemsize for a in list(operands) + list(outs))
    count = len(operands)

    def run(*refs):
        kernel(refs[:count], refs[count + len(after) :])

    return pl.pallas_call(
        run,
        out_shape=list(outs),
        in_specs=list(specs) + [ANY] * len(after),
        out_specs=[VMEM] * len(outs),
        scratch_shapes=list(scratch),
        compiler_params=pltpu.CompilerParams(vmem_limit_bytes=big),
        cost_estimate=pl.CostEstimate(flops=flops, bytes_accessed=moved, transcendentals=0),
    )(*operands, *after)


def swap(x, k, axis):
    n = lax.axis_size(axis)
    return lax.ppermute(x, axis, [(i, i ^ k) for i in range(n)])


def stored_row(gst, trp, tasks, k):
    me = lax.axis_index("dp")
    return lax.rem(trp[gst[me ^ k, me]], tasks)


def pack_up(gst, trp, up, slot_row, score_row):
    groups = gst.shape[0]
    tasks, rank, cols = up.shape

    def kernel(ins, outs):
        gst, trp, up, slot, score = ins
        sem = outs[-1]
        copies = []
        for k in reversed(range(groups)):
            row = stored_row(gst, trp, tasks, k)
            copies.append(
                pltpu.make_async_copy(up.at[row], outs[k].at[pl.ds(0, rank), :], sem.at[k])
            )
            copies[-1].start()
        hot = slot[...] == lax.broadcasted_iota(jnp.int32, (groups, slot.shape[1]), 0)
        sums = jnp.sum(jnp.where(hot, score[...].astype(f32), 0.0), axis=1, keepdims=True)
        counts = jnp.sum(jnp.where(hot, 1.0, 0.0), axis=1, keepdims=True)
        here = lax.broadcasted_iota(jnp.int32, (groups, cols), 0) == lax.broadcasted_iota(
            jnp.int32, (groups, cols), 1
        )
        sums = jnp.sum(jnp.where(here, sums, 0.0), axis=0, keepdims=True)
        counts = jnp.sum(jnp.where(here, counts, 0.0), axis=0, keepdims=True)
        line = lax.broadcasted_iota(jnp.int32, (spare, cols), 0)
        both = jnp.where(line == 0, sums, jnp.where(line == 1, counts, 0.0)).astype(bf)
        for k in range(groups):
            outs[k][rank:, :] = both
        for c in copies:
            c.wait()

    return call(
        kernel,
        [shaped((rank + spare, cols), bf)] * groups,
        (gst, trp, up, slot_row, score_row),
        [SMEM, SMEM, ANY, VMEM, VMEM],
        scratch=[pltpu.SemaphoreType.DMA((groups,))],
    )


def pack_down(gst, trp, down, after):
    groups = gst.shape[0]
    tasks, rank, width = down.shape

    def kernel(ins, outs):
        gst, trp, down = ins
        out, sem = outs
        me = lax.axis_index("dp")
        copies = []
        for g in range(groups):
            row = lax.rem(trp[gst[g, me]], tasks)
            copies.append(pltpu.make_async_copy(down.at[row], out.at[g], sem.at[g]))
            copies[-1].start()
        for c in copies:
            c.wait()

    return call(
        kernel,
        [shaped((groups, rank, width), bf)],
        (gst, trp, down),
        [SMEM, SMEM, ANY],
        scratch=[pltpu.SemaphoreType.DMA((groups,))],
        after=after,
    )[0]


def base_parts(rows, weight, parts, after):
    n, width = rows.shape
    cols = weight.shape[1] // parts
    mine = lax.axis_index("tensor").astype(jnp.int32).reshape(1)

    def kernel(mine, rows, weight, *rest):
        rest[-1][0] = jnp.dot(rows[...], weight[...], preferred_element_type=f32).astype(bf)

    return pl.pallas_call(
        kernel,
        out_shape=shaped((parts, n, cols), bf),
        grid_spec=pltpu.PrefetchScalarGridSpec(
            num_scalar_prefetch=1,
            grid=(parts,),
            in_specs=[
                pl.BlockSpec((n, width), lambda i, m: (0, 0)),
                pl.BlockSpec((width, cols), lambda i, m: (0, m[0] ^ i)),
            ]
            + [ANY] * len(after),
            out_specs=pl.BlockSpec((1, n, cols), lambda i, m: (i, 0, 0)),
        ),
        compiler_params=pltpu.CompilerParams(vmem_limit_bytes=big),
        cost_estimate=pl.CostEstimate(
            flops=2 * n * width * weight.shape[1],
            bytes_accessed=2 * (rows.size + weight.size + n * weight.shape[1]),
            transcendentals=0,
        ),
    )(mine, rows, weight, *after)


def inner_up(place, rows, blocks, after):
    rank = blocks[0].shape[0] - spare
    n, cols = rows.shape

    def kernel(ins, outs):
        place, rows = ins[:2]
        acc = jnp.zeros((rank, n), f32)
        for k, block in enumerate(ins[2:]):
            part = lax.dot_general(
                block[:rank, :], rows[...], (((1,), (1,)), ((), ())), preferred_element_type=f32
            )
            acc = jnp.where(place[...] == k, part, acc)
        outs[0][...] = acc

    operands = (place, rows, *blocks)
    return call(
        kernel,
        [shaped((rank, n), f32)],
        operands,
        [VMEM] * len(operands),
        flops=2 * n * cols * rank * len(blocks),
        after=after,
    )[0]


def inner_down(slot_rows, rows, blocks, after):
    groups, rank, width = blocks.shape
    n = rows.shape[0]

    def kernel(ins, outs):
        slot, rows, blocks = ins
        acc = jnp.zeros((rank, n), f32)
        for s in range(groups):
            part = lax.dot_general(
                blocks[s], rows[...], (((1,), (1,)), ((), ())), preferred_element_type=f32
            )
            acc = jnp.where(slot[...] == s, part, acc)
        outs[0][...] = acc

    return call(
        kernel,
        [shaped((rank, n), f32)],
        (slot_rows, rows, blocks),
        [VMEM] * 3,
        flops=2 * n * width * rank * groups,
        after=after,
    )[0]


def sum_first(x, axis):
    k = 1
    while 2 * k < lax.axis_size(axis):
        x = x + swap(x, k, axis)
        k *= 2
    return x, swap(x, k, axis)


def spread(place, inner_t, k):
    return jnp.where(place == k, inner_t, jnp.zeros((), inner_t.dtype))


def down_grads(gst, slot_rows, score_rows, t, t_got, rows, up_blocks):
    groups = len(up_blocks)
    rank, n = t.shape
    width = rows.shape[1]

    def kernel(ins, outs):
        gst, slot, score, t, t_got, rows = ins[:6]
        me = lax.axis_index("dp")
        mine = gst[pl.ds(me, 1), :]
        sums = jnp.zeros((1, groups), f32)
        counts = jnp.zeros((1, groups), f32)
        for k, block in enumerate(ins[6:]):
            same = gst[pl.ds(me ^ k, 1), :] == mine
            x = block[rank:, :].astype(f32)
            sums += jnp.where(same, x[0:1, :groups], 0.0)
            counts += jnp.where(same, x[1:2, :groups], 0.0)
        mean = sums / jnp.maximum(counts, 1.0)
        here = lax.broadcasted_iota(jnp.int32, (groups, groups), 0) == lax.broadcasted_iota(
            jnp.int32, (groups, groups), 1
        )
        mean = jnp.sum(jnp.where(here, mean, 0.0), axis=1, keepdims=True)
        hot = slot[...] == lax.broadcasted_iota(jnp.int32, (groups, n), 0)
        adv = score[...].astype(f32) - jnp.sum(jnp.where(hot, mean, 0.0), axis=0, keepdims=True)
        total = (adv * (t[...] + t_got[...])).astype(bf)
        outs[0][...] = adv
        for s in range(groups):
            part = spread(slot[...], total, s)
            outs[1][s] = (scale * jnp.dot(part, rows[...], preferred_element_type=f32)).astype(bf)

    operands = (gst, slot_rows, score_rows, t, t_got, rows, *up_blocks)
    return call(
        kernel,
        [shaped((1, n), f32), shaped((groups, rank, width), bf)],
        operands,
        [VMEM] * len(operands),
        flops=2 * n * width * rank * groups,
    )


def up_grads(place, adv, t, t_got, cot, groups):
    rank, n = t.shape
    cols = cot.shape[1]

    def kernel(ins, outs):
        place, adv, t, t_got, cot = ins
        total = t[...] + t_got[...]
        outs[0][...] = total.astype(bf)
        total = (adv[...] * total).astype(bf)
        for k in range(groups):
            part = spread(place[...], total, k)
            outs[1 + k][...] = (
                scale * jnp.dot(part, cot[...], preferred_element_type=f32)
            ).astype(bf)

    out = call(
        kernel,
        [shaped((rank, n), bf)] + [shaped((rank, cols), bf)] * groups,
        (place, adv, t, t_got, cot),
        [VMEM] * 5,
        flops=2 * n * cols * rank * groups,
    )
    return out[0], out[1:]


def adapted(place, inner_t, base_mine, base_got, blocks, after):
    n, cols = base_got.shape
    rank = inner_t.shape[0]

    def kernel(ins, outs):
        place, t, base_mine, base_got = ins[:4]
        blocks = ins[4:]
        wide = jnp.concatenate([spread(place[...], t[...], k) for k in range(len(blocks))], axis=0)
        ups = jnp.concatenate([b[:rank, :] for b in blocks], axis=0)
        delta = lax.dot_general(wide, ups, (((0,), (0,)), ((), ())), preferred_element_type=f32)
        delta = (scale * delta).astype(bf).astype(f32)
        outs[0][...] = (base_mine[...].astype(f32) + base_got[...].astype(f32) + delta).astype(bf)

    operands = (place, inner_t, base_mine, base_got, *blocks)
    return call(
        kernel,
        [shaped((n, cols), bf)],
        operands,
        [VMEM] * len(operands),
        flops=2 * n * cols * rank * len(blocks),
        after=after,
    )[0]


def combine(gst, trp, blocks, tasks, stacked, after):
    groups = gst.shape[0]
    rank, width = blocks[0].shape[-2:]
    chunk = 4 if tasks % 4 == 0 else 1

    def run(gst, trp, *refs):
        ins = refs[: len(blocks)]
        out, acc = refs[-2:]
        me = lax.axis_index("dp")
        rows = [
            lax.rem(trp[gst[g if stacked else me ^ g, me]], tasks) for g in range(groups)
        ]
        read = [ins[0].at[g] if stacked else ins[g] for g in range(groups)]
        for j in range(chunk):
            here = pl.program_id(0) * chunk + j
            hits = jnp.int32(0)
            for r in rows:
                hits += (r == here).astype(jnp.int32)

            @pl.when(hits == 0)
            def _():
                out[j] = jnp.zeros((rank, width), bf)

            @pl.when(hits == 1)
            def _():
                for g, r in enumerate(rows):

                    @pl.when(r == here)
                    def _():
                        out[j] = read[g][...]

            @pl.when(hits > 1)
            def _():
                acc[...] = jnp.zeros((rank, width), f32)
                for g, r in enumerate(rows):

                    @pl.when(r == here)
                    def _():
                        acc[...] += read[g][...].astype(f32)

                out[j] = acc[...].astype(bf)

    return pl.pallas_call(
        run,
        out_shape=shaped((tasks, rank, width), bf),
        grid=(tasks // chunk,),
        in_specs=[SMEM, SMEM] + [VMEM] * len(blocks) + [ANY] * len(after),
        out_specs=pl.BlockSpec((chunk, rank, width), lambda t: (t, 0, 0)),
        scratch_shapes=[pltpu.VMEM((rank, width), f32)],
        compiler_params=pltpu.CompilerParams(vmem_limit_bytes=big),
        cost_estimate=pl.CostEstimate(
            flops=0,
            bytes_accessed=2 * (groups + tasks) * rank * width,
            transcendentals=0,
        ),
    )(gst, trp, *blocks, *after)


def exchange(x):
    return lax.all_to_all(x, "dp", split_axis=0, concat_axis=0, tiled=True)


def body(hidden, weight, down, up, slot, gst, trp, scores, cotangent):
    groups, parts = lax.axis_size("dp"), lax.axis_size("tensor")
    me = lax.axis_index("dp")
    att, steps, width = hidden.shape
    cols = cotangent.shape[2]
    n = att * steps
    tasks = down.shape[0]
    down = jnp.swapaxes(down, 1, 2)

    slot_row = slot.reshape(1, att)
    score_row = scores.reshape(1, att)
    up_out = pack_up(gst, trp, up, slot_row, score_row)
    up_got = [up_out[0]] + [swap(up_out[k], k, "dp") for k in range(1, groups)]
    down_out = pack_down(gst, trp, down, (up_out[0],))
    down_got = exchange(lax.optimization_barrier((down_out, *up_got))[0])

    hidden, cotangent, slot_row, score_row, _ = lax.optimization_barrier(
        (hidden, cotangent, slot_row, score_row, down_out)
    )
    slot_rows = jnp.repeat(slot_row, steps, axis=1)
    score_rows = jnp.repeat(score_row, steps, axis=1)
    place = slot_rows ^ me
    cot = cotangent.reshape(n, cols)
    rows = hidden.reshape(n, width)

    base = base_parts(rows, weight, parts, (down_out,))
    held = [base[i] for i in range(parts)]
    k = 1
    while 2 * k < parts:
        got = swap(jnp.stack(held[1::2]), k, "tensor")
        held = [
            (a.astype(f32) + got[i].astype(f32)).astype(bf) for i, a in enumerate(held[0::2])
        ]
        k *= 2
    base_mine, base_got = held[0], swap(held[1], k, "tensor")

    back = inner_up(place, cot, up_got, (base,))
    back, back_got = sum_first(back, "tensor")
    adv, down_grad = down_grads(gst, slot_rows, score_rows, back, back_got, rows, up_got)
    down_grad_got = exchange(down_grad)

    ahead = inner_down(slot_rows, rows, down_got, (adv,))
    ahead, ahead_got = sum_first(ahead, "tensor")
    inner_all, up_grad = up_grads(place, adv, ahead, ahead_got, cot, groups)
    up_grad_got = [up_grad[0]] + [swap(up_grad[k], k, "dp") for k in range(1, groups)]
    kv_new = adapted(place, inner_all, base_mine, base_got, up_got, (up_grad[0],))
    kv_out = kv_new.reshape(att, steps, cols)

    grad_down = combine(gst, trp, [down_grad_got], tasks, True, (kv_new,))
    grad_up = combine(gst, trp, up_grad_got, tasks, False, (grad_down,))
    return (kv_out, jnp.swapaxes(grad_down, 1, 2), grad_up)


def solution(mesh):
    in_specs = (
        P("dp", None, "tensor"),
        P("tensor", None),
        P("dp", "tensor", None),
        P("dp", None, "tensor"),
        P("dp", None),
        P(),
        P(),
        P("dp"),
        P("dp", None, "tensor"),
    )
    out_specs = (P("dp", None, "tensor"), P("dp", "tensor", None), P("dp", None, "tensor"))
    return jax.shard_map(body, mesh=mesh, in_specs=in_specs, out_specs=out_specs, check_vma=False)
```

time: 267 us -> 149 us (0.56)
  waiting for transfers between devices: 118 us -> 47.1 us
  Pallas kernels: 0 us -> 45.8 us
  blocking collectives: 45.1 us -> 0 us
  matrix products: 30.7 us -> 0 us
  local copies, waits for them, and re-layouts: 25 us -> 9.59 us
  starting transfers between devices: 26.9 us -> 41.3 us
  between operations: 14.2 us -> 0.95 us
    all_to_all x4 -> x2, waiting for transfers between devices: 118 us -> 27.2 us  [exchange(): return lax.all_to_all(x, 'dp', split_axis=0, concat_axis=0, tiled=True)]
    pallas_call x0 -> x10, Pallas kernels: none -> 45.8 us  [the longest x7 29.4 us: call(): pl.pallas_call(run, out_shape=list(outs), in_specs=list(specs) + [ANY] *...]
    psum x2 -> x0, blocking collectives: 45.1 us -> none  [the longest x1 32 us: body(): score_sums, task_counts = lax.psum((sums_local, counts_local), 'dp')]
    ppermute x0 -> x20, starting transfers between devices: none -> 31.1 us  [swap(): return lax.ppermute(x, axis, [(i, i ^ k) for i in range(n)])]
    dot_general x10 -> x0, matrix products: 30.7 us -> none  [the longest x1 10.5 us: body(): jnp.dot(flat_rows, key_value_weight, preferred_element_type=jnp.float32)]
    ppermute x0 -> x20, waiting for transfers between devices: none -> 19.8 us  [swap(): return lax.ppermute(x, axis, [(i, i ^ k) for i in range(n)])]
    all_to_all x4 -> x2, starting transfers between devices: 26.9 us -> 10.2 us  [exchange(): return lax.all_to_all(x, 'dp', split_axis=0, concat_axis=0, tiled=True)]
    mul x2 -> x0, local copies, waits for them, and re-layouts: 5.98 us -> none  [the longest x1 4.4 us: body(): adapter_output_scale * jnp.einsum('nd,nsr->sdr', flat_rows, back_spread,...]
  transfers between devices with their start and end apart: 5 -> 22, of which waited for: 3 -> 9; matrix products, arithmetic and copies ran while one was open for 17% -> 7% of each run, Pallas kernels for 0% -> 27%
where the time goes in v2:
time: 149 us; the launch traced here: 148 us
  waiting for transfers between devices  47.1 us (32%)
  Pallas kernels  45.8 us (31%)
  starting transfers between devices  41.3 us (28%)
  local copies, waits for them, and re-layouts  9.59 us (6%)
  other arithmetic  3.8 us (3%)
    ppermute x20, starting transfers between devices, swap(): return lax.ppermute(x, axis, [(i, i ^ k) for i in range(n)])  31.1 us
    pallas_call x7, Pallas kernels, call(): pl.pallas_call(run, out_shape=list(outs), in_specs=list(specs) + [ANY] *...  29.4 us
    all_to_all x2, waiting for transfers between devices, exchange(): return lax.all_to_all(x, 'dp', split_axis=0, concat_axis=0, tiled=True)  27.2 us
    ppermute x20, waiting for transfers between devices, swap(): return lax.ppermute(x, axis, [(i, i ^ k) for i in range(n)])  19.8 us
    all_to_all x2, starting transfers between devices, exchange(): return lax.all_to_all(x, 'dp', split_axis=0, concat_axis=0, tiled=True)  10.2 us
    pallas_call x1, Pallas kernels, base_parts(): pl.pallas_call(kernel, out_shape=shaped((parts, n, cols), bf), grid_spec=...  8.77 us
    pallas_call x2, Pallas kernels, combine(): pl.pallas_call(run, out_shape=shaped((tasks, rank, width), bf), grid=(tas...  7.64 us
    unnamed x50, local copies, waits for them, and re-layouts  3.25 us
  transfers between devices with their start and end apart: 22, of which 9 were waited for; matrix products, arithmetic and copies ran while one was open for 7% of the time, Pallas kernels for 27%

profile of v2, /device:TPU:0, one launch (start us, length us, event | category | flops | bytes accessed | tf_op | source)
XLA Modules:
  0.0 148.5 jit_solution(17354252736572168782)
XLA Ops:
  0.6 2.7 %shard_map.112 = (bf16[80,512]{1,0:T(8,128)(2,1)}, bf16[80,512]{1,0:T(8,128)(2,1)}, bf16[80,512]{1,0:T(8,128)(2,1)}, bf16[80,512]{1,0:T(8,128)(2,1)}, bf16[80,51...) custom-call(s32[8,8]{1,0:T(8,128)} %gst.3, s32[128]{0:T(128)} %trp.3, ...), custom_call_target="tpu_custom_call" | custom-call | bytes 1706752 | tf_op jit(solution)/shard_map/pallas_call | solution.py:32
  3.3 3.0 %collective-permute-start = (bf16[80,512]{1,0:T(8,128)(2,1)}, bf16[80,512]{1,0:T(8,128)(2,1)S(1)}, u32[]{:S(2)}, u32[]{:S(2)}) collective-permute-start(bf16[80,512]{1,0:T(8,128)(2,1)} %get-tuple-element.31), channel_id=1, source_target_pairs={{0,4},{4,0},{8,12},{12,8},{16,20},{20,16},{24,28},{28,24},{1,5},{5... | collective-permute-start | bytes 245768 | tf_op jit(solution)/shard_map/ppermute | solution.py:45
  6.4 1.6 %collective-permute-start.1 = (bf16[80,512]{1,0:T(8,128)(2,1)}, bf16[80,512]{1,0:T(8,128)(2,1)S(1)}, u32[]{:S(2)}, u32[]{:S(2)}) collective-permute-start(bf16[80,512]{1,0:T(8,128)(2,1)} %get-tuple-element.32), channel_id=1, source_target_pairs={{0,8},{4,12},{8,0},{12,4},{16,24},{20,28},{24,16},{28,20},{1,9},{5... | collective-permute-start | bytes 245768 | tf_op jit(solution)/shard_map/ppermute | solution.py:45
  7.9 3.0 %collective-permute-start.3 = (bf16[80,512]{1,0:T(8,128)(2,1)}, bf16[80,512]{1,0:T(8,128)(2,1)S(1)}, u32[]{:S(2)}, u32[]{:S(2)}) collective-permute-start(bf16[80,512]{1,0:T(8,128)(2,1)} %get-tuple-element.34), channel_id=1, source_target_pairs={{0,16},{4,20},{8,24},{12,28},{16,0},{20,4},{24,8},{28,12},{1,17},{... | collective-permute-start | bytes 245768 | tf_op jit(solution)/shard_map/ppermute | solution.py:45
  12.2 3.6 %collective-permute-start.5 = (bf16[80,512]{1,0:T(8,128)(2,1)}, bf16[80,512]{1,0:T(8,128)(2,1)S(1)}, u32[]{:S(2)}, u32[]{:S(2)}) collective-permute-start(bf16[80,512]{1,0:T(8,128)(2,1)} %get-tuple-element.36), channel_id=1, source_target_pairs={{0,24},{4,28},{8,16},{12,20},{16,8},{20,12},{24,0},{28,4},{1,25},{... | collective-permute-start | bytes 245768 | tf_op jit(solution)/shard_map/ppermute | solution.py:45
  15.9 3.7 %shard_map.113.rest_0_ = bf16[8,64,2048]{2,1,0:T(8,128)(2,1)} custom-call(s32[8,8]{1,0:T(8,128)} %gst.3, s32[128]{0:T(128)} %trp.3, bf16[16,64,2048]{2,1,0:T(8,128)(2,1)} %bitcast.12, bf16[80,512]{1,0:T(8,128)(2,1)} %get-tuple-element.27.refs_3_.refs_2_.refs_6_.refs_4_), custom_call_target="tpu_custom_call" | custom-call | bytes 6292224 | tf_op jit(solution)/shard_map/pallas_call | solution.py:32
  19.7 4.7 %collective-permute-done.4.refs_7_.refs_11_.refs_9_ = bf16[80,512]{1,0:T(8,128)(2,1)S(1)} collective-permute-done((bf16[80,512]{1,0:T(8,128)(2,1)}, bf16[80,512]{1,0:T(8,128)(2,1)S(1)}, u32[]{:S(2)}, u32[]{:S(2)}) %collective-permute-start.4) | collective-permute-done | bytes 81952 | tf_op jit(solution)/shard_map/ppermute | solution.py:45
  25.1 5.5 %all-to-all-start = ((bf16[8,64,2048]{2,1,0:T(8,128)(2,1)}), bf16[8,64,2048]{2,1,0:T(8,128)(2,1)}, u32[]{:S(2)}, u32[]{:S(2)}) async-start(bf16[8,64,2048]{2,1,0:T(8,128)(2,1)} %shard_map.113.rest_0_), calls=%async_computation | async-start | bytes 4194304 | tf_op jit(solution)/shard_map/all_to_all | solution.py:355
  31.9 2.2 %reshape.61.rows.refs_5_.refs_1_ = bf16[512,2048]{1,0:T(8,128)(2,1)} reshape(bf16[256,2,2048]{2,1,0:T(2,128)(2,1)S(1)} %copy-done.1) | data formatting | bytes 4194304 | tf_op jit(solution)/shard_map/reshape | solution.py:381
  34.6 8.8 %shard_map.114.refs_10_ = bf16[4,512,512]{2,1,0:T(8,128)(2,1)} custom-call(s32[1]{0:T(128)} %bitcast.5.mine, bf16[512,2048]{1,0:T(8,128)(2,1)} %reshape.61.rows.refs_5_.refs_1_, bf16[2048,2048]{1,0:T(8,128)(2,1)} %weight.1, bf16[8,64,2048]{2,1,0:T(8,128)(2,1)} %shard_map.113.rest_0_), custom_call_target="tpu_custom_call" | custom-call | flops 4294967296 | bytes 12582912 | tf_op jit(solution)/shard_map/pallas_call | solution.py:125
  43.4 3.3 %shard_map.115 = f32[64,512]{1,0:T(8,128)} custom-call(s32[1,512]{1,0:T(1,128)} %broadcast_xor_fusion.refs_0_, bf16[512,512]{1,0:T(8,128)(2,1)} %reshape.59.refs_1_.refs_4_, bf16[80,512]{1,0:T(8,128)(2,1)} %get-tuple-element.27.refs_3_.refs_2_.refs_6_.refs_4_, bf16[80,512]{1,0:T(8,128)(2,1)} %copy-done.4, bf16[80,512]{1,0:T(8,128)(2,1)} %copy-done.5, ...), custom_call_target="tpu_custom_call" | custom-call | flops 268435456 | bytes 1312768 | tf_op jit(solution)/shard_map/pallas_call | solution.py:32
  46.7 1.6 %collective-permute-done.7 = f32[64,512]{1,0:T(8,128)S(1)} collective-permute-done((f32[64,512]{1,0:T(8,128)}, f32[64,512]{1,0:T(8,128)S(1)}, u32[]{:S(2)}, u32[]{:S(2)}) %collective-permute-start.7) | collective-permute-done | bytes 131104 | tf_op jit(solution)/shard_map/ppermute | solution.py:45
  49.2 1.6 %collective-permute-start.8 = (f32[64,512]{1,0:T(8,128)S(1)}, f32[64,512]{1,0:T(8,128)S(1)}, u32[]{:S(2)}, u32[]{:S(2)}) collective-permute-start(f32[64,512]{1,0:T(8,128)S(1)} %add.14.refs_3_), channel_id=1, source_target_pairs={{0,2},{1,3},{2,0},{3,1},{4,6},{5,7},{6,4},{7,5},{8,10},{9,11},{10,... | collective-permute-start | bytes 393224 | tf_op jit(solution)/shard_map/ppermute | solution.py:45
  51.6 3.2 %collective-permute-done.8.refs_4_ = f32[64,512]{1,0:T(8,128)S(1)} collective-permute-done((f32[64,512]{1,0:T(8,128)S(1)}, f32[64,512]{1,0:T(8,128)S(1)}, u32[]{:S(2)}, u32[]{:S(2)}) %collective-permute-start.8) | collective-permute-done | bytes 131104 | tf_op jit(solution)/shard_map/ppermute | solution.py:45
  55.4 6.3 %shard_map.116 = (f32[1,512]{1,0:T(1,128)}, bf16[8,64,2048]{2,1,0:T(8,128)(2,1)}) custom-call(s32[8,8]{1,0:T(8,128)} %gst.3, s32[1,512]{1,0:T(1,128)} %copy-done.20, s32[1,512]{1,0:T(1,128)} %broadcast_in_dim.13.refs_2_, f32[64,512]{1,0:T(8,128)} %copy-done.12, f32[64,512]{1,0:T(8,128)} %copy-done.24, bf16[512,2048]{1,0:T(8,128)(2,1)} %reshape.61.rows.refs_5_.refs_1_, ...), custom_call_target="tpu_custom_call" | custom-call | flops 1073741824 | bytes 5118208 | tf_op jit(solution)/shard_map/pallas_call | solution.py:32
  61.7 18.0 %all-to-all-done.refs_2_ = bf16[8,64,2048]{2,1,0:T(8,128)(2,1)} async-done(((bf16[8,64,2048]{2,1,0:T(8,128)(2,1)}), bf16[8,64,2048]{2,1,0:T(8,128)(2,1)}, u32[]{:S(2)}, u32[]{:S(2)}) %all-to-all-start) | async-done | bytes 2097184 | tf_op jit(solution)/shard_map/all_to_all | solution.py:355
  79.8 4.7 %all-to-all-start.1 = ((bf16[8,64,2048]{2,1,0:T(8,128)(2,1)}), bf16[8,64,2048]{2,1,0:T(8,128)(2,1)}, u32[]{:S(2)}, u32[]{:S(2)}) async-start(bf16[8,64,2048]{2,1,0:T(8,128)(2,1)} %get-tuple-element.43), calls=%async_computation.1 | async-start | bytes 4194304 | tf_op jit(solution)/shard_map/all_to_all | solution.py:355
  84.7 2.6 %collective-permute-done.11 = bf16[2,512,512]{2,1,0:T(8,128)(2,1)S(1)} collective-permute-done((bf16[2,512,512]{2,1,0:T(8,128)(2,1)S(1)}, bf16[2,512,512]{2,1,0:T(8,128)(2,1)S(1)}, u32[]{:S(2)}, u32[]{:S(2)}) %collective-permute-start.11) | collective-permute-done | bytes 1048608 | tf_op jit(solution)/shard_map/ppermute | solution.py:45
  88.6 1.5 %collective-permute-start.12 = (bf16[512,512]{1,0:T(8,128)(2,1)}, bf16[512,512]{1,0:T(8,128)(2,1)S(1)}, u32[]{:S(2)}, u32[]{:S(2)}) collective-permute-start(bf16[512,512]{1,0:T(8,128)(2,1)} %get-tuple-element.51), channel_id=1, source_target_pairs={{0,2},{1,3},{2,0},{3,1},{4,6},{5,7},{6,4},{7,5},{8,10},{9,11},{10,... | collective-permute-start | bytes 1572872 | tf_op jit(solution)/shard_map/ppermute | solution.py:45
  90.2 8.0 %shard_map.117 = f32[64,512]{1,0:T(8,128)} custom-call(s32[1,512]{1,0:T(1,128)} %copy-done.20, bf16[512,2048]{1,0:T(8,128)(2,1)} %reshape.61.rows.refs_5_.refs_1_, bf16[8,64,2048]{2,1,0:T(8,128)(2,1)} %all-to-all-done.refs_2_, f32[1,512]{1,0:T(1,128)} %get-tuple-element.39.refs_3_.refs_1_), custom_call_target="tpu_custom_call" | custom-call | flops 1073741824 | bytes 4327424 | tf_op jit(solution)/shard_map/pallas_call | solution.py:32
  98.2 1.6 %collective-permute-done.9 = f32[64,512]{1,0:T(8,128)S(1)} collective-permute-done((f32[64,512]{1,0:T(8,128)}, f32[64,512]{1,0:T(8,128)S(1)}, u32[]{:S(2)}, u32[]{:S(2)}) %collective-permute-start.9) | collective-permute-done | bytes 131104 | tf_op jit(solution)/shard_map/ppermute | solution.py:45
  101.2 5.0 %collective-permute-done.10.refs_3_ = f32[64,512]{1,0:T(8,128)S(1)} collective-permute-done((f32[64,512]{1,0:T(8,128)S(1)}, f32[64,512]{1,0:T(8,128)S(1)}, u32[]{:S(2)}, u32[]{:S(2)}) %collective-permute-start.10) | collective-permute-done | bytes 131104 | tf_op jit(solution)/shard_map/ppermute | solution.py:45
  106.9 2.6 %shard_map.118 = (bf16[64,512]{1,0:T(8,128)(2,1)}, bf16[64,512]{1,0:T(8,128)(2,1)}, bf16[64,512]{1,0:T(8,128)(2,1)}, bf16[64,512]{1,0:T(8,128)(2,1)}, bf16[64,51...) custom-call(s32[1,512]{1,0:T(1,128)} %broadcast_xor_fusion.refs_0_, ...), custom_call_target="tpu_custom_call" | custom-call | flops 268435456 | bytes 1380352 | tf_op jit(solution)/shard_map/pallas_call | solution.py:32
  109.6 1.7 %collective-permute-start.13 = (bf16[64,512]{1,0:T(8,128)(2,1)}, bf16[64,512]{1,0:T(8,128)(2,1)S(1)}, u32[]{:S(2)}, u32[]{:S(2)}) collective-permute-start(bf16[64,512]{1,0:T(8,128)(2,1)} %get-tuple-element.44), channel_id=1, source_target_pairs={{0,4},{4,0},{8,12},{12,8},{16,20},{20,16},{24,28},{28,24},{1,5},{5... | collective-permute-start | bytes 196616 | tf_op jit(solution)/shard_map/ppermute | solution.py:45
  113.1 2.6 %collective-permute-start.16 = (bf16[64,512]{1,0:T(8,128)(2,1)}, bf16[64,512]{1,0:T(8,128)(2,1)S(1)}, u32[]{:S(2)}, u32[]{:S(2)}) collective-permute-start(bf16[64,512]{1,0:T(8,128)(2,1)} %get-tuple-element.47), channel_id=1, source_target_pairs={{0,16},{4,20},{8,24},{12,28},{16,0},{20,4},{24,8},{28,12},{1,17},{... | collective-permute-start | bytes 196616 | tf_op jit(solution)/shard_map/ppermute | solution.py:45
  117.1 3.3 %collective-permute-start.18 = (bf16[64,512]{1,0:T(8,128)(2,1)}, bf16[64,512]{1,0:T(8,128)(2,1)S(1)}, u32[]{:S(2)}, u32[]{:S(2)}) collective-permute-start(bf16[64,512]{1,0:T(8,128)(2,1)} %get-tuple-element.49), channel_id=1, source_target_pairs={{0,24},{4,28},{8,16},{12,20},{16,8},{20,12},{24,0},{28,4},{1,25},{... | collective-permute-start | bytes 196616 | tf_op jit(solution)/shard_map/ppermute | solution.py:45
  121.5 4.0 %collective-permute-start.19 = (bf16[64,512]{1,0:T(8,128)(2,1)}, bf16[64,512]{1,0:T(8,128)(2,1)S(1)}, u32[]{:S(2)}, u32[]{:S(2)}) collective-permute-start(bf16[64,512]{1,0:T(8,128)(2,1)} %get-tuple-element.50), channel_id=1, source_target_pairs={{0,28},{4,24},{8,20},{12,16},{16,12},{20,8},{24,4},{28,0},{1,29},{... | collective-permute-start | bytes 196616 | tf_op jit(solution)/shard_map/ppermute | solution.py:45
  125.6 2.7 %shard_map.119.refs_1_ = bf16[512,512]{1,0:T(8,128)(2,1)} custom-call(s32[1,512]{1,0:T(1,128)} %broadcast_xor_fusion.refs_0_, bf16[64,512]{1,0:T(8,128)(2,1)} %get-tuple-element.41.refs_1_, bf16[512,512]{1,0:T(8,128)(2,1)} %get-tuple-element.52.refs_2_, bf16[512,512]{1,0:T(8,128)(2,1)} %copy-done.3, ...), custom_call_target="tpu_custom_call" | custom-call | flops 268435456 | bytes 2295808 | tf_op jit(solution)/shard_map/pallas_call | solution.py:32
  128.3 2.0 %reshape.62 = bf16[256,2,512]{2,1,0:T(2,128)(2,1)} reshape(bf16[512,512]{1,0:T(8,128)(2,1)} %shard_map.119.refs_1_) | data formatting | bytes 1048576 | tf_op jit(solution)/shard_map/reshape | solution.py:404
  130.3 9.2 %all-to-all-done.1.refs_0_ = bf16[8,64,2048]{2,1,0:T(8,128)(2,1)} async-done(((bf16[8,64,2048]{2,1,0:T(8,128)(2,1)}), bf16[8,64,2048]{2,1,0:T(8,128)(2,1)}, u32[]{:S(2)}, u32[]{:S(2)}) %all-to-all-start.1) | async-done | bytes 2097184 | tf_op jit(solution)/shard_map/all_to_all | solution.py:355
  139.5 4.5 %shard_map.120.refs_8_ = bf16[16,64,2048]{2,1,0:T(8,128)(2,1)} custom-call(s32[8,8]{1,0:T(8,128)} %gst.3, s32[128]{0:T(128)} %trp.3, bf16[8,64,2048]{2,1,0:T(8,128)(2,1)} %all-to-all-done.1.refs_0_, bf16[512,512]{1,0:T(8,128)(2,1)} %shard_map.119.refs_1_), custom_call_target="tpu_custom_call" | custom-call | bytes 6291456 | tf_op jit(solution)/shard_map/pallas_call | solution.py:338
  145.3 3.2 %shard_map.121 = bf16[16,64,512]{2,1,0:T(8,128)(2,1)} custom-call(s32[8,8]{1,0:T(8,128)} %gst.3, s32[128]{0:T(128)} %trp.3, bf16[64,512]{1,0:T(8,128)(2,1)} %get-tuple-element.42.refs_12_.refs_0_, bf16[64,512]{1,0:T(8,128)(2,1)} %copy-done.13, bf16[64,512]{1,0:T(8,128)(2,1)} %copy-done.14, bf16[64,512]{1,0:T(8,128)(2,1)} %copy-done.15, ...), custom_call_target="tpu_custom_call" | custom-call | bytes 1572864 | tf_op jit(solution)/shard_map/pallas_call | solution.py:338
  (85 shorter events, 15.5 us)
Async XLA Ops:
  3.3 8.9 %collective-permute-start = (bf16[80,512]{1,0:T(8,128)(2,1)}, bf16[80,512]{1,0:T(8,128)(2,1)S(1)}, u32[]{:S(2)}, u32[]{:S(2)}) collective-permute-start(bf16[80,512]{1,0:T(8,128)(2,1)} %get-tuple-element.31), channel_id=1, source_target_pairs={{0,4},{4,0},{8,12},{12,8},{16,20},{20,16},{24,28},{28,24},{1,5},{5... | collective-permute-start | bytes 245768 | tf_op jit(solution)/shard_map/ppermute | solution.py:45
  6.4 9.5 %collective-permute-start.1 = (bf16[80,512]{1,0:T(8,128)(2,1)}, bf16[80,512]{1,0:T(8,128)(2,1)S(1)}, u32[]{:S(2)}, u32[]{:S(2)}) collective-permute-start(bf16[80,512]{1,0:T(8,128)(2,1)} %get-tuple-element.32), channel_id=1, source_target_pairs={{0,8},{4,12},{8,0},{12,4},{16,24},{20,28},{24,16},{28,20},{1,9},{5... | collective-permute-start | bytes 245768 | tf_op jit(solution)/shard_map/ppermute | solution.py:45
  7.9 11.7 %collective-permute-start.2 = (bf16[80,512]{1,0:T(8,128)(2,1)}, bf16[80,512]{1,0:T(8,128)(2,1)S(1)}, u32[]{:S(2)}, u32[]{:S(2)}) collective-permute-start(bf16[80,512]{1,0:T(8,128)(2,1)} %get-tuple-element.33), channel_id=1, source_target_pairs={{0,12},{4,8},{8,4},{12,0},{16,28},{20,24},{24,20},{28,16},{1,13},{... | collective-permute-start | bytes 245768 | tf_op jit(solution)/shard_map/ppermute | solution.py:45
  7.9 11.7 %collective-permute-start.3 = (bf16[80,512]{1,0:T(8,128)(2,1)}, bf16[80,512]{1,0:T(8,128)(2,1)S(1)}, u32[]{:S(2)}, u32[]{:S(2)}) collective-permute-start(bf16[80,512]{1,0:T(8,128)(2,1)} %get-tuple-element.34), channel_id=1, source_target_pairs={{0,16},{4,20},{8,24},{12,28},{16,0},{20,4},{24,8},{28,12},{1,17},{... | collective-permute-start | bytes 245768 | tf_op jit(solution)/shard_map/ppermute | solution.py:45
  10.9 13.4 %collective-permute-start.4 = (bf16[80,512]{1,0:T(8,128)(2,1)}, bf16[80,512]{1,0:T(8,128)(2,1)S(1)}, u32[]{:S(2)}, u32[]{:S(2)}) collective-permute-start(bf16[80,512]{1,0:T(8,128)(2,1)} %get-tuple-element.35), channel_id=1, source_target_pairs={{0,20},{4,16},{8,28},{12,24},{16,4},{20,0},{24,12},{28,8},{1,21},{... | collective-permute-start | bytes 245768 | tf_op jit(solution)/shard_map/ppermute | solution.py:45
  12.2 7.3 %copy-start.4 = (bf16[80,512]{1,0:T(8,128)(2,1)}, bf16[80,512]{1,0:T(8,128)(2,1)S(1)}, u32[]{:S(2)}) copy-start(bf16[80,512]{1,0:T(8,128)(2,1)S(1)} %collective-permute-done.refs_3_.refs_7_.refs_5_) | copy-start | bytes 245764
  12.2 12.2 %collective-permute-start.5 = (bf16[80,512]{1,0:T(8,128)(2,1)}, bf16[80,512]{1,0:T(8,128)(2,1)S(1)}, u32[]{:S(2)}, u32[]{:S(2)}) collective-permute-start(bf16[80,512]{1,0:T(8,128)(2,1)} %get-tuple-element.36), channel_id=1, source_target_pairs={{0,24},{4,28},{8,16},{12,20},{16,8},{20,12},{24,0},{28,4},{1,25},{... | collective-permute-start | bytes 245768 | tf_op jit(solution)/shard_map/ppermute | solution.py:45
  15.8 8.6 %collective-permute-start.6 = (bf16[80,512]{1,0:T(8,128)(2,1)}, bf16[80,512]{1,0:T(8,128)(2,1)S(1)}, u32[]{:S(2)}, u32[]{:S(2)}) collective-permute-start(bf16[80,512]{1,0:T(8,128)(2,1)} %get-tuple-element.37), channel_id=1, source_target_pairs={{0,28},{4,24},{8,20},{12,16},{16,12},{20,8},{24,4},{28,0},{1,29},{... | collective-permute-start | bytes 245768 | tf_op jit(solution)/shard_map/ppermute | solution.py:45
  19.6 11.0 %copy-start.21 = (s32[256,1]{0,1:T(1,128)S(1)}, s32[256,1]{0,1:T(1,128)}, u32[]{:S(2)}) copy-start(s32[256,1]{0,1:T(1,128)} %param.13) | copy-start | bytes 3076
  19.6 11.3 %copy-start.2 = (bf16[256,2,512]{2,1,0:T(2,128)(2,1)S(1)}, bf16[256,2,512]{2,1,0:T(2,128)(2,1)}, u32[]{:S(2)}) copy-start(bf16[256,2,512]{2,1,0:T(2,128)(2,1)} %param.17) | copy-start | bytes 1572868
  19.6 12.3 %copy-start.1 = (bf16[256,2,2048]{2,1,0:T(2,128)(2,1)S(1)}, bf16[256,2,2048]{2,1,0:T(2,128)(2,1)}, u32[]{:S(2)}) copy-start(bf16[256,2,2048]{2,1,0:T(2,128)(2,1)} %param.9) | copy-start | bytes 6291460
  25.1 54.7 %all-to-all-start = ((bf16[8,64,2048]{2,1,0:T(8,128)(2,1)}), bf16[8,64,2048]{2,1,0:T(8,128)(2,1)}, u32[]{:S(2)}, u32[]{:S(2)}) async-start(bf16[8,64,2048]{2,1,0:T(8,128)(2,1)} %shard_map.113.rest_0_), calls=%async_computation | async-start | bytes 4194304 | tf_op jit(solution)/shard_map/all_to_all | solution.py:355
  43.4 7.4 %copy-start.22 = (s32[256]{0:T(256)S(1)}, s32[256]{0:T(256)}, u32[]{:S(2)}) copy-start(s32[256]{0:T(256)} %param.16) | copy-start | bytes 3076
  46.7 1.6 %collective-permute-start.7 = (f32[64,512]{1,0:T(8,128)}, f32[64,512]{1,0:T(8,128)S(1)}, u32[]{:S(2)}, u32[]{:S(2)}) collective-permute-start(f32[64,512]{1,0:T(8,128)} %shard_map.115), channel_id=1, source_target_pairs={{0,1},{1,0},{2,3},{3,2},{4,5},{5,4},{6,7},{7,6},{8,9},{9,8},{10,11... | collective-permute-start | bytes 393224 | tf_op jit(solution)/shard_map/ppermute | solution.py:45
  49.2 5.6 %copy-start.12 = (f32[64,512]{1,0:T(8,128)}, f32[64,512]{1,0:T(8,128)S(1)}, u32[]{:S(2)}) copy-start(f32[64,512]{1,0:T(8,128)S(1)} %add.14.refs_3_) | copy-start | bytes 393220
  49.2 5.6 %collective-permute-start.8 = (f32[64,512]{1,0:T(8,128)S(1)}, f32[64,512]{1,0:T(8,128)S(1)}, u32[]{:S(2)}, u32[]{:S(2)}) collective-permute-start(f32[64,512]{1,0:T(8,128)S(1)} %add.14.refs_3_), channel_id=1, source_target_pairs={{0,2},{1,3},{2,0},{3,1},{4,6},{5,7},{6,4},{7,5},{8,10},{9,11},{10,... | collective-permute-start | bytes 393224 | tf_op jit(solution)/shard_map/ppermute | solution.py:45
  79.8 59.8 %all-to-all-start.1 = ((bf16[8,64,2048]{2,1,0:T(8,128)(2,1)}), bf16[8,64,2048]{2,1,0:T(8,128)(2,1)}, u32[]{:S(2)}, u32[]{:S(2)}) async-start(bf16[8,64,2048]{2,1,0:T(8,128)(2,1)} %get-tuple-element.43), calls=%async_computation.1 | async-start | bytes 4194304 | tf_op jit(solution)/shard_map/all_to_all | solution.py:355
  84.6 2.7 %collective-permute-start.11 = (bf16[2,512,512]{2,1,0:T(8,128)(2,1)S(1)}, bf16[2,512,512]{2,1,0:T(8,128)(2,1)S(1)}, u32[]{:S(2)}, u32[]{:S(2)}) collective-permute-start(bf16[2,512,512]{2,1,0:T(8,128)(2,1)S(1)} %pad_maximum_fusion), channel_id=1, source_target_pairs={{0,1},{1,0},{2,3},{3,2},{4,5},{5,4},{6,7},{7,6},{8,9},{9,8},{10,11... | collective-permute-start | bytes 3145736 | tf_op jit(solution)/shard_map/ppermute | solution.py:45
  88.6 27.1 %collective-permute-start.12 = (bf16[512,512]{1,0:T(8,128)(2,1)}, bf16[512,512]{1,0:T(8,128)(2,1)S(1)}, u32[]{:S(2)}, u32[]{:S(2)}) collective-permute-start(bf16[512,512]{1,0:T(8,128)(2,1)} %get-tuple-element.51), channel_id=1, source_target_pairs={{0,2},{1,3},{2,0},{3,1},{4,6},{5,7},{6,4},{7,5},{8,10},{9,11},{10,... | collective-permute-start | bytes 1572872 | tf_op jit(solution)/shard_map/ppermute | solution.py:45
  98.2 1.6 %collective-permute-start.9 = (f32[64,512]{1,0:T(8,128)}, f32[64,512]{1,0:T(8,128)S(1)}, u32[]{:S(2)}, u32[]{:S(2)}) collective-permute-start(f32[64,512]{1,0:T(8,128)} %shard_map.117), channel_id=1, source_target_pairs={{0,1},{1,0},{2,3},{3,2},{4,5},{5,4},{6,7},{7,6},{8,9},{9,8},{10,11... | collective-permute-start | bytes 393224 | tf_op jit(solution)/shard_map/ppermute | solution.py:45
  100.7 5.6 %copy-start.11 = (f32[64,512]{1,0:T(8,128)}, f32[64,512]{1,0:T(8,128)S(1)}, u32[]{:S(2)}) copy-start(f32[64,512]{1,0:T(8,128)S(1)} %add.15.refs_2_) | copy-start | bytes 393220
  100.7 5.6 %collective-permute-start.10 = (f32[64,512]{1,0:T(8,128)S(1)}, f32[64,512]{1,0:T(8,128)S(1)}, u32[]{:S(2)}, u32[]{:S(2)}) collective-permute-start(f32[64,512]{1,0:T(8,128)S(1)} %add.15.refs_2_), channel_id=1, source_target_pairs={{0,2},{1,3},{2,0},{3,1},{4,6},{5,7},{6,4},{7,5},{8,10},{9,11},{10,... | collective-permute-start | bytes 393224 | tf_op jit(solution)/shard_map/ppermute | solution.py:45
  109.6 7.6 %collective-permute-start.13 = (bf16[64,512]{1,0:T(8,128)(2,1)}, bf16[64,512]{1,0:T(8,128)(2,1)S(1)}, u32[]{:S(2)}, u32[]{:S(2)}) collective-permute-start(bf16[64,512]{1,0:T(8,128)(2,1)} %get-tuple-element.44), channel_id=1, source_target_pairs={{0,4},{4,0},{8,12},{12,8},{16,20},{20,16},{24,28},{28,24},{1,5},{5... | collective-permute-start | bytes 196616 | tf_op jit(solution)/shard_map/ppermute | solution.py:45
  111.3 10.2 %collective-permute-start.14 = (bf16[64,512]{1,0:T(8,128)(2,1)}, bf16[64,512]{1,0:T(8,128)(2,1)S(1)}, u32[]{:S(2)}, u32[]{:S(2)}) collective-permute-start(bf16[64,512]{1,0:T(8,128)(2,1)} %get-tuple-element.45), channel_id=1, source_target_pairs={{0,8},{4,12},{8,0},{12,4},{16,24},{20,28},{24,16},{28,20},{1,9},{5... | collective-permute-start | bytes 196616 | tf_op jit(solution)/shard_map/ppermute | solution.py:45
  112.8 31.3 %collective-permute-start.15 = (bf16[64,512]{1,0:T(8,128)(2,1)}, bf16[64,512]{1,0:T(8,128)(2,1)S(1)}, u32[]{:S(2)}, u32[]{:S(2)}) collective-permute-start(bf16[64,512]{1,0:T(8,128)(2,1)} %get-tuple-element.46), channel_id=1, source_target_pairs={{0,12},{4,8},{8,4},{12,0},{16,28},{20,24},{24,20},{28,16},{1,13},{... | collective-permute-start | bytes 196616 | tf_op jit(solution)/shard_map/ppermute | solution.py:45
  113.1 31.0 %collective-permute-start.16 = (bf16[64,512]{1,0:T(8,128)(2,1)}, bf16[64,512]{1,0:T(8,128)(2,1)S(1)}, u32[]{:S(2)}, u32[]{:S(2)}) collective-permute-start(bf16[64,512]{1,0:T(8,128)(2,1)} %get-tuple-element.47), channel_id=1, source_target_pairs={{0,16},{4,20},{8,24},{12,28},{16,0},{20,4},{24,8},{28,12},{1,17},{... | collective-permute-start | bytes 196616 | tf_op jit(solution)/shard_map/ppermute | solution.py:45
  115.7 9.9 %copy-start.3 = (bf16[512,512]{1,0:T(8,128)(2,1)}, bf16[512,512]{1,0:T(8,128)(2,1)S(1)}, u32[]{:S(2)}) copy-start(bf16[512,512]{1,0:T(8,128)(2,1)S(1)} %collective-permute-done.12.refs_3_) | copy-start | bytes 1572868
  115.7 28.4 %collective-permute-start.17 = (bf16[64,512]{1,0:T(8,128)(2,1)}, bf16[64,512]{1,0:T(8,128)(2,1)S(1)}, u32[]{:S(2)}, u32[]{:S(2)}) collective-permute-start(bf16[64,512]{1,0:T(8,128)(2,1)} %get-tuple-element.48), channel_id=1, source_target_pairs={{0,20},{4,16},{8,28},{12,24},{16,4},{20,0},{24,12},{28,8},{1,21},{... | collective-permute-start | bytes 196616 | tf_op jit(solution)/shard_map/ppermute | solution.py:45
  117.1 26.9 %copy-start.13 = (bf16[64,512]{1,0:T(8,128)(2,1)}, bf16[64,512]{1,0:T(8,128)(2,1)S(1)}, u32[]{:S(2)}) copy-start(bf16[64,512]{1,0:T(8,128)(2,1)S(1)} %collective-permute-done.13.refs_1_) | copy-start | bytes 196612
  117.1 27.0 %collective-permute-start.18 = (bf16[64,512]{1,0:T(8,128)(2,1)}, bf16[64,512]{1,0:T(8,128)(2,1)S(1)}, u32[]{:S(2)}, u32[]{:S(2)}) collective-permute-start(bf16[64,512]{1,0:T(8,128)(2,1)} %get-tuple-element.49), channel_id=1, source_target_pairs={{0,24},{4,28},{8,16},{12,20},{16,8},{20,12},{24,0},{28,4},{1,25},{... | collective-permute-start | bytes 196616 | tf_op jit(solution)/shard_map/ppermute | solution.py:45
  121.5 22.5 %copy-start.14 = (bf16[64,512]{1,0:T(8,128)(2,1)}, bf16[64,512]{1,0:T(8,128)(2,1)S(1)}, u32[]{:S(2)}) copy-start(bf16[64,512]{1,0:T(8,128)(2,1)S(1)} %collective-permute-done.14.refs_2_) | copy-start | bytes 196612
  121.5 22.6 %collective-permute-start.19 = (bf16[64,512]{1,0:T(8,128)(2,1)}, bf16[64,512]{1,0:T(8,128)(2,1)S(1)}, u32[]{:S(2)}, u32[]{:S(2)}) collective-permute-start(bf16[64,512]{1,0:T(8,128)(2,1)} %get-tuple-element.50), channel_id=1, source_target_pairs={{0,28},{4,24},{8,20},{12,16},{16,12},{20,8},{24,4},{28,0},{1,29},{... | collective-permute-start | bytes 196616 | tf_op jit(solution)/shard_map/ppermute | solution.py:45
  (15 other events, 27.6 us)

commit v3 on v2

v3 whole, which is shorter than its diff:
```python
import functools

import jax
import jax.numpy as jnp
from jax import lax
from jax.experimental import pallas as pl
from jax.experimental.pallas import tpu as pltpu
from jax.sharding import PartitionSpec as P

scale = 0.25
bf = jnp.bfloat16
f32 = jnp.float32
big = 64 * 1024 * 1024
spare = 16
lanes = 128

ANY = pl.BlockSpec(memory_space=pl.ANY)
SMEM = pl.BlockSpec(memory_space=pltpu.SMEM)
VMEM = pl.BlockSpec(memory_space=pltpu.VMEM)


def shaped(shape, dtype):
    return jax.ShapeDtypeStruct(shape, dtype)


def call(kernel, outs, operands, specs, flops=0, scratch=(), after=(), vmem_outs=True):
    moved = sum(a.size * a.dtype.itemsize for a in list(operands) + list(outs))
    count = len(operands)

    def run(*refs):
        kernel(refs[:count], refs[count + len(after) :])

    return pl.pallas_call(
        run,
        out_shape=list(outs),
        in_specs=list(specs) + [ANY] * len(after),
        out_specs=[VMEM] * len(outs),
        scratch_shapes=list(scratch),
        compiler_params=pltpu.CompilerParams(vmem_limit_bytes=big),
        cost_estimate=pl.CostEstimate(flops=0, bytes_accessed=0, transcendentals=0),
    )(*operands, *after)


def swap(x, k, axis):
    n = lax.axis_size(axis)
    return lax.ppermute(x, axis, [(i, i ^ k) for i in range(n)])


def stored_row(gst, trp, tasks, k):
    me = lax.axis_index("dp")
    return lax.rem(trp[gst[me ^ k, me]], tasks)


def pack_up(gst, trp, up, slot_row, score_row):
    groups = gst.shape[0]
    tasks, rank, cols = up.shape
    tiles = cols // lanes

    def kernel(ins, outs):
        gst, trp, up, slot, score = ins
        sem = outs[-1]
        copies = []
        for k in reversed(range(groups)):
            row = stored_row(gst, trp, tasks, k)
            for j in range(tiles):
                copies.append(
                    pltpu.make_async_copy(
                        up.at[row, :, pl.ds(j * lanes, lanes)],
                        outs[k].at[pl.ds(j * rank, rank), :],
                        sem.at[k, j],
                    )
                )
                copies[-1].start()
        hot = slot[...] == lax.broadcasted_iota(jnp.int32, (groups, slot.shape[1]), 0)
        sums = jnp.sum(jnp.where(hot, score[...].astype(f32), 0.0), axis=1, keepdims=True)
        counts = jnp.sum(jnp.where(hot, 1.0, 0.0), axis=1, keepdims=True)
        here = lax.broadcasted_iota(jnp.int32, (groups, lanes), 0) == lax.broadcasted_iota(
            jnp.int32, (groups, lanes), 1
        )
        sums = jnp.sum(jnp.where(here, sums, 0.0), axis=0, keepdims=True)
        counts = jnp.sum(jnp.where(here, counts, 0.0), axis=0, keepdims=True)
        line = lax.broadcasted_iota(jnp.int32, (spare, lanes), 0)
        both = jnp.where(line == 0, sums, jnp.where(line == 1, counts, 0.0)).astype(bf)
        for k in range(groups):
            outs[k][tiles * rank :, :] = both
        for c in copies:
            c.wait()

    return call(
        kernel,
        [shaped((tiles * rank + spare, lanes), bf)] * groups,
        (gst, trp, up, slot_row, score_row),
        [SMEM, SMEM, ANY, VMEM, VMEM],
        scratch=[pltpu.SemaphoreType.DMA((groups, tiles))],
    )


def up_block(block, rank):
    tiles = block.shape[0] // rank
    return jnp.concatenate([block[j * rank : (j + 1) * rank, :] for j in range(tiles)], axis=1)


def pack_down(gst, trp, down, after):
    groups = gst.shape[0]
    tasks, rank, width = down.shape

    def kernel(ins, outs):
        gst, trp, down = ins
        out, sem = outs
        me = lax.axis_index("dp")
        copies = []
        for g in range(groups):
            row = lax.rem(trp[gst[g, me]], tasks)
            copies.append(pltpu.make_async_copy(down.at[row], out.at[g], sem.at[g]))
            copies[-1].start()
        for c in copies:
            c.wait()

    return call(
        kernel,
        [shaped((groups, rank, width), bf)],
        (gst, trp, down),
        [SMEM, SMEM, ANY],
        scratch=[pltpu.SemaphoreType.DMA((groups,))],
        after=after,
    )[0]


def base_parts(rows, weight, parts, after):
    n, width = rows.shape
    cols = weight.shape[1] // parts
    mine = lax.axis_index("tensor").astype(jnp.int32).reshape(1)

    tiles = 1
    tile = cols // tiles

    def kernel(mine, rows, weight, *rest):
        rest[-1][0] = jnp.dot(rows[...], weight[...], preferred_element_type=f32).astype(bf)

    return pl.pallas_call(
        kernel,
        out_shape=shaped((parts, n, cols), bf),
        grid_spec=pltpu.PrefetchScalarGridSpec(
            num_scalar_prefetch=1,
            grid=(parts, tiles),
            in_specs=[
                pl.BlockSpec((n, width), lambda i, j, m: (0, 0)),
                pl.BlockSpec((width, tile), lambda i, j, m: (0, (m[0] ^ i) * tiles + j)),
            ]
            + [ANY] * len(after),
            out_specs=pl.BlockSpec((1, n, tile), lambda i, j, m: (i, 0, j)),
        ),
        compiler_params=pltpu.CompilerParams(vmem_limit_bytes=big),
        cost_estimate=pl.CostEstimate(
            flops=2 * n * width * weight.shape[1],
            bytes_accessed=2 * (rows.size + weight.size + n * weight.shape[1]),
            transcendentals=0,
        ),
    )(mine, rows, weight, *after)


def inner_up(place, rows, blocks, rank, after):
    n, cols = rows.shape

    def kernel(ins, outs):
        place, rows = ins[:2]
        wide = lax.dot_general(
            jnp.concatenate([up_block(block, rank) for block in ins[2:]], axis=0),
            rows[...],
            (((1,), (1,)), ((), ())),
            preferred_element_type=f32,
        )
        acc = jnp.zeros((rank, n), f32)
        for k in range(len(blocks)):
            acc = jnp.where(place[...] == k, wide[k * rank : (k + 1) * rank], acc)
        outs[0][...] = acc
        outs[1][...] = acc.astype(bf)

    operands = (place, rows, *blocks)
    return call(
        kernel,
        [shaped((rank, n), f32), shaped((rank, n), bf)],
        operands,
        [VMEM] * len(operands),
        flops=2 * n * cols * rank * len(blocks),
        after=after,
    )


def inner_down(slot_rows, rows, blocks, after):
    groups, rank, width = blocks.shape
    n = rows.shape[0]

    def kernel(ins, outs):
        slot, rows, blocks = ins
        wide = lax.dot_general(
            blocks[...].reshape(groups * rank, width),
            rows[...],
            (((1,), (1,)), ((), ())),
            preferred_element_type=f32,
        )
        acc = jnp.zeros((rank, n), f32)
        for s in range(groups):
            acc = jnp.where(slot[...] == s, wide[s * rank : (s + 1) * rank], acc)
        outs[0][...] = acc
        outs[1][...] = acc.astype(bf)

    return call(
        kernel,
        [shaped((rank, n), f32), shaped((rank, n), bf)],
        (slot_rows, rows, blocks),
        [VMEM] * 3,
        flops=2 * n * width * rank * groups,
        after=after,
    )


def plus(x, got):
    def kernel(ins, outs):
        total = ins[0][...] + ins[1][...].astype(f32)
        outs[0][...] = total
        outs[1][...] = total.astype(bf)

    return call(kernel, [shaped(x.shape, f32), shaped(x.shape, bf)], (x, got), [VMEM] * 2)


def sum_first(x, wire, axis):
    k = 1
    while 2 * k < lax.axis_size(axis):
        x, wire = plus(x, swap(wire, k, axis))
        k *= 2
    return x, swap(wire, k, axis)


def spread(place, inner_t, k):
    return jnp.where(place == k, inner_t, jnp.zeros((), inner_t.dtype))


def down_grads(gst, place, slot_rows, score_rows, t, t_got, rows, up_blocks, early):
    groups = len(up_blocks)
    rank, n = t.shape
    width = rows.shape[1]

    def kernel(ins, outs):
        gst, place, slot, score, t, t_got, rows = ins[:7]
        me = lax.axis_index("dp")
        mine = gst[pl.ds(me, 1), :]
        sums = jnp.zeros((1, groups), f32)
        counts = jnp.zeros((1, groups), f32)
        for k, block in enumerate(ins[7:]):
            same = gst[pl.ds(me ^ k, 1), :] == mine
            x = block[block.shape[0] - spare :, :].astype(f32)
            sums += jnp.where(same, x[0:1, :groups], 0.0)
            counts += jnp.where(same, x[1:2, :groups], 0.0)
        mean = sums / jnp.maximum(counts, 1.0)
        here = lax.broadcasted_iota(jnp.int32, (groups, groups), 0) == lax.broadcasted_iota(
            jnp.int32, (groups, groups), 1
        )
        mean = jnp.sum(jnp.where(here, mean, 0.0), axis=1, keepdims=True)
        hot = slot[...] == lax.broadcasted_iota(jnp.int32, (groups, n), 0)
        adv = score[...].astype(f32) - jnp.sum(jnp.where(hot, mean, 0.0), axis=0, keepdims=True)
        total = (adv * (t[...] + t_got[...].astype(f32))).astype(bf)
        outs[0][...] = adv
        wide = jnp.concatenate([spread(place[...], total, k) for k in range(groups)], axis=0)
        part = jnp.dot(wide, rows[:, :early], preferred_element_type=f32)
        part = (scale * part).astype(bf)
        for k in range(groups):
            outs[2 + k][...] = part[k * rank : (k + 1) * rank]
        wide = jnp.concatenate([spread(slot[...], total, s) for s in range(groups)], axis=0)
        part = jnp.dot(wide, rows[:, early:], preferred_element_type=f32)
        outs[1][...] = (scale * part).astype(bf).reshape(groups, rank, width - early)

    operands = (gst, place, slot_rows, score_rows, t, t_got, rows, *up_blocks)
    out = call(
        kernel,
        [shaped((1, n), f32), shaped((groups, rank, width - early), bf)]
        + [shaped((rank, early), bf)] * groups,
        operands,
        [VMEM] * len(operands),
        flops=2 * n * width * rank * groups,
    )
    return out[0], out[1], out[2:]


def up_grads(place, adv, t, t_got, cot, groups):
    rank, n = t.shape
    cols = cot.shape[1]

    def kernel(ins, outs):
        place, adv, t, t_got, cot = ins
        total = t[...] + t_got[...].astype(f32)
        outs[0][...] = total.astype(bf)
        total = (adv[...] * total).astype(bf)
        wide = jnp.concatenate([spread(place[...], total, k) for k in range(groups)], axis=0)
        part = (scale * jnp.dot(wide, cot[...], preferred_element_type=f32)).astype(bf)
        for k in range(groups):
            outs[1 + k][...] = part[k * rank : (k + 1) * rank]

    out = call(
        kernel,
        [shaped((rank, n), bf)] + [shaped((rank, cols), bf)] * groups,
        (place, adv, t, t_got, cot),
        [VMEM] * 5,
        flops=2 * n * cols * rank * groups,
    )
    return out[0], out[1:]


def adapted(place, inner_t, base_mine, base_got, blocks, after):
    n, cols = base_got.shape
    rank = inner_t.shape[0]

    def kernel(ins, outs):
        place, t, base_mine, base_got = ins[:4]
        blocks = ins[4:]
        wide = jnp.concatenate([spread(place[...], t[...], k) for k in range(len(blocks))], axis=0)
        ups = jnp.concatenate([up_block(b, rank) for b in blocks], axis=0)
        delta = lax.dot_general(wide, ups, (((0,), (0,)), ((), ())), preferred_element_type=f32)
        delta = (scale * delta).astype(bf).astype(f32)
        outs[0][...] = (base_mine[...].astype(f32) + base_got[...].astype(f32) + delta).astype(bf)

    operands = (place, inner_t, base_mine, base_got, *blocks)
    return call(
        kernel,
        [shaped((n, cols), bf)],
        operands,
        [VMEM] * len(operands),
        flops=2 * n * cols * rank * len(blocks),
        after=after,
    )[0]


def zeros(shape, after):
    def kernel(refs):
        refs[-1][...] = jnp.zeros(refs[-1].shape, bf)

    chunk = 4 if shape[0] % 4 == 0 else 1
    return pl.pallas_call(
        lambda *refs: kernel(refs),
        out_shape=shaped(shape, bf),
        grid=(shape[0] // chunk,),
        in_specs=[ANY] * len(after),
        out_specs=pl.BlockSpec((chunk,) + shape[1:], lambda t: (t, 0, 0)),
        compiler_params=pltpu.CompilerParams(vmem_limit_bytes=big),
        cost_estimate=pl.CostEstimate(flops=0, bytes_accessed=0, transcendentals=0),
    )(*after)


def combine(gst, trp, blocks, rest, filled, after):
    groups = gst.shape[0]
    tasks, rank, width = filled.shape
    count = len(blocks) + len(rest)
    early = blocks[0].shape[1]

    def kernel(*refs):
        gst, trp = refs[:2]
        ins = refs[2 : 2 + count]
        out, held, acc, sem_in, sem_out = refs[-5:]
        me = lax.axis_index("dp")
        copies = []
        for k in range(groups):
            parts = [pltpu.make_async_copy(ins[k], held.at[k, :, pl.ds(0, early)], sem_in.at[0, k])]
            if rest:
                place = held.at[k, :, pl.ds(early, width - early)]
                parts.append(pltpu.make_async_copy(ins[groups].at[me ^ k], place, sem_in.at[1, k]))
            for c in parts:
                c.start()
            copies.append(parts)
        rows = [stored_row(gst, trp, tasks, k) for k in range(groups)]
        back = [
            pltpu.make_async_copy(held.at[g], out.at[rows[g]], sem_out.at[g])
            for g in range(groups)
        ]
        last = []
        for g in range(groups):
            ends, again = jnp.bool_(True), jnp.bool_(False)
            for h in range(groups):
                if h > g:
                    ends = jnp.logical_and(ends, rows[h] != rows[g])
                if h < g:
                    again = jnp.logical_or(again, rows[h] == rows[g])
            last.append(ends)
            for c in copies[g]:
                c.wait()

            @pl.when(jnp.logical_and(ends, again))
            def _():
                acc[...] = held[g].astype(f32)
                for h in range(g):

                    @pl.when(rows[h] == rows[g])
                    def _():
                        acc[...] += held[h].astype(f32)

                held[g] = acc[...].astype(bf)

            @pl.when(ends)
            def _():
                back[g].start()

        for g in range(groups):

            @pl.when(last[g])
            def _():
                back[g].wait()

    return pl.pallas_call(
        kernel,
        out_shape=shaped(filled.shape, bf),
        in_specs=[SMEM, SMEM] + [ANY] * (count + 1 + len(after)),
        out_specs=ANY,
        scratch_shapes=[
            pltpu.VMEM((groups, rank, width), bf),
            pltpu.VMEM((rank, width), f32),
            pltpu.SemaphoreType.DMA((2, groups)),
            pltpu.SemaphoreType.DMA((groups,)),
        ],
        input_output_aliases={2 + count: 0},
        compiler_params=pltpu.CompilerParams(vmem_limit_bytes=big),
        cost_estimate=pl.CostEstimate(flops=0, bytes_accessed=0, transcendentals=0),
    )(gst, trp, *blocks, *rest, filled, *after)


def exchange(x):
    return lax.all_to_all(x, "dp", split_axis=0, concat_axis=0, tiled=True)


def partners(blocks):
    got = {k: swap(blocks[k], k, "dp") for k in reversed(range(1, len(blocks)))}
    return [blocks[0]] + [got[k] for k in range(1, len(blocks))]


def body(hidden, weight, down, up, slot, gst, trp, scores, cotangent):
    groups, parts = lax.axis_size("dp"), lax.axis_size("tensor")
    me = lax.axis_index("dp")
    att, steps, width = hidden.shape
    cols = cotangent.shape[2]
    n = att * steps
    tasks, rank = down.shape[0], down.shape[2]
    down = jnp.swapaxes(down, 1, 2)

    slot_row = slot.reshape(1, att)
    score_row = scores.reshape(1, att)
    up_out = pack_up(gst, trp, up, slot_row, score_row)
    up_got = partners(up_out)
    down_out = pack_down(gst, trp, down, (up_out[0],))
    down_got = exchange(lax.optimization_barrier((down_out, *up_got))[0])

    hidden, cotangent, slot_row, score_row, _ = lax.optimization_barrier(
        (hidden, cotangent, slot_row, score_row, up_out[0])
    )
    slot_rows = jnp.repeat(slot_row, steps, axis=1)
    score_rows = jnp.repeat(score_row, steps, axis=1)
    place = slot_rows ^ me
    cot = cotangent.reshape(n, cols)
    rows = hidden.reshape(n, width)

    back, back_wire = inner_up(place, cot, up_got, rank, ())
    back, back_got = sum_first(back, back_wire, "tensor")
    early = max(lanes, width // 4)
    adv, down_grad, early_grad = down_grads(
        gst, place, slot_rows, score_rows, back, back_got, rows, up_got, early
    )
    early_got = partners(early_grad)

    base = base_parts(rows, weight, parts, (adv,))
    held = [base[i] for i in range(parts)]
    k = 1
    while 2 * k < parts:
        got = swap(jnp.stack(held[1::2]), k, "tensor")
        held = [
            (a.astype(f32) + got[i].astype(f32)).astype(bf) for i, a in enumerate(held[0::2])
        ]
        k *= 2
    zero_down = zeros((tasks, rank, width), (adv,))
    zero_up = zeros((tasks, rank, cols), (adv,))
    down_grad, base_mine, base_far, zero_down, zero_up = lax.optimization_barrier(
        (down_grad, held[0], held[1], zero_down, zero_up, *early_got)
    )[:5]
    base_got = swap(base_far, k, "tensor")
    down_grad_got = exchange(down_grad)

    ahead, ahead_wire = inner_down(slot_rows, rows, down_got, (base,))
    ahead, ahead_got = sum_first(ahead, ahead_wire, "tensor")
    inner_all, up_grad = up_grads(place, adv, ahead, ahead_got, cot, groups)
    up_grad_got = partners(up_grad)
    kv_new = adapted(place, inner_all, base_mine, base_got, up_got, (up_grad[0],))
    kv_out = kv_new.reshape(att, steps, cols)

    grad_down = combine(gst, trp, early_got, [down_grad_got], zero_down, (kv_new,))
    grad_up = combine(gst, trp, up_grad_got, [], zero_up, (grad_down,))
    return (kv_out, jnp.swapaxes(grad_down, 1, 2), grad_up)


def solution(mesh):
    in_specs = (
        P("dp", None, "tensor"),
        P("tensor", None),
        P("dp", "tensor", None),
        P("dp", None, "tensor"),
        P("dp", None),
        P(),
        P(),
        P("dp"),
        P("dp", None, "tensor"),
    )
    out_specs = (P("dp", None, "tensor"), P("dp", "tensor", None), P("dp", None, "tensor"))
    return jax.shard_map(body, mesh=mesh, in_specs=in_specs, out_specs=out_specs, check_vma=False)
```

time: 149 us -> 142 us (0.953)
  waiting for transfers between devices: 47.1 us -> 28.7 us
  starting transfers between devices: 41.3 us -> 52.6 us
    all_to_all x2, waiting for transfers between devices: 27.2 us -> 6.45 us  [exchange(): return lax.all_to_all(x, 'dp', split_axis=0, concat_axis=0, tiled=True)]
    ppermute x20 -> x27, starting transfers between devices: 31.1 us -> 43.4 us  [swap(): return lax.ppermute(x, axis, [(i, i ^ k) for i in range(n)])]
    pallas_call x7 -> x9, Pallas kernels: 29.4 us -> 25.7 us  [call(): pl.pallas_call(run, out_shape=list(outs), in_specs=list(specs) + [ANY] *...]
    unnamed x50 -> x6, local copies, waits for them, and re-layouts: 3.25 us -> 0.02 us
    ppermute x20 -> x27, waiting for transfers between devices: 19.8 us -> 22.3 us  [swap(): return lax.ppermute(x, axis, [(i, i ^ k) for i in range(n)])]
    pallas_call x2 -> x4, Pallas kernels: 7.64 us -> 10 us  [the longest x2 6.08 us: combine(): pl.pallas_call(kernel, out_shape=shaped(filled.shape, bf), in_specs=[SMEM...]
    reshape x1, local copies, waits for them, and re-layouts: 2.18 us -> 4.12 us  [body(): rows = hidden.reshape(n, width)]
    add x2 -> x0, other arithmetic: 1.85 us -> none  [sum_first(): x = x + swap(x, k, axis)]
  transfers between devices with their start and end apart: 22 -> 29, of which waited for: 9 -> 9; matrix products, arithmetic and copies ran while one was open for 7% -> 10% of each run, Pallas kernels for 27% -> 28%
where the time goes in v3:
time: 142 us; the launch traced here: 141 us
  starting transfers between devices  52.6 us (37%)
  Pallas kernels  44.6 us (31%)
  waiting for transfers between devices  28.7 us (20%)
  local copies, waits for them, and re-layouts  10.2 us (7%)
  other arithmetic  4.49 us (3%)
    ppermute x27, starting transfers between devices, swap(): return lax.ppermute(x, axis, [(i, i ^ k) for i in range(n)])  43.4 us
    pallas_call x9, Pallas kernels, call(): pl.pallas_call(run, out_shape=list(outs), in_specs=list(specs) + [ANY] *...  25.7 us
    ppermute x27, waiting for transfers between devices, swap(): return lax.ppermute(x, axis, [(i, i ^ k) for i in range(n)])  22.3 us
    all_to_all x2, starting transfers between devices, exchange(): return lax.all_to_all(x, 'dp', split_axis=0, concat_axis=0, tiled=True)  9.2 us
    pallas_call x1, Pallas kernels, base_parts(): pl.pallas_call(kernel, out_shape=shaped((parts, n, cols), bf), grid_spec=...  8.81 us
    all_to_all x2, waiting for transfers between devices, exchange(): return lax.all_to_all(x, 'dp', split_axis=0, concat_axis=0, tiled=True)  6.45 us
    pallas_call x2, Pallas kernels, combine(): pl.pallas_call(kernel, out_shape=shaped(filled.shape, bf), in_specs=[SMEM...  6.08 us
    reshape x1, local copies, waits for them, and re-layouts, body(): rows = hidden.reshape(n, width)  4.12 us
  transfers between devices with their start and end apart: 29, of which 9 were waited for; matrix products, arithmetic and copies ran while one was open for 10% of the time, Pallas kernels for 28%

profile of v3, /device:TPU:0, one launch (start us, length us, event | category | flops | bytes accessed | tf_op | source)
XLA Modules:
  0.0 141.3 jit_solution(14050529566532350489)
XLA Ops:
  0.6 2.8 %shard_map.112 = (bf16[272,128]{1,0:T(8,128)(2,1)}, bf16[272,128]{1,0:T(8,128)(2,1)}, bf16[272,128]{1,0:T(8,128)(2,1)}, bf16[272,128]{1,0:T(8,128)(2,1)}, bf16[2...) custom-call(s32[8,8]{1,0:T(8,128)} %refs_0_.9, ...), custom_call_target="tpu_custom_call" | custom-call | tf_op jit(solution)/shard_map/pallas_call | solution.py:33
  3.5 3.0 %collective-permute-start = (bf16[272,128]{1,0:T(8,128)(2,1)}, bf16[272,128]{1,0:T(8,128)(2,1)}, u32[]{:S(2)}, u32[]{:S(2)}) collective-permute-start(bf16[272,128]{1,0:T(8,128)(2,1)} %get-tuple-element.52), channel_id=1, source_target_pairs={{0,4},{4,0},{8,12},{12,8},{16,20},{20,16},{24,28},{28,24},{1,5},{5... | collective-permute-start | bytes 208904 | tf_op jit(solution)/shard_map/ppermute | solution.py:46
  8.1 3.0 %collective-permute-start.3 = (bf16[272,128]{1,0:T(8,128)(2,1)}, bf16[272,128]{1,0:T(8,128)(2,1)}, u32[]{:S(2)}, u32[]{:S(2)}) collective-permute-start(bf16[272,128]{1,0:T(8,128)(2,1)} %get-tuple-element.55), channel_id=1, source_target_pairs={{0,16},{4,20},{8,24},{12,28},{16,0},{20,4},{24,8},{28,12},{1,17},{... | collective-permute-start | bytes 208904 | tf_op jit(solution)/shard_map/ppermute | solution.py:46
  12.3 3.6 %collective-permute-start.5 = (bf16[272,128]{1,0:T(8,128)(2,1)}, bf16[272,128]{1,0:T(8,128)(2,1)}, u32[]{:S(2)}, u32[]{:S(2)}) collective-permute-start(bf16[272,128]{1,0:T(8,128)(2,1)} %get-tuple-element.57), channel_id=1, source_target_pairs={{0,24},{4,28},{8,16},{12,20},{16,8},{20,12},{24,0},{28,4},{1,25},{... | collective-permute-start | bytes 208904 | tf_op jit(solution)/shard_map/ppermute | solution.py:46
  16.0 3.7 %shard_map.116 = bf16[8,64,2048]{2,1,0:T(8,128)(2,1)} custom-call(s32[8,8]{1,0:T(8,128)} %refs_0_.9, s32[128]{0:T(128)} %refs_1_.7, bf16[16,64,2048]{2,1,0:T(8,128)(2,1)} %bitcast.12, bf16[272,128]{1,0:T(8,128)(2,1)} %get-tuple-element.48.refs_2_.refs_7_.refs_3_.refs_4_), custom_call_target="tpu_custom_call" | custom-call | tf_op jit(solution)/shard_map/pallas_call | solution.py:33
  19.7 2.4 %collective-permute-done.4.refs_7_.refs_12_.refs_9_ = bf16[272,128]{1,0:T(8,128)(2,1)} collective-permute-done((bf16[272,128]{1,0:T(8,128)(2,1)}, bf16[272,128]{1,0:T(8,128)(2,1)}, u32[]{:S(2)}, u32[]{:S(2)}) %collective-permute-start.4) | collective-permute-done | bytes 69664 | tf_op jit(solution)/shard_map/ppermute | solution.py:46
  23.4 4.7 %all-to-all-start = ((bf16[8,64,2048]{2,1,0:T(8,128)(2,1)}), bf16[8,64,2048]{2,1,0:T(8,128)(2,1)}, u32[]{:S(2)}, u32[]{:S(2)}) async-start(bf16[8,64,2048]{2,1,0:T(8,128)(2,1)} %shard_map.116), calls=%async_computation | async-start | bytes 4194304 | tf_op jit(solution)/shard_map/all_to_all | solution.py:425
  29.9 2.3 %shard_map.113 = (f32[64,512]{1,0:T(8,128)}, bf16[64,512]{1,0:T(8,128)(2,1)}) custom-call(s32[1,512]{1,0:T(1,128)} %broadcast_xor_fusion.refs_0_.refs_1_, bf16[512,512]{1,0:T(8,128)(2,1)} %reshape.59.refs_1_.refs_4_, bf16[272,128]{1,0:T(8,128)(2,1)} %get-tuple-element.48.refs_2_.refs_7_.refs_3_.refs_4_, ...), custom_call_target="tpu_custom_call" | custom-call | tf_op jit(solution)/shard_map/pallas_call | solution.py:33
  38.5 4.1 %reshape.60.refs_6_.rows.refs_1_ = bf16[512,2048]{1,0:T(8,128)(2,1)} reshape(bf16[256,2,2048]{2,1,0:T(2,128)(2,1)} %param.9) | data formatting | bytes 4194304 | tf_op jit(solution)/shard_map/reshape | solution.py:456
  42.6 4.5 %shard_map.115 = (f32[1,512]{1,0:T(1,128)}, bf16[8,64,1536]{2,1,0:T(8,128)(2,1)}, bf16[64,512]{1,0:T(8,128)(2,1)}, bf16[64,512]{1,0:T(8,128)(2,1)}, bf16[64,512]...) custom-call(s32[8,8]{1,0:T(8,128)} %refs_0_.9, ...), custom_call_target="tpu_custom_call" | custom-call | tf_op jit(solution)/shard_map/pallas_call | solution.py:33
  47.1 8.8 %shard_map.117.refs_3_ = bf16[4,512,512]{2,1,0:T(8,128)(2,1)} custom-call(s32[1]{0:T(128)} %bitcast.5.mine, bf16[512,2048]{1,0:T(8,128)(2,1)} %reshape.60.refs_6_.rows.refs_1_, bf16[2048,2048]{1,0:T(8,128)(2,1)} %weight.1, f32[1,512]{1,0:T(1,128)} %get-tuple-element.64.rest_0_.refs_1_.refs_0_), custom_call_target="tpu_custom_call" | custom-call | flops 4294967296 | bytes 12582912 | tf_op jit(solution)/shard_map/pallas_call | solution.py:140
  58.2 2.0 %collective-permute-start.12 = (bf16[64,512]{1,0:T(8,128)(2,1)}, bf16[64,512]{1,0:T(8,128)(2,1)}, u32[]{:S(2)}, u32[]{:S(2)}) collective-permute-start(bf16[64,512]{1,0:T(8,128)(2,1)} %get-tuple-element.73), channel_id=1, source_target_pairs={{0,4},{4,0},{8,12},{12,8},{16,20},{20,16},{24,28},{28,24},{1,5},{5... | collective-permute-start | bytes 196616 | tf_op jit(solution)/shard_map/ppermute | solution.py:46
  61.7 2.4 %shard_map.121.refs_11_ = bf16[16,64,2048]{2,1,0:T(8,128)(2,1)} custom-call(f32[1,512]{1,0:T(1,128)} %get-tuple-element.64.rest_0_.refs_1_.refs_0_), custom_call_target="tpu_custom_call" | custom-call | tf_op jit(solution)/shard_map/pallas_call | solution.py:338
  65.7 3.0 %collective-permute-start.15 = (bf16[64,512]{1,0:T(8,128)(2,1)}, bf16[64,512]{1,0:T(8,128)(2,1)}, u32[]{:S(2)}, u32[]{:S(2)}) collective-permute-start(bf16[64,512]{1,0:T(8,128)(2,1)} %get-tuple-element.76), channel_id=1, source_target_pairs={{0,16},{4,20},{8,24},{12,28},{16,0},{20,4},{24,8},{28,12},{1,17},{... | collective-permute-start | bytes 196616 | tf_op jit(solution)/shard_map/ppermute | solution.py:46
  70.1 4.3 %collective-permute-start.17 = (bf16[64,512]{1,0:T(8,128)(2,1)}, bf16[64,512]{1,0:T(8,128)(2,1)}, u32[]{:S(2)}, u32[]{:S(2)}) collective-permute-start(bf16[64,512]{1,0:T(8,128)(2,1)} %get-tuple-element.78), channel_id=1, source_target_pairs={{0,24},{4,28},{8,16},{12,20},{16,8},{20,12},{24,0},{28,4},{1,25},{... | collective-permute-start | bytes 196616 | tf_op jit(solution)/shard_map/ppermute | solution.py:46
  74.4 2.8 %fusion.1 = (bf16[512,512]{1,0:T(8,128)(2,1)}, bf16[512,512]{1,0:T(8,128)(2,1)}) fusion(bf16[2,512,512]{2,1,0:T(8,128)(2,1)} %collective-permute-done.11, bf16[4,512,512]{2,1,0:T(8,128)(2,1)} %shard_map.117.refs_3_), kind=kLoop, calls=%fused_computation.4 | loop fusion | flops 2097152 | bytes 3145728 | tf_op jit(solution)/shard_map/convert_element_type | solution.py:472
  77.2 8.0 %collective-permute-done.15.refs_6_ = bf16[64,512]{1,0:T(8,128)(2,1)} collective-permute-done((bf16[64,512]{1,0:T(8,128)(2,1)}, bf16[64,512]{1,0:T(8,128)(2,1)}, u32[]{:S(2)}, u32[]{:S(2)}) %collective-permute-start.15) | collective-permute-done | bytes 65568 | tf_op jit(solution)/shard_map/ppermute | solution.py:46
  86.5 4.5 %all-to-all-start.1 = ((bf16[8,64,1536]{2,1,0:T(8,128)(2,1)}), bf16[8,64,1536]{2,1,0:T(8,128)(2,1)}, u32[]{:S(2)}, u32[]{:S(2)}) async-start(bf16[8,64,1536]{2,1,0:T(8,128)(2,1)} %get-tuple-element.83), calls=%async_computation.1 | async-start | bytes 3145728 | tf_op jit(solution)/shard_map/all_to_all | solution.py:425
  91.1 2.0 %collective-permute-start.19 = (bf16[512,512]{1,0:T(8,128)(2,1)}, bf16[512,512]{1,0:T(8,128)(2,1)}, u32[]{:S(2)}, u32[]{:S(2)}) collective-permute-start(bf16[512,512]{1,0:T(8,128)(2,1)} %get-tuple-element.81), channel_id=1, source_target_pairs={{0,2},{1,3},{2,0},{3,1},{4,6},{5,7},{6,4},{7,5},{8,10},{9,11},{10,... | collective-permute-start | bytes 1572872 | tf_op jit(solution)/shard_map/ppermute | solution.py:46
  93.1 4.2 %shard_map.118 = (f32[64,512]{1,0:T(8,128)}, bf16[64,512]{1,0:T(8,128)(2,1)}) custom-call(s32[1,512]{1,0:T(1,128)} %copy-done.1, bf16[512,2048]{1,0:T(8,128)(2,1)} %reshape.60.refs_6_.rows.refs_1_, bf16[8,64,2048]{2,1,0:T(8,128)(2,1)} %all-to-all-done.refs_2_, bf16[4,512,512]{2,1,0:T(8,128)(2,1)} %shard_map.117.refs_3_), custom_call_target="tpu_custom_call" | custom-call | tf_op jit(solution)/shard_map/pallas_call | solution.py:33
  98.9 1.6 %shard_map.119 = (f32[64,512]{1,0:T(8,128)}, bf16[64,512]{1,0:T(8,128)(2,1)}) custom-call(f32[64,512]{1,0:T(8,128)} %get-tuple-element.66.refs_0_, bf16[64,512]{1,0:T(8,128)(2,1)} %collective-permute-done.9.refs_1_), custom_call_target="tpu_custom_call" | custom-call | tf_op jit(solution)/shard_map/pallas_call | solution.py:33
  100.5 5.8 %collective-permute-done.10.refs_3_ = bf16[64,512]{1,0:T(8,128)(2,1)} collective-permute-done((bf16[64,512]{1,0:T(8,128)(2,1)}, bf16[64,512]{1,0:T(8,128)(2,1)}, u32[]{:S(2)}, u32[]{:S(2)}) %collective-permute-start.10) | collective-permute-done | bytes 65568 | tf_op jit(solution)/shard_map/ppermute | solution.py:46
  106.3 2.3 %shard_map.120 = (bf16[64,512]{1,0:T(8,128)(2,1)}, bf16[64,512]{1,0:T(8,128)(2,1)}, bf16[64,512]{1,0:T(8,128)(2,1)}, bf16[64,512]{1,0:T(8,128)(2,1)}, bf16[64,51...) custom-call(s32[1,512]{1,0:T(1,128)} %broadcast_xor_fusion.refs_0_.r, ...), custom_call_target="tpu_custom_call" | custom-call | tf_op jit(solution)/shard_map/pallas_call | solution.py:33
  108.6 1.7 %collective-permute-start.20 = (bf16[64,512]{1,0:T(8,128)(2,1)}, bf16[64,512]{1,0:T(8,128)(2,1)}, u32[]{:S(2)}, u32[]{:S(2)}) collective-permute-start(bf16[64,512]{1,0:T(8,128)(2,1)} %get-tuple-element.85), channel_id=1, source_target_pairs={{0,4},{4,0},{8,12},{12,8},{16,20},{20,16},{24,28},{28,24},{1,5},{5... | collective-permute-start | bytes 196616 | tf_op jit(solution)/shard_map/ppermute | solution.py:46
  112.1 2.6 %collective-permute-start.23 = (bf16[64,512]{1,0:T(8,128)(2,1)}, bf16[64,512]{1,0:T(8,128)(2,1)}, u32[]{:S(2)}, u32[]{:S(2)}) collective-permute-start(bf16[64,512]{1,0:T(8,128)(2,1)} %get-tuple-element.88), channel_id=1, source_target_pairs={{0,16},{4,20},{8,24},{12,28},{16,0},{20,4},{24,8},{28,12},{1,17},{... | collective-permute-start | bytes 196616 | tf_op jit(solution)/shard_map/ppermute | solution.py:46
  116.2 3.7 %collective-permute-start.25 = (bf16[64,512]{1,0:T(8,128)(2,1)}, bf16[64,512]{1,0:T(8,128)(2,1)}, u32[]{:S(2)}, u32[]{:S(2)}) collective-permute-start(bf16[64,512]{1,0:T(8,128)(2,1)} %get-tuple-element.90), channel_id=1, source_target_pairs={{0,24},{4,28},{8,16},{12,20},{16,8},{20,12},{24,0},{28,4},{1,25},{... | collective-permute-start | bytes 196616 | tf_op jit(solution)/shard_map/ppermute | solution.py:46
  120.1 3.9 %collective-permute-start.26 = (bf16[64,512]{1,0:T(8,128)(2,1)}, bf16[64,512]{1,0:T(8,128)(2,1)}, u32[]{:S(2)}, u32[]{:S(2)}) collective-permute-start(bf16[64,512]{1,0:T(8,128)(2,1)} %get-tuple-element.91), channel_id=1, source_target_pairs={{0,28},{4,24},{8,20},{12,16},{16,12},{20,8},{24,4},{28,0},{1,29},{... | collective-permute-start | bytes 196616 | tf_op jit(solution)/shard_map/ppermute | solution.py:46
  124.0 2.7 %shard_map.123.refs_12_ = bf16[512,512]{1,0:T(8,128)(2,1)} custom-call(s32[1,512]{1,0:T(1,128)} %broadcast_xor_fusion.refs_0_.refs_1_, bf16[64,512]{1,0:T(8,128)(2,1)} %get-tuple-element.70.refs_1_, bf16[512,512]{1,0:T(8,128)(2,1)} %get-tuple-element.80.refs_2_, bf16[512,512]{1,0:T(8,128)(2,1)} %collective-permute-done.19.refs_3_, ...), custom_call_target="tpu_custom_call" | custom-call | tf_op jit(solution)/shard_map/pallas_call | solution.py:33
  126.7 2.0 %reshape.62 = bf16[256,2,512]{2,1,0:T(2,128)(2,1)} reshape(bf16[512,512]{1,0:T(8,128)(2,1)} %shard_map.123.refs_12_) | data formatting | bytes 1048576 | tf_op jit(solution)/shard_map/reshape | solution.py:488
  128.8 6.4 %all-to-all-done.1.refs_10_ = bf16[8,64,1536]{2,1,0:T(8,128)(2,1)} async-done(((bf16[8,64,1536]{2,1,0:T(8,128)(2,1)}), bf16[8,64,1536]{2,1,0:T(8,128)(2,1)}, u32[]{:S(2)}, u32[]{:S(2)}) %all-to-all-start.1) | async-done | bytes 1572896 | tf_op jit(solution)/shard_map/all_to_all | solution.py:425
  135.2 3.4 %shard_map.124.refs_11_ = bf16[16,64,2048]{2,1,0:T(8,128)(2,1)} custom-call(s32[8,8]{1,0:T(8,128)} %refs_0_.9, s32[128]{0:T(128)} %refs_1_.7, bf16[64,512]{1,0:T(8,128)(2,1)} %get-tuple-element.72.refs_2_, bf16[64,512]{1,0:T(8,128)(2,1)} %collective-permute-done.12.refs_3_, ...), custom_call_target="tpu_custom_call", output_to_operand_aliasing={{}: (11, {})} | custom-call | tf_op jit(solution)/shard_map/pallas_call | solution.py:407
  138.7 2.7 %shard_map.125 = bf16[16,64,512]{2,1,0:T(8,128)(2,1)} custom-call(s32[8,8]{1,0:T(8,128)} %refs_0_.9, s32[128]{0:T(128)} %refs_1_.7, bf16[64,512]{1,0:T(8,128)(2,1)} %get-tuple-element.82.refs_12_.refs_2_, bf16[64,512]{1,0:T(8,128)(2,1)} %collective-permute-done.20.refs_3_, ...), custom_call_target="tpu_custom_call", output_to_operand_aliasing={{}: (10, {})} | custom-call | tf_op jit(solution)/shard_map/pallas_call | solution.py:407
  (57 shorter events, 25.3 us)
Async XLA Ops:
  3.5 8.9 %collective-permute-start = (bf16[272,128]{1,0:T(8,128)(2,1)}, bf16[272,128]{1,0:T(8,128)(2,1)}, u32[]{:S(2)}, u32[]{:S(2)}) collective-permute-start(bf16[272,128]{1,0:T(8,128)(2,1)} %get-tuple-element.52), channel_id=1, source_target_pairs={{0,4},{4,0},{8,12},{12,8},{16,20},{20,16},{24,28},{28,24},{1,5},{5... | collective-permute-start | bytes 208904 | tf_op jit(solution)/shard_map/ppermute | solution.py:46
  6.5 9.5 %collective-permute-start.1 = (bf16[272,128]{1,0:T(8,128)(2,1)}, bf16[272,128]{1,0:T(8,128)(2,1)}, u32[]{:S(2)}, u32[]{:S(2)}) collective-permute-start(bf16[272,128]{1,0:T(8,128)(2,1)} %get-tuple-element.53), channel_id=1, source_target_pairs={{0,8},{4,12},{8,0},{12,4},{16,24},{20,28},{24,16},{28,20},{1,9},{5... | collective-permute-start | bytes 208904 | tf_op jit(solution)/shard_map/ppermute | solution.py:46
  8.1 11.6 %collective-permute-start.2 = (bf16[272,128]{1,0:T(8,128)(2,1)}, bf16[272,128]{1,0:T(8,128)(2,1)}, u32[]{:S(2)}, u32[]{:S(2)}) collective-permute-start(bf16[272,128]{1,0:T(8,128)(2,1)} %get-tuple-element.54), channel_id=1, source_target_pairs={{0,12},{4,8},{8,4},{12,0},{16,28},{20,24},{24,20},{28,16},{1,13},{... | collective-permute-start | bytes 208904 | tf_op jit(solution)/shard_map/ppermute | solution.py:46
  8.1 11.6 %collective-permute-start.3 = (bf16[272,128]{1,0:T(8,128)(2,1)}, bf16[272,128]{1,0:T(8,128)(2,1)}, u32[]{:S(2)}, u32[]{:S(2)}) collective-permute-start(bf16[272,128]{1,0:T(8,128)(2,1)} %get-tuple-element.55), channel_id=1, source_target_pairs={{0,16},{4,20},{8,24},{12,28},{16,0},{20,4},{24,8},{28,12},{1,17},{... | collective-permute-start | bytes 208904 | tf_op jit(solution)/shard_map/ppermute | solution.py:46
  11.1 11.0 %collective-permute-start.4 = (bf16[272,128]{1,0:T(8,128)(2,1)}, bf16[272,128]{1,0:T(8,128)(2,1)}, u32[]{:S(2)}, u32[]{:S(2)}) collective-permute-start(bf16[272,128]{1,0:T(8,128)(2,1)} %get-tuple-element.56), channel_id=1, source_target_pairs={{0,20},{4,16},{8,28},{12,24},{16,4},{20,0},{24,12},{28,8},{1,21},{... | collective-permute-start | bytes 208904 | tf_op jit(solution)/shard_map/ppermute | solution.py:46
  12.3 9.8 %collective-permute-start.5 = (bf16[272,128]{1,0:T(8,128)(2,1)}, bf16[272,128]{1,0:T(8,128)(2,1)}, u32[]{:S(2)}, u32[]{:S(2)}) collective-permute-start(bf16[272,128]{1,0:T(8,128)(2,1)} %get-tuple-element.57), channel_id=1, source_target_pairs={{0,24},{4,28},{8,16},{12,20},{16,8},{20,12},{24,0},{28,4},{1,25},{... | collective-permute-start | bytes 208904 | tf_op jit(solution)/shard_map/ppermute | solution.py:46
  15.9 7.4 %collective-permute-start.6 = (bf16[272,128]{1,0:T(8,128)(2,1)}, bf16[272,128]{1,0:T(8,128)(2,1)}, u32[]{:S(2)}, u32[]{:S(2)}) collective-permute-start(bf16[272,128]{1,0:T(8,128)(2,1)} %get-tuple-element.58), channel_id=1, source_target_pairs={{0,28},{4,24},{8,20},{12,16},{16,12},{20,8},{24,4},{28,0},{1,29},{... | collective-permute-start | bytes 208904 | tf_op jit(solution)/shard_map/ppermute | solution.py:46
  19.6 8.4 %copy-start.2 = (s32[256,1]{0,1:T(1,128)S(1)}, s32[256,1]{0,1:T(1,128)}, u32[]{:S(2)}) copy-start(s32[256,1]{0,1:T(1,128)} %param.13) | copy-start | bytes 3076
  19.7 8.6 %copy-start = (bf16[256,2,512]{2,1,0:T(2,128)(2,1)S(1)}, bf16[256,2,512]{2,1,0:T(2,128)(2,1)}, u32[]{:S(2)}) copy-start(bf16[256,2,512]{2,1,0:T(2,128)(2,1)} %param.17) | copy-start | bytes 1572868
  23.4 63.2 %all-to-all-start = ((bf16[8,64,2048]{2,1,0:T(8,128)(2,1)}), bf16[8,64,2048]{2,1,0:T(8,128)(2,1)}, u32[]{:S(2)}, u32[]{:S(2)}) async-start(bf16[8,64,2048]{2,1,0:T(8,128)(2,1)} %shard_map.116), calls=%async_computation | async-start | bytes 4194304 | tf_op jit(solution)/shard_map/all_to_all | solution.py:425
  28.3 1.0 copy-start.1
  32.2 1.6 %collective-permute-start.7 = (bf16[64,512]{1,0:T(8,128)(2,1)}, bf16[64,512]{1,0:T(8,128)(2,1)}, u32[]{:S(2)}, u32[]{:S(2)}) collective-permute-start(bf16[64,512]{1,0:T(8,128)(2,1)} %get-tuple-element.60), channel_id=1, source_target_pairs={{0,1},{1,0},{2,3},{3,2},{4,5},{5,4},{6,7},{7,6},{8,9},{9,8},{10,11... | collective-permute-start | bytes 196616 | tf_op jit(solution)/shard_map/ppermute | solution.py:46
  35.4 7.1 %collective-permute-start.8 = (bf16[64,512]{1,0:T(8,128)(2,1)}, bf16[64,512]{1,0:T(8,128)(2,1)}, u32[]{:S(2)}, u32[]{:S(2)}) collective-permute-start(bf16[64,512]{1,0:T(8,128)(2,1)} %get-tuple-element.62), channel_id=1, source_target_pairs={{0,2},{1,3},{2,0},{3,1},{4,6},{5,7},{6,4},{7,5},{8,10},{9,11},{10,... | collective-permute-start | bytes 196616 | tf_op jit(solution)/shard_map/ppermute | solution.py:46
  58.2 16.1 %collective-permute-start.11 = (bf16[2,512,512]{2,1,0:T(8,128)(2,1)}, bf16[2,512,512]{2,1,0:T(8,128)(2,1)}, u32[]{:S(2)}, u32[]{:S(2)}) collective-permute-start(bf16[2,512,512]{2,1,0:T(8,128)(2,1)} %pad_maximum_fusion), channel_id=1, source_target_pairs={{0,1},{1,0},{2,3},{3,2},{4,5},{5,4},{6,7},{7,6},{8,9},{9,8},{10,11... | collective-permute-start | bytes 3145736 | tf_op jit(solution)/shard_map/ppermute | solution.py:46
  58.2 10.5 %collective-permute-start.12 = (bf16[64,512]{1,0:T(8,128)(2,1)}, bf16[64,512]{1,0:T(8,128)(2,1)}, u32[]{:S(2)}, u32[]{:S(2)}) collective-permute-start(bf16[64,512]{1,0:T(8,128)(2,1)} %get-tuple-element.73), channel_id=1, source_target_pairs={{0,4},{4,0},{8,12},{12,8},{16,20},{20,16},{24,28},{28,24},{1,5},{5... | collective-permute-start | bytes 196616 | tf_op jit(solution)/shard_map/ppermute | solution.py:46
  60.3 9.8 %collective-permute-start.13 = (bf16[64,512]{1,0:T(8,128)(2,1)}, bf16[64,512]{1,0:T(8,128)(2,1)}, u32[]{:S(2)}, u32[]{:S(2)}) collective-permute-start(bf16[64,512]{1,0:T(8,128)(2,1)} %get-tuple-element.74), channel_id=1, source_target_pairs={{0,8},{4,12},{8,0},{12,4},{16,24},{20,28},{24,16},{28,20},{1,9},{5... | collective-permute-start | bytes 196616 | tf_op jit(solution)/shard_map/ppermute | solution.py:46
  65.7 11.5 %collective-permute-start.14 = (bf16[64,512]{1,0:T(8,128)(2,1)}, bf16[64,512]{1,0:T(8,128)(2,1)}, u32[]{:S(2)}, u32[]{:S(2)}) collective-permute-start(bf16[64,512]{1,0:T(8,128)(2,1)} %get-tuple-element.75), channel_id=1, source_target_pairs={{0,12},{4,8},{8,4},{12,0},{16,28},{20,24},{24,20},{28,16},{1,13},{... | collective-permute-start | bytes 196616 | tf_op jit(solution)/shard_map/ppermute | solution.py:46
  65.7 19.5 %collective-permute-start.15 = (bf16[64,512]{1,0:T(8,128)(2,1)}, bf16[64,512]{1,0:T(8,128)(2,1)}, u32[]{:S(2)}, u32[]{:S(2)}) collective-permute-start(bf16[64,512]{1,0:T(8,128)(2,1)} %get-tuple-element.76), channel_id=1, source_target_pairs={{0,16},{4,20},{8,24},{12,28},{16,0},{20,4},{24,8},{28,12},{1,17},{... | collective-permute-start | bytes 196616 | tf_op jit(solution)/shard_map/ppermute | solution.py:46
  68.7 17.8 %collective-permute-start.16 = (bf16[64,512]{1,0:T(8,128)(2,1)}, bf16[64,512]{1,0:T(8,128)(2,1)}, u32[]{:S(2)}, u32[]{:S(2)}) collective-permute-start(bf16[64,512]{1,0:T(8,128)(2,1)} %get-tuple-element.77), channel_id=1, source_target_pairs={{0,20},{4,16},{8,28},{12,24},{16,4},{20,0},{24,12},{28,8},{1,21},{... | collective-permute-start | bytes 196616 | tf_op jit(solution)/shard_map/ppermute | solution.py:46
  70.1 16.5 %collective-permute-start.17 = (bf16[64,512]{1,0:T(8,128)(2,1)}, bf16[64,512]{1,0:T(8,128)(2,1)}, u32[]{:S(2)}, u32[]{:S(2)}) collective-permute-start(bf16[64,512]{1,0:T(8,128)(2,1)} %get-tuple-element.78), channel_id=1, source_target_pairs={{0,24},{4,28},{8,16},{12,20},{16,8},{20,12},{24,0},{28,4},{1,25},{... | collective-permute-start | bytes 196616 | tf_op jit(solution)/shard_map/ppermute | solution.py:46
  74.4 12.2 %collective-permute-start.18 = (bf16[64,512]{1,0:T(8,128)(2,1)}, bf16[64,512]{1,0:T(8,128)(2,1)}, u32[]{:S(2)}, u32[]{:S(2)}) collective-permute-start(bf16[64,512]{1,0:T(8,128)(2,1)} %get-tuple-element.79), channel_id=1, source_target_pairs={{0,28},{4,24},{8,20},{12,16},{16,12},{20,8},{24,4},{28,0},{1,29},{... | collective-permute-start | bytes 196616 | tf_op jit(solution)/shard_map/ppermute | solution.py:46
  86.5 48.7 %all-to-all-start.1 = ((bf16[8,64,1536]{2,1,0:T(8,128)(2,1)}), bf16[8,64,1536]{2,1,0:T(8,128)(2,1)}, u32[]{:S(2)}, u32[]{:S(2)}) async-start(bf16[8,64,1536]{2,1,0:T(8,128)(2,1)} %get-tuple-element.83), calls=%async_computation.1 | async-start | bytes 3145728 | tf_op jit(solution)/shard_map/all_to_all | solution.py:425
  91.1 23.7 %collective-permute-start.19 = (bf16[512,512]{1,0:T(8,128)(2,1)}, bf16[512,512]{1,0:T(8,128)(2,1)}, u32[]{:S(2)}, u32[]{:S(2)}) collective-permute-start(bf16[512,512]{1,0:T(8,128)(2,1)} %get-tuple-element.81), channel_id=1, source_target_pairs={{0,2},{1,3},{2,0},{3,1},{4,6},{5,7},{6,4},{7,5},{8,10},{9,11},{10,... | collective-permute-start | bytes 1572872 | tf_op jit(solution)/shard_map/ppermute | solution.py:46
  97.3 1.6 %collective-permute-start.9 = (bf16[64,512]{1,0:T(8,128)(2,1)}, bf16[64,512]{1,0:T(8,128)(2,1)}, u32[]{:S(2)}, u32[]{:S(2)}) collective-permute-start(bf16[64,512]{1,0:T(8,128)(2,1)} %get-tuple-element.67), channel_id=1, source_target_pairs={{0,1},{1,0},{2,3},{3,2},{4,5},{5,4},{6,7},{7,6},{8,9},{9,8},{10,11... | collective-permute-start | bytes 196616 | tf_op jit(solution)/shard_map/ppermute | solution.py:46
  100.5 5.8 %collective-permute-start.10 = (bf16[64,512]{1,0:T(8,128)(2,1)}, bf16[64,512]{1,0:T(8,128)(2,1)}, u32[]{:S(2)}, u32[]{:S(2)}) collective-permute-start(bf16[64,512]{1,0:T(8,128)(2,1)} %get-tuple-element.69), channel_id=1, source_target_pairs={{0,2},{1,3},{2,0},{3,1},{4,6},{5,7},{6,4},{7,5},{8,10},{9,11},{10,... | collective-permute-start | bytes 196616 | tf_op jit(solution)/shard_map/ppermute | solution.py:46
  108.6 7.6 %collective-permute-start.20 = (bf16[64,512]{1,0:T(8,128)(2,1)}, bf16[64,512]{1,0:T(8,128)(2,1)}, u32[]{:S(2)}, u32[]{:S(2)}) collective-permute-start(bf16[64,512]{1,0:T(8,128)(2,1)} %get-tuple-element.85), channel_id=1, source_target_pairs={{0,4},{4,0},{8,12},{12,8},{16,20},{20,16},{24,28},{28,24},{1,5},{5... | collective-permute-start | bytes 196616 | tf_op jit(solution)/shard_map/ppermute | solution.py:46
  110.3 9.8 %collective-permute-start.21 = (bf16[64,512]{1,0:T(8,128)(2,1)}, bf16[64,512]{1,0:T(8,128)(2,1)}, u32[]{:S(2)}, u32[]{:S(2)}) collective-permute-start(bf16[64,512]{1,0:T(8,128)(2,1)} %get-tuple-element.86), channel_id=1, source_target_pairs={{0,8},{4,12},{8,0},{12,4},{16,24},{20,28},{24,16},{28,20},{1,9},{5... | collective-permute-start | bytes 196616 | tf_op jit(solution)/shard_map/ppermute | solution.py:46
  111.8 26.8 %collective-permute-start.22 = (bf16[64,512]{1,0:T(8,128)(2,1)}, bf16[64,512]{1,0:T(8,128)(2,1)}, u32[]{:S(2)}, u32[]{:S(2)}) collective-permute-start(bf16[64,512]{1,0:T(8,128)(2,1)} %get-tuple-element.87), channel_id=1, source_target_pairs={{0,12},{4,8},{8,4},{12,0},{16,28},{20,24},{24,20},{28,16},{1,13},{... | collective-permute-start | bytes 196616 | tf_op jit(solution)/shard_map/ppermute | solution.py:46
  112.1 26.5 %collective-permute-start.23 = (bf16[64,512]{1,0:T(8,128)(2,1)}, bf16[64,512]{1,0:T(8,128)(2,1)}, u32[]{:S(2)}, u32[]{:S(2)}) collective-permute-start(bf16[64,512]{1,0:T(8,128)(2,1)} %get-tuple-element.88), channel_id=1, source_target_pairs={{0,16},{4,20},{8,24},{12,28},{16,0},{20,4},{24,8},{28,12},{1,17},{... | collective-permute-start | bytes 196616 | tf_op jit(solution)/shard_map/ppermute | solution.py:46
  114.7 23.9 %collective-permute-start.24 = (bf16[64,512]{1,0:T(8,128)(2,1)}, bf16[64,512]{1,0:T(8,128)(2,1)}, u32[]{:S(2)}, u32[]{:S(2)}) collective-permute-start(bf16[64,512]{1,0:T(8,128)(2,1)} %get-tuple-element.89), channel_id=1, source_target_pairs={{0,20},{4,16},{8,28},{12,24},{16,4},{20,0},{24,12},{28,8},{1,21},{... | collective-permute-start | bytes 196616 | tf_op jit(solution)/shard_map/ppermute | solution.py:46
  116.2 22.4 %collective-permute-start.25 = (bf16[64,512]{1,0:T(8,128)(2,1)}, bf16[64,512]{1,0:T(8,128)(2,1)}, u32[]{:S(2)}, u32[]{:S(2)}) collective-permute-start(bf16[64,512]{1,0:T(8,128)(2,1)} %get-tuple-element.90), channel_id=1, source_target_pairs={{0,24},{4,28},{8,16},{12,20},{16,8},{20,12},{24,0},{28,4},{1,25},{... | collective-permute-start | bytes 196616 | tf_op jit(solution)/shard_map/ppermute | solution.py:46
  120.1 18.5 %collective-permute-start.26 = (bf16[64,512]{1,0:T(8,128)(2,1)}, bf16[64,512]{1,0:T(8,128)(2,1)}, u32[]{:S(2)}, u32[]{:S(2)}) collective-permute-start(bf16[64,512]{1,0:T(8,128)(2,1)} %get-tuple-element.91), channel_id=1, source_target_pairs={{0,28},{4,24},{8,20},{12,16},{16,12},{20,8},{24,4},{28,0},{1,29},{... | collective-permute-start | bytes 196616 | tf_op jit(solution)/shard_map/ppermute | solution.py:46

commit v4 on v3

--- a/solution.py
+++ b/solution.py
@@ -126,60 +126,109 @@
     )[0]
 
 
-def base_parts(rows, weight, parts, after):
+def base_parts(rows, weight, parts, shapes, after):
     n, width = rows.shape
     cols = weight.shape[1] // parts
+    half = parts // 2
+    tasks, rank = shapes[0][:2]
+    widest = max(x[2] for x in shapes)
     mine = lax.axis_index("tensor").astype(jnp.int32).reshape(1)
 
-    tiles = 1
-    tile = cols // tiles
+    def shard(i, m):
+        return m[0] ^ jnp.where(i < half, 2 * i + 1, 2 * (i - half))
 
     def kernel(mine, rows, weight, *rest):
-        rest[-1][0] = jnp.dot(rows[...], weight[...], preferred_element_type=f32).astype(bf)
+        odd, even, *zeros, blank, sem = rest[len(after) :]
+        step = pl.program_id(0)
+        copies = [
+            pltpu.make_async_copy(blank.at[:, pl.ds(0, z.shape[2])], z.at[t], sem.at[i, t])
+            for i, z in enumerate(zeros)
+            for t in range(tasks)
+        ]
+
+        @pl.when(step == 0)
+        def _():
+            blank[...] = jnp.zeros((rank, widest), bf)
+            for c in copies:
+                c.start()
+
+        part = jnp.dot(rows[...], weight[...], preferred_element_type=f32).astype(bf)
+
+        @pl.when(step < half)
+        def _():
+            odd[0] = part
+
+        @pl.when(step >= half)
+        def _():
+            even[0] = part
+
+        @pl.when(step == parts - 1)
+        def _():
+            for c in copies:
+                c.wait()
 
     return pl.pallas_call(
         kernel,
-        out_shape=shaped((parts, n, cols), bf),
+        out_shape=[shaped((half, n, cols), bf)] * 2 + [shaped(x, bf) for x in shapes],
         grid_spec=pltpu.PrefetchScalarGridSpec(
             num_scalar_prefetch=1,
-            grid=(parts, tiles),
+            grid=(parts,),
             in_specs=[
-                pl.BlockSpec((n, width), lambda i, j, m: (0, 0)),
-                pl.BlockSpec((width, tile), lambda i, j, m: (0, (m[0] ^ i) * tiles + j)),
+                pl.BlockSpec((n, width), lambda i, m: (0, 0)),
+                pl.BlockSpec((width, cols), lambda i, m: (0, shard(i, m))),
             ]
             + [ANY] * len(after),
-            out_specs=pl.BlockSpec((1, n, tile), lambda i, j, m: (i, 0, j)),
+            out_specs=[
+                pl.BlockSpec((1, n, cols), lambda i, m: (jnp.minimum(i, half - 1), 0, 0)),
+                pl.BlockSpec((1, n, cols), lambda i, m: (jnp.maximum(i - half, 0), 0, 0)),
+            ]
+            + [ANY] * len(shapes),
+            scratch_shapes=[
+                pltpu.VMEM((rank, widest), bf),
+                pltpu.SemaphoreType.DMA((len(shapes), tasks)),
+            ],
         ),
         compiler_params=pltpu.CompilerParams(vmem_limit_bytes=big),
-        cost_estimate=pl.CostEstimate(
-            flops=2 * n * width * weight.shape[1],
-            bytes_accessed=2 * (rows.size + weight.size + n * weight.shape[1]),
-            transcendentals=0,
-        ),
+        cost_estimate=pl.CostEstimate(flops=0, bytes_accessed=0, transcendentals=0),
     )(mine, rows, weight, *after)
 
 
-def inner_up(place, rows, blocks, rank, after):
+def inner_up(slot_row, score_row, rows, blocks, rank, after):
     n, cols = rows.shape
-
-    def kernel(ins, outs):
-        place, rows = ins[:2]
+    att = slot_row.shape[1]
+    steps = n // att
+
+    def kernel(ins, outs):
+        slot, score, rows = ins[:3]
+        start = steps * lax.broadcasted_iota(jnp.int32, (att, n), 0)
+        row = lax.broadcasted_iota(jnp.int32, (att, n), 1)
+        own = jnp.logical_and(row >= start, row < start + steps).astype(bf)
+        line = lax.broadcasted_iota(jnp.int32, (8, att), 0)
+        both = jnp.where(line == 0, slot[...], jnp.where(line == 1, score[...], 0))
+        both = jnp.dot(both.astype(f32).astype(bf), own, preferred_element_type=f32)
+        slots = both[0:1, :].astype(jnp.int32)
+        place = slots ^ lax.axis_index("dp")
+        outs[2][...] = slots
+        outs[3][...] = place
+        outs[4][...] = both[1:2, :]
         wide = lax.dot_general(
-            jnp.concatenate([up_block(block, rank) for block in ins[2:]], axis=0),
+            jnp.concatenate([up_block(block, rank) for block in ins[3:]], axis=0),
             rows[...],
             (((1,), (1,)), ((), ())),
             preferred_element_type=f32,
         )
         acc = jnp.zeros((rank, n), f32)
         for k in range(len(blocks)):
-            acc = jnp.where(place[...] == k, wide[k * rank : (k + 1) * rank], acc)
+            acc = jnp.where(place == k, wide[k * rank : (k + 1) * rank], acc)
         outs[0][...] = acc
         outs[1][...] = acc.astype(bf)
 
-    operands = (place, rows, *blocks)
+    operands = (slot_row, score_row, rows, *blocks)
     return call(
         kernel,
-        [shaped((rank, n), f32), shaped((rank, n), bf)],
+        [shaped((rank, n), f32), shaped((rank, n), bf)]
+        + [shaped((1, n), jnp.int32)] * 2
+        + [shaped((1, n), f32)],
         operands,
         [VMEM] * len(operands),
         flops=2 * n * cols * rank * len(blocks),
@@ -215,19 +264,19 @@
     )
 
 
-def plus(x, got):
+def plus(x, got, after):
     def kernel(ins, outs):
         total = ins[0][...] + ins[1][...].astype(f32)
         outs[0][...] = total
         outs[1][...] = total.astype(bf)
 
-    return call(kernel, [shaped(x.shape, f32), shaped(x.shape, bf)], (x, got), [VMEM] * 2)
-
-
-def sum_first(x, wire, axis):
+    return call(kernel, [shaped(x.shape, f32), shaped(x.shape, bf)], (x, got), [VMEM] * 2, after=after)
+
+
+def sum_first(x, wire, axis, after=()):
     k = 1
     while 2 * k < lax.axis_size(axis):
-        x, wire = plus(x, swap(wire, k, axis))
+        x, wire = plus(x, swap(wire, k, axis), after)
         k *= 2
     return x, swap(wire, k, axis)
 
@@ -236,7 +285,7 @@
     return jnp.where(place == k, inner_t, jnp.zeros((), inner_t.dtype))
 
 
-def down_grads(gst, place, slot_rows, score_rows, t, t_got, rows, up_blocks, early):
+def down_grads(gst, place, slot_rows, score_rows, t, t_got, rows, up_blocks):
     groups = len(up_blocks)
     rank, n = t.shape
     width = rows.shape[1]
@@ -258,68 +307,66 @@
         )
         mean = jnp.sum(jnp.where(here, mean, 0.0), axis=1, keepdims=True)
         hot = slot[...] == lax.broadcasted_iota(jnp.int32, (groups, n), 0)
-        adv = score[...].astype(f32) - jnp.sum(jnp.where(hot, mean, 0.0), axis=0, keepdims=True)
+        adv = score[...] - jnp.sum(jnp.where(hot, mean, 0.0), axis=0, keepdims=True)
         total = (adv * (t[...] + t_got[...].astype(f32))).astype(bf)
         outs[0][...] = adv
         wide = jnp.concatenate([spread(place[...], total, k) for k in range(groups)], axis=0)
-        part = jnp.dot(wide, rows[:, :early], preferred_element_type=f32)
-        part = (scale * part).astype(bf)
-        for k in range(groups):
-            outs[2 + k][...] = part[k * rank : (k + 1) * rank]
-        wide = jnp.concatenate([spread(slot[...], total, s) for s in range(groups)], axis=0)
-        part = jnp.dot(wide, rows[:, early:], preferred_element_type=f32)
-        outs[1][...] = (scale * part).astype(bf).reshape(groups, rank, width - early)
+        chunk = width // 2 if width % 256 == 0 else width
+        for first in range(0, width, chunk):
+            part = jnp.dot(wide, rows[:, first : first + chunk], preferred_element_type=f32)
+            part = (scale * part).astype(bf)
+            for k in range(groups):
+                outs[1 + k][:, first : first + chunk] = part[k * rank : (k + 1) * rank]
 
     operands = (gst, place, slot_rows, score_rows, t, t_got, rows, *up_blocks)
     out = call(
         kernel,
-        [shaped((1, n), f32), shaped((groups, rank, width - early), bf)]
-        + [shaped((rank, early), bf)] * groups,
+        [shaped((1, n), f32)] + [shaped((rank, width), bf)] * groups,
         operands,
         [VMEM] * len(operands),
         flops=2 * n * width * rank * groups,
     )
-    return out[0], out[1], out[2:]
-
-
-def up_grads(place, adv, t, t_got, cot, groups):
+    return out[0], out[1:]
+
+
+def up_grads(place, adv, t, t_got, cot, groups, after):
     rank, n = t.shape
     cols = cot.shape[1]
 
     def kernel(ins, outs):
         place, adv, t, t_got, cot = ins
         total = t[...] + t_got[...].astype(f32)
-        outs[0][...] = total.astype(bf)
         total = (adv[...] * total).astype(bf)
         wide = jnp.concatenate([spread(place[...], total, k) for k in range(groups)], axis=0)
         part = (scale * jnp.dot(wide, cot[...], preferred_element_type=f32)).astype(bf)
         for k in range(groups):
-            outs[1 + k][...] = part[k * rank : (k + 1) * rank]
-
-    out = call(
-        kernel,
-        [shaped((rank, n), bf)] + [shaped((rank, cols), bf)] * groups,
+            outs[k][...] = part[k * rank : (k + 1) * rank]
+
+    return call(
+        kernel,
+        [shaped((rank, cols), bf)] * groups,
         (place, adv, t, t_got, cot),
         [VMEM] * 5,
+        after=after,
         flops=2 * n * cols * rank * groups,
     )
-    return out[0], out[1:]
-
-
-def adapted(place, inner_t, base_mine, base_got, blocks, after):
+
+
+def adapted(place, t, t_got, base_mine, base_got, blocks, after):
     n, cols = base_got.shape
-    rank = inner_t.shape[0]
-
-    def kernel(ins, outs):
-        place, t, base_mine, base_got = ins[:4]
-        blocks = ins[4:]
-        wide = jnp.concatenate([spread(place[...], t[...], k) for k in range(len(blocks))], axis=0)
+    rank = t.shape[0]
+
+    def kernel(ins, outs):
+        place, t, t_got, base_mine, base_got = ins[:5]
+        blocks = ins[5:]
+        total = (t[...] + t_got[...].astype(f32)).astype(bf)
+        wide = jnp.concatenate([spread(place[...], total, k) for k in range(len(blocks))], axis=0)
         ups = jnp.concatenate([up_block(b, rank) for b in blocks], axis=0)
         delta = lax.dot_general(wide, ups, (((0,), (0,)), ((), ())), preferred_element_type=f32)
         delta = (scale * delta).astype(bf).astype(f32)
         outs[0][...] = (base_mine[...].astype(f32) + base_got[...].astype(f32) + delta).astype(bf)
 
-    operands = (place, inner_t, base_mine, base_got, *blocks)
+    operands = (place, t, t_got, base_mine, base_got, *blocks)
     return call(
         kernel,
         [shaped((n, cols), bf)],
@@ -330,27 +377,10 @@
     )[0]
 
 
-def zeros(shape, after):
-    def kernel(refs):
-        refs[-1][...] = jnp.zeros(refs[-1].shape, bf)
-
-    chunk = 4 if shape[0] % 4 == 0 else 1
-    return pl.pallas_call(
-        lambda *refs: kernel(refs),
-        out_shape=shaped(shape, bf),
-        grid=(shape[0] // chunk,),
-        in_specs=[ANY] * len(after),
-        out_specs=pl.BlockSpec((chunk,) + shape[1:], lambda t: (t, 0, 0)),
-        compiler_params=pltpu.CompilerParams(vmem_limit_bytes=big),
-        cost_estimate=pl.CostEstimate(flops=0, bytes_accessed=0, transcendentals=0),
-    )(*after)
-
-
-def combine(gst, trp, blocks, rest, filled, after):
+def combine(gst, trp, blocks, filled, after):
     groups = gst.shape[0]
     tasks, rank, width = filled.shape
-    count = len(blocks) + len(rest)
-    early = blocks[0].shape[1]
+    count = len(blocks)
 
     def kernel(*refs):
         gst, trp = refs[:2]
@@ -359,13 +389,9 @@
         me = lax.axis_index("dp")
         copies = []
         for k in range(groups):
-            parts = [pltpu.make_async_copy(ins[k], held.at[k, :, pl.ds(0, early)], sem_in.at[0, k])]
-            if rest:
-                place = held.at[k, :, pl.ds(early, width - early)]
-                parts.append(pltpu.make_async_copy(ins[groups].at[me ^ k], place, sem_in.at[1, k]))
-            for c in parts:
-                c.start()
-            copies.append(parts)
+            source = ins[k] if count > 1 else ins[0].at[me ^ k]
+            copies.append(pltpu.make_async_copy(source, held.at[k], sem_in.at[k]))
+            copies[-1].start()
         rows = [stored_row(gst, trp, tasks, k) for k in range(groups)]
         back = [
             pltpu.make_async_copy(held.at[g], out.at[rows[g]], sem_out.at[g])
@@ -380,8 +406,7 @@
                 if h < g:
                     again = jnp.logical_or(again, rows[h] == rows[g])
             last.append(ends)
-            for c in copies[g]:
-                c.wait()
+            copies[g].wait()
 
             @pl.when(jnp.logical_and(ends, again))
             def _():
@@ -412,13 +437,13 @@
         scratch_shapes=[
             pltpu.VMEM((groups, rank, width), bf),
             pltpu.VMEM((rank, width), f32),
-            pltpu.SemaphoreType.DMA((2, groups)),
+            pltpu.SemaphoreType.DMA((groups,)),
             pltpu.SemaphoreType.DMA((groups,)),
         ],
         input_output_aliases={2 + count: 0},
         compiler_params=pltpu.CompilerParams(vmem_limit_bytes=big),
         cost_estimate=pl.CostEstimate(flops=0, bytes_accessed=0, transcendentals=0),
-    )(gst, trp, *blocks, *rest, filled, *after)
+    )(gst, trp, *blocks, filled, *after)
 
 
 def exchange(x):
@@ -432,6 +457,7 @@
 
 def body(hidden, weight, down, up, slot, gst, trp, scores, cotangent):
     groups, parts = lax.axis_size("dp"), lax.axis_size("tensor")
+    half = groups // 2
     me = lax.axis_index("dp")
     att, steps, width = hidden.shape
     cols = cotangent.shape[2]
@@ -446,49 +472,47 @@
     down_out = pack_down(gst, trp, down, (up_out[0],))
     down_got = exchange(lax.optimization_barrier((down_out, *up_got))[0])
 
-    hidden, cotangent, slot_row, score_row, _ = lax.optimization_barrier(
-        (hidden, cotangent, slot_row, score_row, up_out[0])
-    )
-    slot_rows = jnp.repeat(slot_row, steps, axis=1)
-    score_rows = jnp.repeat(score_row, steps, axis=1)
-    place = slot_rows ^ me
+    hidden, cotangent, _ = lax.optimization_barrier((hidden, cotangent, up_out[0]))
     cot = cotangent.reshape(n, cols)
     rows = hidden.reshape(n, width)
 
-    back, back_wire = inner_up(place, cot, up_got, rank, ())
+    back, back_wire, slot_rows, place, score_rows = inner_up(
+        slot_row, score_row, cot, up_got, rank, ()
+    )
     back, back_got = sum_first(back, back_wire, "tensor")
-    early = max(lanes, width // 4)
-    adv, down_grad, early_grad = down_grads(
-        gst, place, slot_rows, score_rows, back, back_got, rows, up_got, early
-    )
-    early_got = partners(early_grad)
-
-    base = base_parts(rows, weight, parts, (adv,))
-    held = [base[i] for i in range(parts)]
-    k = 1
+    adv, down_grad = down_grads(
+        gst, place, slot_rows, score_rows, back, back_got, rows, up_got
+    )
+    late = range(half + half // 2, groups)
+    down_grad = list(down_grad)
+    for k in late:
+        down_grad[k] = lax.optimization_barrier((down_grad[k], down_got))[0]
+    down_grad_got = partners(down_grad)
+
+    odd, even, zero_down, zero_up = base_parts(
+        rows, weight, parts, ((tasks, rank, width), (tasks, rank, cols)), (adv,)
+    )
+    held, k = [odd, even], 1
     while 2 * k < parts:
-        got = swap(jnp.stack(held[1::2]), k, "tensor")
-        held = [
-            (a.astype(f32) + got[i].astype(f32)).astype(bf) for i, a in enumerate(held[0::2])
-        ]
-        k *= 2
-    zero_down = zeros((tasks, rank, width), (adv,))
-    zero_up = zeros((tasks, rank, cols), (adv,))
-    down_grad, base_mine, base_far, zero_down, zero_up = lax.optimization_barrier(
-        (down_grad, held[0], held[1], zero_down, zero_up, *early_got)
-    )[:5]
+        got = swap(held[0], k, "tensor").astype(f32)
+        both = (held[1].astype(f32) + got).astype(bf)
+        held, k = [both[1::2], both[0::2]], 2 * k
+    base_far, base_mine = held[0].reshape(n, cols), held[1].reshape(n, cols)
     base_got = swap(base_far, k, "tensor")
-    down_grad_got = exchange(down_grad)
-
-    ahead, ahead_wire = inner_down(slot_rows, rows, down_got, (base,))
+
+    ahead, ahead_wire = inner_down(slot_rows, rows, down_got, (base_got, *down_grad_got[1:half]))
     ahead, ahead_got = sum_first(ahead, ahead_wire, "tensor")
-    inner_all, up_grad = up_grads(place, adv, ahead, ahead_got, cot, groups)
-    up_grad_got = partners(up_grad)
-    kv_new = adapted(place, inner_all, base_mine, base_got, up_got, (up_grad[0],))
+    kv_new = adapted(place, ahead, ahead_got, base_mine, base_got, up_got, ())
     kv_out = kv_new.reshape(att, steps, cols)
-
-    grad_down = combine(gst, trp, early_got, [down_grad_got], zero_down, (kv_new,))
-    grad_up = combine(gst, trp, up_grad_got, [], zero_up, (grad_down,))
+    up_grad = up_grads(
+        place, adv, ahead, ahead_got, cot, groups, (kv_out, *down_grad_got[half : half + half // 2])
+    )
+    up_grad_got = [up_grad[0]] + [None] * (groups - 1)
+    for k in [*range(half, groups), *range(1, half)]:
+        x = lax.optimization_barrier((up_grad[k], down_grad_got[k]))[0]
+        up_grad_got[k] = swap(x, k, "dp")
+    grad_down = combine(gst, trp, down_grad_got, zero_down, ())
+    grad_up = combine(gst, trp, up_grad_got, zero_up, (grad_down,))
     return (kv_out, jnp.swapaxes(grad_down, 1, 2), grad_up)
 
 

time: 142 us -> 139 us (0.979)
  waiting for transfers between devices: 28.7 us -> 36.7 us
  starting transfers between devices: 52.6 us -> 49.1 us
  Pallas kernels: 44.6 us -> 41.5 us
  other arithmetic: 4.49 us -> 1.6 us
  local copies, waits for them, and re-layouts: 10.2 us -> 8.07 us
    all_to_all x2 -> x1, starting transfers between devices: 9.2 us -> 4.68 us  [exchange(): return lax.all_to_all(x, 'dp', split_axis=0, concat_axis=0, tiled=True)]
    all_to_all x2 -> x1, waiting for transfers between devices: 6.45 us -> 10.7 us  [exchange(): return lax.all_to_all(x, 'dp', split_axis=0, concat_axis=0, tiled=True)]
    ppermute x27, waiting for transfers between devices: 22.3 us -> 26 us  [swap(): return lax.ppermute(x, axis, [(i, i ^ k) for i in range(n)])]
    pallas_call x3 -> x1, Pallas kernels: 12.7 us -> 9.83 us  [base_parts(): pl.pallas_call(kernel, out_shape=[shaped((half, n, cols), bf)] * 2 + [sha...]
    broadcast_in_dim x4 -> x0, local copies, waits for them, and re-layouts: 1.72 us -> none  [the longest x2 1.49 us: body(): score_rows = jnp.repeat(score_row, steps, axis=1)]
  transfers between devices with their start and end apart: 29 -> 28, of which waited for: 9 -> 11; matrix products, arithmetic and copies ran while one was open for 10% -> 7% of each run, Pallas kernels for 28% -> 26%
where the time goes in v4:
time: 139 us; the launch traced here: 138 us
  starting transfers between devices  49.1 us (35%)
  Pallas kernels  41.5 us (30%)
  waiting for transfers between devices  36.7 us (26%)
  local copies, waits for them, and re-layouts  8.07 us (6%)
  other arithmetic  1.6 us (1%)
    ppermute x27, starting transfers between devices, swap(): return lax.ppermute(x, axis, [(i, i ^ k) for i in range(n)])  44.5 us
    ppermute x27, waiting for transfers between devices, swap(): return lax.ppermute(x, axis, [(i, i ^ k) for i in range(n)])  26 us
    pallas_call x9, Pallas kernels, call(): pl.pallas_call(run, out_shape=list(outs), in_specs=list(specs) + [ANY] *...  25.9 us
    all_to_all x1, waiting for transfers between devices, exchange(): return lax.all_to_all(x, 'dp', split_axis=0, concat_axis=0, tiled=True)  10.7 us
    pallas_call x1, Pallas kernels, base_parts(): pl.pallas_call(kernel, out_shape=[shaped((half, n, cols), bf)] * 2 + [sha...  9.83 us
    pallas_call x2, Pallas kernels, combine(): pl.pallas_call(kernel, out_shape=shaped(filled.shape, bf), in_specs=[SMEM...  5.78 us
    all_to_all x1, starting transfers between devices, exchange(): return lax.all_to_all(x, 'dp', split_axis=0, concat_axis=0, tiled=True)  4.68 us
    reshape x1, local copies, waits for them, and re-layouts, body(): rows = hidden.reshape(n, width)  4.13 us
  transfers between devices with their start and end apart: 28, of which 11 were waited for; matrix products, arithmetic and copies ran while one was open for 7% of the time, Pallas kernels for 26%

profile of v4, /device:TPU:0, one launch (start us, length us, event | category | flops | bytes accessed | tf_op | source)
XLA Modules:
  0.0 137.8 jit_solution(1016254110678831687)
XLA Ops:
  0.6 2.8 %shard_map.112 = (bf16[272,128]{1,0:T(8,128)(2,1)}, bf16[272,128]{1,0:T(8,128)(2,1)}, bf16[272,128]{1,0:T(8,128)(2,1)}, bf16[272,128]{1,0:T(8,128)(2,1)}, bf16[2...) custom-call(s32[8,8]{1,0:T(8,128)} %refs_0_.9, ...), custom_call_target="tpu_custom_call" | custom-call | tf_op jit(solution)/shard_map/pallas_call | solution.py:33
  3.5 3.0 %collective-permute-start = (bf16[272,128]{1,0:T(8,128)(2,1)}, bf16[272,128]{1,0:T(8,128)(2,1)}, u32[]{:S(2)}, u32[]{:S(2)}) collective-permute-start(bf16[272,128]{1,0:T(8,128)(2,1)} %get-tuple-element.57), channel_id=1, source_target_pairs={{0,4},{4,0},{8,12},{12,8},{16,20},{20,16},{24,28},{28,24},{1,5},{5... | collective-permute-start | bytes 208904 | tf_op jit(solution)/shard_map/ppermute | solution.py:46
  8.1 3.0 %collective-permute-start.3 = (bf16[272,128]{1,0:T(8,128)(2,1)}, bf16[272,128]{1,0:T(8,128)(2,1)}, u32[]{:S(2)}, u32[]{:S(2)}) collective-permute-start(bf16[272,128]{1,0:T(8,128)(2,1)} %get-tuple-element.60), channel_id=1, source_target_pairs={{0,16},{4,20},{8,24},{12,28},{16,0},{20,4},{24,8},{28,12},{1,17},{... | collective-permute-start | bytes 208904 | tf_op jit(solution)/shard_map/ppermute | solution.py:46
  12.3 3.6 %collective-permute-start.5 = (bf16[272,128]{1,0:T(8,128)(2,1)}, bf16[272,128]{1,0:T(8,128)(2,1)}, u32[]{:S(2)}, u32[]{:S(2)}) collective-permute-start(bf16[272,128]{1,0:T(8,128)(2,1)} %get-tuple-element.62), channel_id=1, source_target_pairs={{0,24},{4,28},{8,16},{12,20},{16,8},{20,12},{24,0},{28,4},{1,25},{... | collective-permute-start | bytes 208904 | tf_op jit(solution)/shard_map/ppermute | solution.py:46
  16.0 3.7 %shard_map.114 = bf16[8,64,2048]{2,1,0:T(8,128)(2,1)} custom-call(s32[8,8]{1,0:T(8,128)} %refs_0_.9, s32[128]{0:T(128)} %refs_1_.7, bf16[16,64,2048]{2,1,0:T(8,128)(2,1)} %bitcast.10, bf16[272,128]{1,0:T(8,128)(2,1)} %get-tuple-element.55.refs_3_.refs_7_.refs_5_), custom_call_target="tpu_custom_call" | custom-call | tf_op jit(solution)/shard_map/pallas_call | solution.py:33
  19.7 2.4 %collective-permute-done.4.refs_8_.refs_12_.refs_10_ = bf16[272,128]{1,0:T(8,128)(2,1)} collective-permute-done((bf16[272,128]{1,0:T(8,128)(2,1)}, bf16[272,128]{1,0:T(8,128)(2,1)}, u32[]{:S(2)}, u32[]{:S(2)}) %collective-permute-start.4) | collective-permute-done | bytes 69664 | tf_op jit(solution)/shard_map/ppermute | solution.py:46
  23.4 4.7 %all-to-all-start = ((bf16[8,64,2048]{2,1,0:T(8,128)(2,1)}), bf16[8,64,2048]{2,1,0:T(8,128)(2,1)}, u32[]{:S(2)}, u32[]{:S(2)}) async-start(bf16[8,64,2048]{2,1,0:T(8,128)(2,1)} %shard_map.114), calls=%async_computation | async-start | bytes 4194304 | tf_op jit(solution)/shard_map/all_to_all | solution.py:450
  29.1 2.5 %shard_map.113 = (f32[64,512]{1,0:T(8,128)}, bf16[64,512]{1,0:T(8,128)(2,1)}, s32[1,512]{1,0:T(1,128)}, s32[1,512]{1,0:T(1,128)}, f32[1,512]{1,0:T(1,128)}) custom-call(s32[1,256]{1,0:T(1,128)} %bitcast.12, s32[1,256]{1,0:T(1,128)} %bitcast.14, bf16[512,512]{1,0:T(8,128)(2,1)} %reshape.32.refs_2_.refs_4_, ...), custom_call_target="tpu_custom_call" | custom-call | tf_op jit(solution)/shard_map/pallas_call | solution.py:33
  33.2 1.6 %shard_map.115 = (f32[64,512]{1,0:T(8,128)}, bf16[64,512]{1,0:T(8,128)(2,1)}) custom-call(f32[64,512]{1,0:T(8,128)} %get-tuple-element.69.refs_0_, bf16[64,512]{1,0:T(8,128)(2,1)} %collective-permute-done.7.refs_1_), custom_call_target="tpu_custom_call" | custom-call | tf_op jit(solution)/shard_map/pallas_call | solution.py:33
  36.3 4.1 %reshape.33.refs_6_.rows.refs_1_ = bf16[512,2048]{1,0:T(8,128)(2,1)} reshape(bf16[256,2,2048]{2,1,0:T(2,128)(2,1)} %param.9) | data formatting | bytes 4194304 | tf_op jit(solution)/shard_map/reshape | solution.py:477
  40.4 4.5 %shard_map.116 = (f32[1,512]{1,0:T(1,128)}, bf16[64,2048]{1,0:T(8,128)(2,1)}, bf16[64,2048]{1,0:T(8,128)(2,1)}, bf16[64,2048]{1,0:T(8,128)(2,1)}, bf16[64,2048]{...) custom-call(s32[8,8]{1,0:T(8,128)} %refs_0_.9, ...), custom_call_target="tpu_custom_call" | custom-call | tf_op jit(solution)/shard_map/pallas_call | solution.py:33
  44.9 9.8 %shard_map.117 = (bf16[2,512,512]{2,1,0:T(8,128)(2,1)}, bf16[2,512,512]{2,1,0:T(8,128)(2,1)}, bf16[16,64,2048]{2,1,0:T(8,128)(2,1)}, bf16[16,64,512]{2,1,0:T(8,128)(2,1)}) custom-call(s32[1]{0:T(128)} %bitcast.3.mine, bf16[512,2048]{1,0:T(8,128)(2,1)} %reshape.33.refs_6_.rows.refs_1_, bf16[2048,2048]{1,0:T(8,128)(2,1)} %weight.1, ...), custom_call_target="tpu_custom_call" | custom-call | tf_op jit(solution)/shard_map/pallas_call | solution.py:170
  54.8 2.9 %collective-permute-done.9 = bf16[2,512,512]{2,1,0:T(8,128)(2,1)S(1)} collective-permute-done((bf16[2,512,512]{2,1,0:T(8,128)(2,1)}, bf16[2,512,512]{2,1,0:T(8,128)(2,1)S(1)}, u32[]{:S(2)}, u32[]{:S(2)}) %collective-permute-start.9) | collective-permute-done | bytes 1048608 | tf_op jit(solution)/shard_map/ppermute | solution.py:46
  57.7 1.6 %add_convert_fusion = bf16[2,512,512]{2,1,0:T(8,128)(2,1)S(1)} fusion(bf16[2,512,512]{2,1,0:T(8,128)(2,1)S(1)} %collective-permute-done.9, bf16[2,512,512]{2,1,0:T(8,128)(2,1)} %get-tuple-element.74), kind=kLoop, calls=%fused_computation | loop fusion | flops 2097152 | bytes 3145728 | tf_op jit(solution)/shard_map/convert_element_type | solution.py:498
  60.6 2.0 %collective-permute-start.11 = (bf16[64,2048]{1,0:T(8,128)(2,1)S(1)}, bf16[64,2048]{1,0:T(8,128)(2,1)}, u32[]{:S(2)}, u32[]{:S(2)}) collective-permute-start(bf16[64,2048]{1,0:T(8,128)(2,1)S(1)} %copy-done.3), channel_id=1, source_target_pairs={{0,4},{4,0},{8,12},{12,8},{16,20},{20,16},{24,28},{28,24},{1,5},{5... | collective-permute-start | bytes 786440 | tf_op jit(solution)/shard_map/ppermute | solution.py:46
  64.2 3.0 %collective-permute-start.16 = (bf16[64,2048]{1,0:T(8,128)(2,1)}, bf16[64,2048]{1,0:T(8,128)(2,1)}, u32[]{:S(2)}, u32[]{:S(2)}) collective-permute-start(bf16[64,2048]{1,0:T(8,128)(2,1)} %get-tuple-element.84), channel_id=1, source_target_pairs={{0,16},{4,20},{8,24},{12,28},{16,0},{20,4},{24,8},{28,12},{1,17},{... | collective-permute-start | bytes 786440 | tf_op jit(solution)/shard_map/ppermute | solution.py:46
  67.2 6.1 %collective-permute-done.11.refs_4_.refs_3_ = bf16[64,2048]{1,0:T(8,128)(2,1)} collective-permute-done((bf16[64,2048]{1,0:T(8,128)(2,1)S(1)}, bf16[64,2048]{1,0:T(8,128)(2,1)}, u32[]{:S(2)}, u32[]{:S(2)}) %collective-permute-start.11) | collective-permute-done | bytes 262176 | tf_op jit(solution)/shard_map/ppermute | solution.py:46
  73.2 8.3 %collective-permute-start.17 = (bf16[64,2048]{1,0:T(8,128)(2,1)}, bf16[64,2048]{1,0:T(8,128)(2,1)}, u32[]{:S(2)}, u32[]{:S(2)}) collective-permute-start(bf16[64,2048]{1,0:T(8,128)(2,1)} %get-tuple-element.85), channel_id=1, source_target_pairs={{0,20},{4,16},{8,28},{12,24},{16,4},{20,0},{24,12},{28,8},{1,21},{... | collective-permute-start | bytes 786440 | tf_op jit(solution)/shard_map/ppermute | solution.py:46
  81.5 10.7 %all-to-all-done.refs_2_ = bf16[8,64,2048]{2,1,0:T(8,128)(2,1)} async-done(((bf16[8,64,2048]{2,1,0:T(8,128)(2,1)}), bf16[8,64,2048]{2,1,0:T(8,128)(2,1)}, u32[]{:S(2)}, u32[]{:S(2)}) %all-to-all-start) | async-done | bytes 2097184 | tf_op jit(solution)/shard_map/all_to_all | solution.py:450
  93.6 4.2 %shard_map.118 = (f32[64,512]{1,0:T(8,128)}, bf16[64,512]{1,0:T(8,128)(2,1)}) custom-call(s32[1,512]{1,0:T(1,128)} %get-tuple-element.65.refs_2_.refs_0_, bf16[512,2048]{1,0:T(8,128)(2,1)} %reshape.33.refs_6_.rows.refs_1_, bf16[8,64,2048]{2,1,0:T(8,128)(2,1)} %all-to-all-done.refs_2_, bf16[512,512]{1,0:T(8,128)(2,1)} %collective-permute-done.10.refs_3_.refs_4_, ...), custom_call_target="tpu_custom_call" | custom-call | tf_op jit(solution)/shard_map/pallas_call | solution.py:33
  97.7 1.6 %collective-permute-done.14.refs_1_ = bf16[64,512]{1,0:T(8,128)(2,1)} collective-permute-done((bf16[64,512]{1,0:T(8,128)(2,1)}, bf16[64,512]{1,0:T(8,128)(2,1)}, u32[]{:S(2)}, u32[]{:S(2)}) %collective-permute-start.14) | collective-permute-done | bytes 65568 | tf_op jit(solution)/shard_map/ppermute | solution.py:46
  102.4 3.1 %collective-permute-done.15.refs_2_.refs_3_ = bf16[64,512]{1,0:T(8,128)(2,1)} collective-permute-done((bf16[64,512]{1,0:T(8,128)(2,1)}, bf16[64,512]{1,0:T(8,128)(2,1)}, u32[]{:S(2)}, u32[]{:S(2)}) %collective-permute-start.15) | collective-permute-done | bytes 65568 | tf_op jit(solution)/shard_map/ppermute | solution.py:46
  105.5 2.8 %shard_map.120 = bf16[512,512]{1,0:T(8,128)(2,1)} custom-call(s32[1,512]{1,0:T(1,128)} %get-tuple-element.64.refs_1_.refs_0_, f32[64,512]{1,0:T(8,128)} %get-tuple-element.81.refs_1_.refs_2_, bf16[64,512]{1,0:T(8,128)(2,1)} %collective-permute-done.15.refs_2_.refs_3_, bf16[512,512]{1,0:T(8,128)(2,1)} %get-tuple-element.107.refs_3_, ...), custom_call_target="tpu_custom_call" | custom-call | tf_op jit(solution)/shard_map/pallas_call | solution.py:33
  108.3 2.0 %reshape.37.refs_5_ = bf16[256,2,512]{2,1,0:T(2,128)(2,1)} reshape(bf16[512,512]{1,0:T(8,128)(2,1)} %shard_map.120) | data formatting | bytes 1048576 | tf_op jit(solution)/shard_map/reshape | solution.py:506
  110.3 1.6 %collective-permute-done.17.refs_7_ = bf16[64,2048]{1,0:T(8,128)(2,1)} collective-permute-done((bf16[64,2048]{1,0:T(8,128)(2,1)}, bf16[64,2048]{1,0:T(8,128)(2,1)}, u32[]{:S(2)}, u32[]{:S(2)}) %collective-permute-start.17) | collective-permute-done | bytes 262176 | tf_op jit(solution)/shard_map/ppermute | solution.py:46
  111.9 2.3 %shard_map.122 = (bf16[64,512]{1,0:T(8,128)(2,1)}, bf16[64,512]{1,0:T(8,128)(2,1)}, bf16[64,512]{1,0:T(8,128)(2,1)}, bf16[64,512]{1,0:T(8,128)(2,1)}, bf16[64,51...) custom-call(s32[1,512]{1,0:T(1,128)} %get-tuple-element.64.refs_1_.refs_0_, ...), custom_call_target="tpu_custom_call" | custom-call | tf_op jit(solution)/shard_map/pallas_call | solution.py:33
  114.2 4.7 %collective-permute-start.23 = (bf16[64,512]{1,0:T(8,128)(2,1)}, bf16[64,512]{1,0:T(8,128)(2,1)}, u32[]{:S(2)}, u32[]{:S(2)}) collective-permute-start(bf16[64,512]{1,0:T(8,128)(2,1)} %get-tuple-element.99), channel_id=1, source_target_pairs={{0,16},{4,20},{8,24},{12,28},{16,0},{20,4},{24,8},{28,12},{1,17},{... | collective-permute-start | bytes 196616 | tf_op jit(solution)/shard_map/ppermute | solution.py:46
  120.1 2.3 %collective-permute-start.20 = (bf16[64,512]{1,0:T(8,128)(2,1)}, bf16[64,512]{1,0:T(8,128)(2,1)}, u32[]{:S(2)}, u32[]{:S(2)}) collective-permute-start(bf16[64,512]{1,0:T(8,128)(2,1)} %get-tuple-element.93), channel_id=1, source_target_pairs={{0,4},{4,0},{8,12},{12,8},{16,20},{20,16},{24,28},{28,24},{1,5},{5... | collective-permute-start | bytes 196616 | tf_op jit(solution)/shard_map/ppermute | solution.py:46
  122.4 5.2 %collective-permute-done.24.refs_7_ = bf16[64,512]{1,0:T(8,128)(2,1)} collective-permute-done((bf16[64,512]{1,0:T(8,128)(2,1)}, bf16[64,512]{1,0:T(8,128)(2,1)}, u32[]{:S(2)}, u32[]{:S(2)}) %collective-permute-start.24) | collective-permute-done | bytes 65568 | tf_op jit(solution)/shard_map/ppermute | solution.py:46
  128.6 3.0 %collective-permute-start.25 = (bf16[64,512]{1,0:T(8,128)(2,1)}, bf16[64,512]{1,0:T(8,128)(2,1)}, u32[]{:S(2)}, u32[]{:S(2)}) collective-permute-start(bf16[64,512]{1,0:T(8,128)(2,1)} %get-tuple-element.103), channel_id=1, source_target_pairs={{0,24},{4,28},{8,16},{12,20},{16,8},{20,12},{24,0},{28,4},{1,25},{... | collective-permute-start | bytes 196616 | tf_op jit(solution)/shard_map/ppermute | solution.py:46
  131.7 3.2 %shard_map.121.refs_11_ = bf16[16,64,2048]{2,1,0:T(8,128)(2,1)} custom-call(s32[8,8]{1,0:T(8,128)} %refs_0_.9, s32[128]{0:T(128)} %refs_1_.7, bf16[64,2048]{1,0:T(8,128)(2,1)} %get-tuple-element.83.refs_2_, bf16[64,2048]{1,0:T(8,128)(2,1)} %collective-permute-done.11.refs_4_.refs_3_, ...), custom_call_target="tpu_custom_call", output_to_operand_aliasing={{}: (10, {})} | custom-call | tf_op jit(solution)/shard_map/pallas_call | solution.py:432
  135.2 2.6 %shard_map.123 = bf16[16,64,512]{2,1,0:T(8,128)(2,1)} custom-call(s32[8,8]{1,0:T(8,128)} %refs_0_.9, s32[128]{0:T(128)} %refs_1_.7, bf16[64,512]{1,0:T(8,128)(2,1)} %get-tuple-element.91.refs_2_, bf16[64,512]{1,0:T(8,128)(2,1)} %collective-permute-done.20.refs_3_, bf16[64,512]{1,0:T(8,128)(2,1)} %collective-permute-done.21.refs_4_, ...), custom_call_target="tpu_custom_call", output_to_operand_aliasing={{}: (10, {})} | custom-call | tf_op jit(solution)/shard_map/pallas_call | solution.py:432
  (49 shorter events, 18.2 us)
Async XLA Ops:
  3.5 8.9 %collective-permute-start = (bf16[272,128]{1,0:T(8,128)(2,1)}, bf16[272,128]{1,0:T(8,128)(2,1)}, u32[]{:S(2)}, u32[]{:S(2)}) collective-permute-start(bf16[272,128]{1,0:T(8,128)(2,1)} %get-tuple-element.57), channel_id=1, source_target_pairs={{0,4},{4,0},{8,12},{12,8},{16,20},{20,16},{24,28},{28,24},{1,5},{5... | collective-permute-start | bytes 208904 | tf_op jit(solution)/shard_map/ppermute | solution.py:46
  6.5 9.5 %collective-permute-start.1 = (bf16[272,128]{1,0:T(8,128)(2,1)}, bf16[272,128]{1,0:T(8,128)(2,1)}, u32[]{:S(2)}, u32[]{:S(2)}) collective-permute-start(bf16[272,128]{1,0:T(8,128)(2,1)} %get-tuple-element.58), channel_id=1, source_target_pairs={{0,8},{4,12},{8,0},{12,4},{16,24},{20,28},{24,16},{28,20},{1,9},{5... | collective-permute-start | bytes 208904 | tf_op jit(solution)/shard_map/ppermute | solution.py:46
  8.1 11.6 %collective-permute-start.2 = (bf16[272,128]{1,0:T(8,128)(2,1)}, bf16[272,128]{1,0:T(8,128)(2,1)}, u32[]{:S(2)}, u32[]{:S(2)}) collective-permute-start(bf16[272,128]{1,0:T(8,128)(2,1)} %get-tuple-element.59), channel_id=1, source_target_pairs={{0,12},{4,8},{8,4},{12,0},{16,28},{20,24},{24,20},{28,16},{1,13},{... | collective-permute-start | bytes 208904 | tf_op jit(solution)/shard_map/ppermute | solution.py:46
  8.1 11.6 %collective-permute-start.3 = (bf16[272,128]{1,0:T(8,128)(2,1)}, bf16[272,128]{1,0:T(8,128)(2,1)}, u32[]{:S(2)}, u32[]{:S(2)}) collective-permute-start(bf16[272,128]{1,0:T(8,128)(2,1)} %get-tuple-element.60), channel_id=1, source_target_pairs={{0,16},{4,20},{8,24},{12,28},{16,0},{20,4},{24,8},{28,12},{1,17},{... | collective-permute-start | bytes 208904 | tf_op jit(solution)/shard_map/ppermute | solution.py:46
  11.1 11.0 %collective-permute-start.4 = (bf16[272,128]{1,0:T(8,128)(2,1)}, bf16[272,128]{1,0:T(8,128)(2,1)}, u32[]{:S(2)}, u32[]{:S(2)}) collective-permute-start(bf16[272,128]{1,0:T(8,128)(2,1)} %get-tuple-element.61), channel_id=1, source_target_pairs={{0,20},{4,16},{8,28},{12,24},{16,4},{20,0},{24,12},{28,8},{1,21},{... | collective-permute-start | bytes 208904 | tf_op jit(solution)/shard_map/ppermute | solution.py:46
  12.3 9.8 %collective-permute-start.5 = (bf16[272,128]{1,0:T(8,128)(2,1)}, bf16[272,128]{1,0:T(8,128)(2,1)}, u32[]{:S(2)}, u32[]{:S(2)}) collective-permute-start(bf16[272,128]{1,0:T(8,128)(2,1)} %get-tuple-element.62), channel_id=1, source_target_pairs={{0,24},{4,28},{8,16},{12,20},{16,8},{20,12},{24,0},{28,4},{1,25},{... | collective-permute-start | bytes 208904 | tf_op jit(solution)/shard_map/ppermute | solution.py:46
  15.9 7.4 %collective-permute-start.6 = (bf16[272,128]{1,0:T(8,128)(2,1)}, bf16[272,128]{1,0:T(8,128)(2,1)}, u32[]{:S(2)}, u32[]{:S(2)}) collective-permute-start(bf16[272,128]{1,0:T(8,128)(2,1)} %get-tuple-element.63), channel_id=1, source_target_pairs={{0,28},{4,24},{8,20},{12,16},{16,12},{20,8},{24,4},{28,0},{1,29},{... | collective-permute-start | bytes 208904 | tf_op jit(solution)/shard_map/ppermute | solution.py:46
  19.7 8.4 %copy-start = (bf16[256,2,512]{2,1,0:T(2,128)(2,1)S(1)}, bf16[256,2,512]{2,1,0:T(2,128)(2,1)}, u32[]{:S(2)}) copy-start(bf16[256,2,512]{2,1,0:T(2,128)(2,1)} %param.17) | copy-start | bytes 1572868
  23.4 68.8 %all-to-all-start = ((bf16[8,64,2048]{2,1,0:T(8,128)(2,1)}), bf16[8,64,2048]{2,1,0:T(8,128)(2,1)}, u32[]{:S(2)}, u32[]{:S(2)}) async-start(bf16[8,64,2048]{2,1,0:T(8,128)(2,1)} %shard_map.114), calls=%async_computation | async-start | bytes 4194304 | tf_op jit(solution)/shard_map/all_to_all | solution.py:450
  31.6 1.6 %collective-permute-start.7 = (bf16[64,512]{1,0:T(8,128)(2,1)}, bf16[64,512]{1,0:T(8,128)(2,1)}, u32[]{:S(2)}, u32[]{:S(2)}) collective-permute-start(bf16[64,512]{1,0:T(8,128)(2,1)} %get-tuple-element.70), channel_id=1, source_target_pairs={{0,1},{1,0},{2,3},{3,2},{4,5},{5,4},{6,7},{7,6},{8,9},{9,8},{10,11... | collective-permute-start | bytes 196616 | tf_op jit(solution)/shard_map/ppermute | solution.py:46
  34.8 5.7 %collective-permute-start.8 = (bf16[64,512]{1,0:T(8,128)(2,1)}, bf16[64,512]{1,0:T(8,128)(2,1)}, u32[]{:S(2)}, u32[]{:S(2)}) collective-permute-start(bf16[64,512]{1,0:T(8,128)(2,1)} %get-tuple-element.72), channel_id=1, source_target_pairs={{0,2},{1,3},{2,0},{3,1},{4,6},{5,7},{6,4},{7,5},{8,10},{9,11},{10,... | collective-permute-start | bytes 196616 | tf_op jit(solution)/shard_map/ppermute | solution.py:46
  54.7 2.9 %collective-permute-start.9 = (bf16[2,512,512]{2,1,0:T(8,128)(2,1)}, bf16[2,512,512]{2,1,0:T(8,128)(2,1)S(1)}, u32[]{:S(2)}, u32[]{:S(2)}) collective-permute-start(bf16[2,512,512]{2,1,0:T(8,128)(2,1)} %get-tuple-element.75), channel_id=1, source_target_pairs={{0,1},{1,0},{2,3},{3,2},{4,5},{5,4},{6,7},{7,6},{8,9},{9,8},{10,11... | collective-permute-start | bytes 3145736 | tf_op jit(solution)/shard_map/ppermute | solution.py:46
  57.7 3.0 %copy-start.3 = (bf16[64,2048]{1,0:T(8,128)(2,1)S(1)}, bf16[64,2048]{1,0:T(8,128)(2,1)}, u32[]{:S(2)}) copy-start(bf16[64,2048]{1,0:T(8,128)(2,1)} %get-tuple-element.76) | copy-start | bytes 786436
  57.7 5.0 %copy-start.2 = (bf16[64,2048]{1,0:T(8,128)(2,1)S(1)}, bf16[64,2048]{1,0:T(8,128)(2,1)}, u32[]{:S(2)}) copy-start(bf16[64,2048]{1,0:T(8,128)(2,1)} %get-tuple-element.77) | copy-start | bytes 786436
  57.7 6.5 %copy-start.1 = (bf16[64,2048]{1,0:T(8,128)(2,1)S(1)}, bf16[64,2048]{1,0:T(8,128)(2,1)}, u32[]{:S(2)}) copy-start(bf16[64,2048]{1,0:T(8,128)(2,1)} %get-tuple-element.78) | copy-start | bytes 786436
  60.1 33.4 %collective-permute-start.10 = (bf16[512,512]{1,0:T(8,128)(2,1)S(1)}, bf16[512,512]{1,0:T(8,128)(2,1)}, u32[]{:S(2)}, u32[]{:S(2)}) collective-permute-start(bf16[512,512]{1,0:T(8,128)(2,1)S(1)} %get-tuple-element.108), channel_id=1, source_target_pairs={{0,2},{1,3},{2,0},{3,1},{4,6},{5,7},{6,4},{7,5},{8,10},{9,11},{10,... | collective-permute-start | bytes 1572872 | tf_op jit(solution)/shard_map/ppermute | solution.py:46
  60.6 12.6 %collective-permute-start.11 = (bf16[64,2048]{1,0:T(8,128)(2,1)S(1)}, bf16[64,2048]{1,0:T(8,128)(2,1)}, u32[]{:S(2)}, u32[]{:S(2)}) collective-permute-start(bf16[64,2048]{1,0:T(8,128)(2,1)S(1)} %copy-done.3), channel_id=1, source_target_pairs={{0,4},{4,0},{8,12},{12,8},{16,20},{20,16},{24,28},{28,24},{1,5},{5... | collective-permute-start | bytes 786440 | tf_op jit(solution)/shard_map/ppermute | solution.py:46
  62.7 29.5 %collective-permute-start.12 = (bf16[64,2048]{1,0:T(8,128)(2,1)S(1)}, bf16[64,2048]{1,0:T(8,128)(2,1)}, u32[]{:S(2)}, u32[]{:S(2)}) collective-permute-start(bf16[64,2048]{1,0:T(8,128)(2,1)S(1)} %copy-done.2), channel_id=1, source_target_pairs={{0,8},{4,12},{8,0},{12,4},{16,24},{20,28},{24,16},{28,20},{1,9},{5... | collective-permute-start | bytes 786440 | tf_op jit(solution)/shard_map/ppermute | solution.py:46
  64.1 28.1 %collective-permute-start.13 = (bf16[64,2048]{1,0:T(8,128)(2,1)S(1)}, bf16[64,2048]{1,0:T(8,128)(2,1)}, u32[]{:S(2)}, u32[]{:S(2)}) collective-permute-start(bf16[64,2048]{1,0:T(8,128)(2,1)S(1)} %copy-done.1), channel_id=1, source_target_pairs={{0,12},{4,8},{8,4},{12,0},{16,28},{20,24},{24,20},{28,16},{1,13},{... | collective-permute-start | bytes 786440 | tf_op jit(solution)/shard_map/ppermute | solution.py:46
  64.2 46.1 %collective-permute-start.16 = (bf16[64,2048]{1,0:T(8,128)(2,1)}, bf16[64,2048]{1,0:T(8,128)(2,1)}, u32[]{:S(2)}, u32[]{:S(2)}) collective-permute-start(bf16[64,2048]{1,0:T(8,128)(2,1)} %get-tuple-element.84), channel_id=1, source_target_pairs={{0,16},{4,20},{8,24},{12,28},{16,0},{20,4},{24,8},{28,12},{1,17},{... | collective-permute-start | bytes 786440 | tf_op jit(solution)/shard_map/ppermute | solution.py:46
  73.2 38.7 %collective-permute-start.17 = (bf16[64,2048]{1,0:T(8,128)(2,1)}, bf16[64,2048]{1,0:T(8,128)(2,1)}, u32[]{:S(2)}, u32[]{:S(2)}) collective-permute-start(bf16[64,2048]{1,0:T(8,128)(2,1)} %get-tuple-element.85), channel_id=1, source_target_pairs={{0,20},{4,16},{8,28},{12,24},{16,4},{20,0},{24,12},{28,8},{1,21},{... | collective-permute-start | bytes 786440 | tf_op jit(solution)/shard_map/ppermute | solution.py:46
  92.2 26.7 %collective-permute-start.18 = (bf16[64,2048]{1,0:T(8,128)(2,1)}, bf16[64,2048]{1,0:T(8,128)(2,1)}, u32[]{:S(2)}, u32[]{:S(2)}) collective-permute-start(bf16[64,2048]{1,0:T(8,128)(2,1)} %get-tuple-element.87), channel_id=1, source_target_pairs={{0,24},{4,28},{8,16},{12,20},{16,8},{20,12},{24,0},{28,4},{1,25},{... | collective-permute-start | bytes 786440 | tf_op jit(solution)/shard_map/ppermute | solution.py:46
  92.2 27.8 %collective-permute-start.19 = (bf16[64,2048]{1,0:T(8,128)(2,1)}, bf16[64,2048]{1,0:T(8,128)(2,1)}, u32[]{:S(2)}, u32[]{:S(2)}) collective-permute-start(bf16[64,2048]{1,0:T(8,128)(2,1)} %get-tuple-element.89), channel_id=1, source_target_pairs={{0,28},{4,24},{8,20},{12,16},{16,12},{20,8},{24,4},{28,0},{1,29},{... | collective-permute-start | bytes 786440 | tf_op jit(solution)/shard_map/ppermute | solution.py:46
  97.7 1.6 %collective-permute-start.14 = (bf16[64,512]{1,0:T(8,128)(2,1)}, bf16[64,512]{1,0:T(8,128)(2,1)}, u32[]{:S(2)}, u32[]{:S(2)}) collective-permute-start(bf16[64,512]{1,0:T(8,128)(2,1)} %get-tuple-element.80), channel_id=1, source_target_pairs={{0,1},{1,0},{2,3},{3,2},{4,5},{5,4},{6,7},{7,6},{8,9},{9,8},{10,11... | collective-permute-start | bytes 196616 | tf_op jit(solution)/shard_map/ppermute | solution.py:46
  100.9 4.6 %collective-permute-start.15 = (bf16[64,512]{1,0:T(8,128)(2,1)}, bf16[64,512]{1,0:T(8,128)(2,1)}, u32[]{:S(2)}, u32[]{:S(2)}) collective-permute-start(bf16[64,512]{1,0:T(8,128)(2,1)} %get-tuple-element.82), channel_id=1, source_target_pairs={{0,2},{1,3},{2,0},{3,1},{4,6},{5,7},{6,4},{7,5},{8,10},{9,11},{10,... | collective-permute-start | bytes 196616 | tf_op jit(solution)/shard_map/ppermute | solution.py:46
  114.2 13.4 %collective-permute-start.24 = (bf16[64,512]{1,0:T(8,128)(2,1)}, bf16[64,512]{1,0:T(8,128)(2,1)}, u32[]{:S(2)}, u32[]{:S(2)}) collective-permute-start(bf16[64,512]{1,0:T(8,128)(2,1)} %get-tuple-element.101), channel_id=1, source_target_pairs={{0,20},{4,16},{8,28},{12,24},{16,4},{20,0},{24,12},{28,8},{1,21},{... | collective-permute-start | bytes 196616 | tf_op jit(solution)/shard_map/ppermute | solution.py:46
  114.2 14.4 %collective-permute-start.23 = (bf16[64,512]{1,0:T(8,128)(2,1)}, bf16[64,512]{1,0:T(8,128)(2,1)}, u32[]{:S(2)}, u32[]{:S(2)}) collective-permute-start(bf16[64,512]{1,0:T(8,128)(2,1)} %get-tuple-element.99), channel_id=1, source_target_pairs={{0,16},{4,20},{8,24},{12,28},{16,0},{20,4},{24,8},{28,12},{1,17},{... | collective-permute-start | bytes 196616 | tf_op jit(solution)/shard_map/ppermute | solution.py:46
  118.9 16.0 %collective-permute-start.22 = (bf16[64,512]{1,0:T(8,128)(2,1)}, bf16[64,512]{1,0:T(8,128)(2,1)}, u32[]{:S(2)}, u32[]{:S(2)}) collective-permute-start(bf16[64,512]{1,0:T(8,128)(2,1)} %get-tuple-element.97), channel_id=1, source_target_pairs={{0,12},{4,8},{8,4},{12,0},{16,28},{20,24},{24,20},{28,16},{1,13},{... | collective-permute-start | bytes 196616 | tf_op jit(solution)/shard_map/ppermute | solution.py:46
  118.9 16.0 %collective-permute-start.21 = (bf16[64,512]{1,0:T(8,128)(2,1)}, bf16[64,512]{1,0:T(8,128)(2,1)}, u32[]{:S(2)}, u32[]{:S(2)}) collective-permute-start(bf16[64,512]{1,0:T(8,128)(2,1)} %get-tuple-element.95), channel_id=1, source_target_pairs={{0,8},{4,12},{8,0},{12,4},{16,24},{20,28},{24,16},{28,20},{1,9},{5... | collective-permute-start | bytes 196616 | tf_op jit(solution)/shard_map/ppermute | solution.py:46
  120.1 14.9 %collective-permute-start.20 = (bf16[64,512]{1,0:T(8,128)(2,1)}, bf16[64,512]{1,0:T(8,128)(2,1)}, u32[]{:S(2)}, u32[]{:S(2)}) collective-permute-start(bf16[64,512]{1,0:T(8,128)(2,1)} %get-tuple-element.93), channel_id=1, source_target_pairs={{0,4},{4,0},{8,12},{12,8},{16,20},{20,16},{24,28},{28,24},{1,5},{5... | collective-permute-start | bytes 196616 | tf_op jit(solution)/shard_map/ppermute | solution.py:46
  127.6 7.6 %collective-permute-start.26 = (bf16[64,512]{1,0:T(8,128)(2,1)}, bf16[64,512]{1,0:T(8,128)(2,1)}, u32[]{:S(2)}, u32[]{:S(2)}) collective-permute-start(bf16[64,512]{1,0:T(8,128)(2,1)} %get-tuple-element.105), channel_id=1, source_target_pairs={{0,28},{4,24},{8,20},{12,16},{16,12},{20,8},{24,4},{28,0},{1,29},{... | collective-permute-start | bytes 196616 | tf_op jit(solution)/shard_map/ppermute | solution.py:46
  128.6 6.6 %collective-permute-start.25 = (bf16[64,512]{1,0:T(8,128)(2,1)}, bf16[64,512]{1,0:T(8,128)(2,1)}, u32[]{:S(2)}, u32[]{:S(2)}) collective-permute-start(bf16[64,512]{1,0:T(8,128)(2,1)} %get-tuple-element.103), channel_id=1, source_target_pairs={{0,24},{4,28},{8,16},{12,20},{16,8},{20,12},{24,0},{28,4},{1,25},{... | collective-permute-start | bytes 196616 | tf_op jit(solution)/shard_map/ppermute | solution.py:46

commit v5 on v4

--- a/solution.py
+++ b/solution.py
@@ -383,15 +383,20 @@
     count = len(blocks)
 
     def kernel(*refs):
-        gst, trp = refs[:2]
+        tables = refs[:2]
         ins = refs[2 : 2 + count]
-        out, held, acc, sem_in, sem_out = refs[-5:]
+        out, held, acc, gst, trp, sem_in, sem_out, sem = refs[-8:]
+        loads = [pltpu.make_async_copy(a, b, sem.at[i]) for i, (a, b) in enumerate(zip(tables, (gst, trp)))]
+        for c in loads:
+            c.start()
         me = lax.axis_index("dp")
         copies = []
         for k in range(groups):
             source = ins[k] if count > 1 else ins[0].at[me ^ k]
             copies.append(pltpu.make_async_copy(source, held.at[k], sem_in.at[k]))
             copies[-1].start()
+        for c in loads:
+            c.wait()
         rows = [stored_row(gst, trp, tasks, k) for k in range(groups)]
         back = [
             pltpu.make_async_copy(held.at[g], out.at[rows[g]], sem_out.at[g])
@@ -432,13 +437,16 @@
     return pl.pallas_call(
         kernel,
         out_shape=shaped(filled.shape, bf),
-        in_specs=[SMEM, SMEM] + [ANY] * (count + 1 + len(after)),
+        in_specs=[ANY] * (count + 3 + len(after)),
         out_specs=ANY,
         scratch_shapes=[
             pltpu.VMEM((groups, rank, width), bf),
             pltpu.VMEM((rank, width), f32),
+            pltpu.SMEM(gst.shape, jnp.int32),
+            pltpu.SMEM(trp.shape, jnp.int32),
             pltpu.SemaphoreType.DMA((groups,)),
             pltpu.SemaphoreType.DMA((groups,)),
+            pltpu.SemaphoreType.DMA((2,)),
         ],
         input_output_aliases={2 + count: 0},
         compiler_params=pltpu.CompilerParams(vmem_limit_bytes=big),

time: 139 us -> 138 us (level)
  Pallas kernels: 41.5 us -> 40.1 us
    pallas_call x2, Pallas kernels: 5.78 us -> 4.38 us  [combine(): pl.pallas_call(kernel, out_shape=shaped(filled.shape, bf), in_specs=[ANY]...]
where the time goes in v5:
time: 138 us; the launch traced here: 137 us
  starting transfers between devices  48.9 us (35%)
  Pallas kernels  40.1 us (29%)
  waiting for transfers between devices  37.7 us (27%)
  local copies, waits for them, and re-layouts  8.07 us (6%)
  other arithmetic  1.6 us (1%)
    ppermute x27, starting transfers between devices, swap(): return lax.ppermute(x, axis, [(i, i ^ k) for i in range(n)])  44.2 us
    ppermute x27, waiting for transfers between devices, swap(): return lax.ppermute(x, axis, [(i, i ^ k) for i in range(n)])  27 us
    pallas_call x9, Pallas kernels, call(): pl.pallas_call(run, out_shape=list(outs), in_specs=list(specs) + [ANY] *...  25.9 us
    all_to_all x1, waiting for transfers between devices, exchange(): return lax.all_to_all(x, 'dp', split_axis=0, concat_axis=0, tiled=True)  10.7 us
    pallas_call x1, Pallas kernels, base_parts(): pl.pallas_call(kernel, out_shape=[shaped((half, n, cols), bf)] * 2 + [sha...  9.83 us
    all_to_all x1, starting transfers between devices, exchange(): return lax.all_to_all(x, 'dp', split_axis=0, concat_axis=0, tiled=True)  4.67 us
    pallas_call x2, Pallas kernels, combine(): pl.pallas_call(kernel, out_shape=shaped(filled.shape, bf), in_specs=[ANY]...  4.38 us
    reshape x1, local copies, waits for them, and re-layouts, body(): rows = hidden.reshape(n, width)  4.13 us
  transfers between devices with their start and end apart: 28, of which 11 were waited for; matrix products, arithmetic and copies ran while one was open for 7% of the time, Pallas kernels for 26%

profile of v5, /device:TPU:0, one launch (start us, length us, event | category | flops | bytes accessed | tf_op | source)
XLA Modules:
  0.0 137.1 jit_solution(13052157995431017034)
XLA Ops:
  0.6 2.8 %shard_map.112 = (bf16[272,128]{1,0:T(8,128)(2,1)}, bf16[272,128]{1,0:T(8,128)(2,1)}, bf16[272,128]{1,0:T(8,128)(2,1)}, bf16[272,128]{1,0:T(8,128)(2,1)}, bf16[2...) custom-call(s32[8,8]{1,0:T(8,128)} %refs_0_.9, ...), custom_call_target="tpu_custom_call" | custom-call | tf_op jit(solution)/shard_map/pallas_call | solution.py:33
  3.5 3.0 %collective-permute-start = (bf16[272,128]{1,0:T(8,128)(2,1)}, bf16[272,128]{1,0:T(8,128)(2,1)}, u32[]{:S(2)}, u32[]{:S(2)}) collective-permute-start(bf16[272,128]{1,0:T(8,128)(2,1)} %get-tuple-element.57), channel_id=1, source_target_pairs={{0,4},{4,0},{8,12},{12,8},{16,20},{20,16},{24,28},{28,24},{1,5},{5... | collective-permute-start | bytes 208904 | tf_op jit(solution)/shard_map/ppermute | solution.py:46
  8.1 3.0 %collective-permute-start.3 = (bf16[272,128]{1,0:T(8,128)(2,1)}, bf16[272,128]{1,0:T(8,128)(2,1)}, u32[]{:S(2)}, u32[]{:S(2)}) collective-permute-start(bf16[272,128]{1,0:T(8,128)(2,1)} %get-tuple-element.60), channel_id=1, source_target_pairs={{0,16},{4,20},{8,24},{12,28},{16,0},{20,4},{24,8},{28,12},{1,17},{... | collective-permute-start | bytes 208904 | tf_op jit(solution)/shard_map/ppermute | solution.py:46
  12.3 3.6 %collective-permute-start.5 = (bf16[272,128]{1,0:T(8,128)(2,1)}, bf16[272,128]{1,0:T(8,128)(2,1)}, u32[]{:S(2)}, u32[]{:S(2)}) collective-permute-start(bf16[272,128]{1,0:T(8,128)(2,1)} %get-tuple-element.62), channel_id=1, source_target_pairs={{0,24},{4,28},{8,16},{12,20},{16,8},{20,12},{24,0},{28,4},{1,25},{... | collective-permute-start | bytes 208904 | tf_op jit(solution)/shard_map/ppermute | solution.py:46
  16.0 3.7 %shard_map.114 = bf16[8,64,2048]{2,1,0:T(8,128)(2,1)} custom-call(s32[8,8]{1,0:T(8,128)} %refs_0_.9, s32[128]{0:T(128)} %refs_1_.7, bf16[16,64,2048]{2,1,0:T(8,128)(2,1)} %bitcast.10, bf16[272,128]{1,0:T(8,128)(2,1)} %get-tuple-element.55.refs_3_.refs_7_.refs_5_), custom_call_target="tpu_custom_call" | custom-call | tf_op jit(solution)/shard_map/pallas_call | solution.py:33
  19.7 2.4 %collective-permute-done.4.refs_8_.refs_12_.refs_10_ = bf16[272,128]{1,0:T(8,128)(2,1)} collective-permute-done((bf16[272,128]{1,0:T(8,128)(2,1)}, bf16[272,128]{1,0:T(8,128)(2,1)}, u32[]{:S(2)}, u32[]{:S(2)}) %collective-permute-start.4) | collective-permute-done | bytes 69664 | tf_op jit(solution)/shard_map/ppermute | solution.py:46
  23.4 4.7 %all-to-all-start = ((bf16[8,64,2048]{2,1,0:T(8,128)(2,1)}), bf16[8,64,2048]{2,1,0:T(8,128)(2,1)}, u32[]{:S(2)}, u32[]{:S(2)}) async-start(bf16[8,64,2048]{2,1,0:T(8,128)(2,1)} %shard_map.114), calls=%async_computation | async-start | bytes 4194304 | tf_op jit(solution)/shard_map/all_to_all | solution.py:458
  29.1 2.5 %shard_map.113 = (f32[64,512]{1,0:T(8,128)}, bf16[64,512]{1,0:T(8,128)(2,1)}, s32[1,512]{1,0:T(1,128)}, s32[1,512]{1,0:T(1,128)}, f32[1,512]{1,0:T(1,128)}) custom-call(s32[1,256]{1,0:T(1,128)} %bitcast.12, s32[1,256]{1,0:T(1,128)} %bitcast.14, bf16[512,512]{1,0:T(8,128)(2,1)} %reshape.32.refs_2_.refs_4_, ...), custom_call_target="tpu_custom_call" | custom-call | tf_op jit(solution)/shard_map/pallas_call | solution.py:33
  33.2 1.6 %shard_map.115 = (f32[64,512]{1,0:T(8,128)}, bf16[64,512]{1,0:T(8,128)(2,1)}) custom-call(f32[64,512]{1,0:T(8,128)} %get-tuple-element.69.refs_0_, bf16[64,512]{1,0:T(8,128)(2,1)} %collective-permute-done.7.refs_1_), custom_call_target="tpu_custom_call" | custom-call | tf_op jit(solution)/shard_map/pallas_call | solution.py:33
  36.3 4.1 %reshape.33.refs_6_.rows.refs_1_ = bf16[512,2048]{1,0:T(8,128)(2,1)} reshape(bf16[256,2,2048]{2,1,0:T(2,128)(2,1)} %param.9) | data formatting | bytes 4194304 | tf_op jit(solution)/shard_map/reshape | solution.py:485
  40.4 4.5 %shard_map.116 = (f32[1,512]{1,0:T(1,128)}, bf16[64,2048]{1,0:T(8,128)(2,1)}, bf16[64,2048]{1,0:T(8,128)(2,1)}, bf16[64,2048]{1,0:T(8,128)(2,1)}, bf16[64,2048]{...) custom-call(s32[8,8]{1,0:T(8,128)} %refs_0_.9, ...), custom_call_target="tpu_custom_call" | custom-call | tf_op jit(solution)/shard_map/pallas_call | solution.py:33
  44.9 9.8 %shard_map.117 = (bf16[2,512,512]{2,1,0:T(8,128)(2,1)}, bf16[2,512,512]{2,1,0:T(8,128)(2,1)}, bf16[16,64,2048]{2,1,0:T(8,128)(2,1)}, bf16[16,64,512]{2,1,0:T(8,128)(2,1)}) custom-call(s32[1]{0:T(128)} %bitcast.3.mine, bf16[512,2048]{1,0:T(8,128)(2,1)} %reshape.33.refs_6_.rows.refs_1_, bf16[2048,2048]{1,0:T(8,128)(2,1)} %weight.1, ...), custom_call_target="tpu_custom_call" | custom-call | tf_op jit(solution)/shard_map/pallas_call | solution.py:170
  54.8 2.9 %collective-permute-done.9 = bf16[2,512,512]{2,1,0:T(8,128)(2,1)S(1)} collective-permute-done((bf16[2,512,512]{2,1,0:T(8,128)(2,1)}, bf16[2,512,512]{2,1,0:T(8,128)(2,1)S(1)}, u32[]{:S(2)}, u32[]{:S(2)}) %collective-permute-start.9) | collective-permute-done | bytes 1048608 | tf_op jit(solution)/shard_map/ppermute | solution.py:46
  57.7 1.6 %add_convert_fusion = bf16[2,512,512]{2,1,0:T(8,128)(2,1)S(1)} fusion(bf16[2,512,512]{2,1,0:T(8,128)(2,1)S(1)} %collective-permute-done.9, bf16[2,512,512]{2,1,0:T(8,128)(2,1)} %get-tuple-element.74), kind=kLoop, calls=%fused_computation | loop fusion | flops 2097152 | bytes 3145728 | tf_op jit(solution)/shard_map/convert_element_type | solution.py:506
  60.6 2.0 %collective-permute-start.11 = (bf16[64,2048]{1,0:T(8,128)(2,1)S(1)}, bf16[64,2048]{1,0:T(8,128)(2,1)}, u32[]{:S(2)}, u32[]{:S(2)}) collective-permute-start(bf16[64,2048]{1,0:T(8,128)(2,1)S(1)} %copy-done.3), channel_id=1, source_target_pairs={{0,4},{4,0},{8,12},{12,8},{16,20},{20,16},{24,28},{28,24},{1,5},{5... | collective-permute-start | bytes 786440 | tf_op jit(solution)/shard_map/ppermute | solution.py:46
  64.2 3.0 %collective-permute-start.16 = (bf16[64,2048]{1,0:T(8,128)(2,1)}, bf16[64,2048]{1,0:T(8,128)(2,1)}, u32[]{:S(2)}, u32[]{:S(2)}) collective-permute-start(bf16[64,2048]{1,0:T(8,128)(2,1)} %get-tuple-element.84), channel_id=1, source_target_pairs={{0,16},{4,20},{8,24},{12,28},{16,0},{20,4},{24,8},{28,12},{1,17},{... | collective-permute-start | bytes 786440 | tf_op jit(solution)/shard_map/ppermute | solution.py:46
  67.2 6.1 %collective-permute-done.11.refs_4_.refs_3_ = bf16[64,2048]{1,0:T(8,128)(2,1)} collective-permute-done((bf16[64,2048]{1,0:T(8,128)(2,1)S(1)}, bf16[64,2048]{1,0:T(8,128)(2,1)}, u32[]{:S(2)}, u32[]{:S(2)}) %collective-permute-start.11) | collective-permute-done | bytes 262176 | tf_op jit(solution)/shard_map/ppermute | solution.py:46
  73.3 8.2 %collective-permute-start.17 = (bf16[64,2048]{1,0:T(8,128)(2,1)}, bf16[64,2048]{1,0:T(8,128)(2,1)}, u32[]{:S(2)}, u32[]{:S(2)}) collective-permute-start(bf16[64,2048]{1,0:T(8,128)(2,1)} %get-tuple-element.85), channel_id=1, source_target_pairs={{0,20},{4,16},{8,28},{12,24},{16,4},{20,0},{24,12},{28,8},{1,21},{... | collective-permute-start | bytes 786440 | tf_op jit(solution)/shard_map/ppermute | solution.py:46
  81.5 10.7 %all-to-all-done.refs_2_ = bf16[8,64,2048]{2,1,0:T(8,128)(2,1)} async-done(((bf16[8,64,2048]{2,1,0:T(8,128)(2,1)}), bf16[8,64,2048]{2,1,0:T(8,128)(2,1)}, u32[]{:S(2)}, u32[]{:S(2)}) %all-to-all-start) | async-done | bytes 2097184 | tf_op jit(solution)/shard_map/all_to_all | solution.py:458
  93.3 4.2 %shard_map.118 = (f32[64,512]{1,0:T(8,128)}, bf16[64,512]{1,0:T(8,128)(2,1)}) custom-call(s32[1,512]{1,0:T(1,128)} %get-tuple-element.65.refs_2_.refs_0_, bf16[512,2048]{1,0:T(8,128)(2,1)} %reshape.33.refs_6_.rows.refs_1_, bf16[8,64,2048]{2,1,0:T(8,128)(2,1)} %all-to-all-done.refs_2_, bf16[512,512]{1,0:T(8,128)(2,1)} %collective-permute-done.10.refs_3_.refs_4_, ...), custom_call_target="tpu_custom_call" | custom-call | tf_op jit(solution)/shard_map/pallas_call | solution.py:33
  97.5 1.6 %collective-permute-done.14.refs_1_ = bf16[64,512]{1,0:T(8,128)(2,1)} collective-permute-done((bf16[64,512]{1,0:T(8,128)(2,1)}, bf16[64,512]{1,0:T(8,128)(2,1)}, u32[]{:S(2)}, u32[]{:S(2)}) %collective-permute-start.14) | collective-permute-done | bytes 65568 | tf_op jit(solution)/shard_map/ppermute | solution.py:46
  102.2 3.1 %collective-permute-done.15.refs_2_.refs_3_ = bf16[64,512]{1,0:T(8,128)(2,1)} collective-permute-done((bf16[64,512]{1,0:T(8,128)(2,1)}, bf16[64,512]{1,0:T(8,128)(2,1)}, u32[]{:S(2)}, u32[]{:S(2)}) %collective-permute-start.15) | collective-permute-done | bytes 65568 | tf_op jit(solution)/shard_map/ppermute | solution.py:46
  105.3 2.8 %shard_map.120 = bf16[512,512]{1,0:T(8,128)(2,1)} custom-call(s32[1,512]{1,0:T(1,128)} %get-tuple-element.64.refs_1_.refs_0_, f32[64,512]{1,0:T(8,128)} %get-tuple-element.81.refs_1_.refs_2_, bf16[64,512]{1,0:T(8,128)(2,1)} %collective-permute-done.15.refs_2_.refs_3_, bf16[512,512]{1,0:T(8,128)(2,1)} %get-tuple-element.107.refs_3_, ...), custom_call_target="tpu_custom_call" | custom-call | tf_op jit(solution)/shard_map/pallas_call | solution.py:33
  108.1 2.0 %reshape.37.refs_5_ = bf16[256,2,512]{2,1,0:T(2,128)(2,1)} reshape(bf16[512,512]{1,0:T(8,128)(2,1)} %shard_map.120) | data formatting | bytes 1048576 | tf_op jit(solution)/shard_map/reshape | solution.py:514
  110.1 1.8 %collective-permute-done.17.refs_7_ = bf16[64,2048]{1,0:T(8,128)(2,1)} collective-permute-done((bf16[64,2048]{1,0:T(8,128)(2,1)}, bf16[64,2048]{1,0:T(8,128)(2,1)}, u32[]{:S(2)}, u32[]{:S(2)}) %collective-permute-start.17) | collective-permute-done | bytes 262176 | tf_op jit(solution)/shard_map/ppermute | solution.py:46
  111.9 2.3 %shard_map.122 = (bf16[64,512]{1,0:T(8,128)(2,1)}, bf16[64,512]{1,0:T(8,128)(2,1)}, bf16[64,512]{1,0:T(8,128)(2,1)}, bf16[64,512]{1,0:T(8,128)(2,1)}, bf16[64,51...) custom-call(s32[1,512]{1,0:T(1,128)} %get-tuple-element.64.refs_1_.refs_0_, ...), custom_call_target="tpu_custom_call" | custom-call | tf_op jit(solution)/shard_map/pallas_call | solution.py:33
  114.2 4.7 %collective-permute-start.23 = (bf16[64,512]{1,0:T(8,128)(2,1)}, bf16[64,512]{1,0:T(8,128)(2,1)}, u32[]{:S(2)}, u32[]{:S(2)}) collective-permute-start(bf16[64,512]{1,0:T(8,128)(2,1)} %get-tuple-element.99), channel_id=1, source_target_pairs={{0,16},{4,20},{8,24},{12,28},{16,0},{20,4},{24,8},{28,12},{1,17},{... | collective-permute-start | bytes 196616 | tf_op jit(solution)/shard_map/ppermute | solution.py:46
  120.1 2.3 %collective-permute-start.20 = (bf16[64,512]{1,0:T(8,128)(2,1)}, bf16[64,512]{1,0:T(8,128)(2,1)}, u32[]{:S(2)}, u32[]{:S(2)}) collective-permute-start(bf16[64,512]{1,0:T(8,128)(2,1)} %get-tuple-element.93), channel_id=1, source_target_pairs={{0,4},{4,0},{8,12},{12,8},{16,20},{20,16},{24,28},{28,24},{1,5},{5... | collective-permute-start | bytes 196616 | tf_op jit(solution)/shard_map/ppermute | solution.py:46
  122.4 5.2 %collective-permute-done.24.refs_7_ = bf16[64,512]{1,0:T(8,128)(2,1)} collective-permute-done((bf16[64,512]{1,0:T(8,128)(2,1)}, bf16[64,512]{1,0:T(8,128)(2,1)}, u32[]{:S(2)}, u32[]{:S(2)}) %collective-permute-start.24) | collective-permute-done | bytes 65568 | tf_op jit(solution)/shard_map/ppermute | solution.py:46
  128.7 3.0 %collective-permute-start.25 = (bf16[64,512]{1,0:T(8,128)(2,1)}, bf16[64,512]{1,0:T(8,128)(2,1)}, u32[]{:S(2)}, u32[]{:S(2)}) collective-permute-start(bf16[64,512]{1,0:T(8,128)(2,1)} %get-tuple-element.103), channel_id=1, source_target_pairs={{0,24},{4,28},{8,16},{12,20},{16,8},{20,12},{24,0},{28,4},{1,25},{... | collective-permute-start | bytes 196616 | tf_op jit(solution)/shard_map/ppermute | solution.py:46
  131.7 2.5 %shard_map.121.refs_11_ = bf16[16,64,2048]{2,1,0:T(8,128)(2,1)} custom-call(s32[8,8]{1,0:T(8,128)} %refs_0_.9, s32[128]{0:T(128)} %refs_1_.7, bf16[64,2048]{1,0:T(8,128)(2,1)} %get-tuple-element.83.refs_2_, bf16[64,2048]{1,0:T(8,128)(2,1)} %collective-permute-done.11.refs_4_.refs_3_, ...), custom_call_target="tpu_custom_call", output_to_operand_aliasing={{}: (10, {})} | custom-call | tf_op jit(solution)/shard_map/pallas_call | solution.py:437
  135.2 1.9 %shard_map.123 = bf16[16,64,512]{2,1,0:T(8,128)(2,1)} custom-call(s32[8,8]{1,0:T(8,128)} %refs_0_.9, s32[128]{0:T(128)} %refs_1_.7, bf16[64,512]{1,0:T(8,128)(2,1)} %get-tuple-element.91.refs_2_, bf16[64,512]{1,0:T(8,128)(2,1)} %collective-permute-done.20.refs_3_, bf16[64,512]{1,0:T(8,128)(2,1)} %collective-permute-done.21.refs_4_, ...), custom_call_target="tpu_custom_call", output_to_operand_aliasing={{}: (10, {})} | custom-call | tf_op jit(solution)/shard_map/pallas_call | solution.py:437
  (49 shorter events, 18.7 us)
Async XLA Ops:
  3.5 8.9 %collective-permute-start = (bf16[272,128]{1,0:T(8,128)(2,1)}, bf16[272,128]{1,0:T(8,128)(2,1)}, u32[]{:S(2)}, u32[]{:S(2)}) collective-permute-start(bf16[272,128]{1,0:T(8,128)(2,1)} %get-tuple-element.57), channel_id=1, source_target_pairs={{0,4},{4,0},{8,12},{12,8},{16,20},{20,16},{24,28},{28,24},{1,5},{5... | collective-permute-start | bytes 208904 | tf_op jit(solution)/shard_map/ppermute | solution.py:46
  6.5 9.5 %collective-permute-start.1 = (bf16[272,128]{1,0:T(8,128)(2,1)}, bf16[272,128]{1,0:T(8,128)(2,1)}, u32[]{:S(2)}, u32[]{:S(2)}) collective-permute-start(bf16[272,128]{1,0:T(8,128)(2,1)} %get-tuple-element.58), channel_id=1, source_target_pairs={{0,8},{4,12},{8,0},{12,4},{16,24},{20,28},{24,16},{28,20},{1,9},{5... | collective-permute-start | bytes 208904 | tf_op jit(solution)/shard_map/ppermute | solution.py:46
  8.1 11.6 %collective-permute-start.2 = (bf16[272,128]{1,0:T(8,128)(2,1)}, bf16[272,128]{1,0:T(8,128)(2,1)}, u32[]{:S(2)}, u32[]{:S(2)}) collective-permute-start(bf16[272,128]{1,0:T(8,128)(2,1)} %get-tuple-element.59), channel_id=1, source_target_pairs={{0,12},{4,8},{8,4},{12,0},{16,28},{20,24},{24,20},{28,16},{1,13},{... | collective-permute-start | bytes 208904 | tf_op jit(solution)/shard_map/ppermute | solution.py:46
  8.1 11.6 %collective-permute-start.3 = (bf16[272,128]{1,0:T(8,128)(2,1)}, bf16[272,128]{1,0:T(8,128)(2,1)}, u32[]{:S(2)}, u32[]{:S(2)}) collective-permute-start(bf16[272,128]{1,0:T(8,128)(2,1)} %get-tuple-element.60), channel_id=1, source_target_pairs={{0,16},{4,20},{8,24},{12,28},{16,0},{20,4},{24,8},{28,12},{1,17},{... | collective-permute-start | bytes 208904 | tf_op jit(solution)/shard_map/ppermute | solution.py:46
  11.1 11.0 %collective-permute-start.4 = (bf16[272,128]{1,0:T(8,128)(2,1)}, bf16[272,128]{1,0:T(8,128)(2,1)}, u32[]{:S(2)}, u32[]{:S(2)}) collective-permute-start(bf16[272,128]{1,0:T(8,128)(2,1)} %get-tuple-element.61), channel_id=1, source_target_pairs={{0,20},{4,16},{8,28},{12,24},{16,4},{20,0},{24,12},{28,8},{1,21},{... | collective-permute-start | bytes 208904 | tf_op jit(solution)/shard_map/ppermute | solution.py:46
  12.3 9.8 %collective-permute-start.5 = (bf16[272,128]{1,0:T(8,128)(2,1)}, bf16[272,128]{1,0:T(8,128)(2,1)}, u32[]{:S(2)}, u32[]{:S(2)}) collective-permute-start(bf16[272,128]{1,0:T(8,128)(2,1)} %get-tuple-element.62), channel_id=1, source_target_pairs={{0,24},{4,28},{8,16},{12,20},{16,8},{20,12},{24,0},{28,4},{1,25},{... | collective-permute-start | bytes 208904 | tf_op jit(solution)/shard_map/ppermute | solution.py:46
  16.0 7.4 %collective-permute-start.6 = (bf16[272,128]{1,0:T(8,128)(2,1)}, bf16[272,128]{1,0:T(8,128)(2,1)}, u32[]{:S(2)}, u32[]{:S(2)}) collective-permute-start(bf16[272,128]{1,0:T(8,128)(2,1)} %get-tuple-element.63), channel_id=1, source_target_pairs={{0,28},{4,24},{8,20},{12,16},{16,12},{20,8},{24,4},{28,0},{1,29},{... | collective-permute-start | bytes 208904 | tf_op jit(solution)/shard_map/ppermute | solution.py:46
  19.7 8.4 %copy-start = (bf16[256,2,512]{2,1,0:T(2,128)(2,1)S(1)}, bf16[256,2,512]{2,1,0:T(2,128)(2,1)}, u32[]{:S(2)}) copy-start(bf16[256,2,512]{2,1,0:T(2,128)(2,1)} %param.17) | copy-start | bytes 1572868
  23.4 68.8 %all-to-all-start = ((bf16[8,64,2048]{2,1,0:T(8,128)(2,1)}), bf16[8,64,2048]{2,1,0:T(8,128)(2,1)}, u32[]{:S(2)}, u32[]{:S(2)}) async-start(bf16[8,64,2048]{2,1,0:T(8,128)(2,1)} %shard_map.114), calls=%async_computation | async-start | bytes 4194304 | tf_op jit(solution)/shard_map/all_to_all | solution.py:458
  31.6 1.6 %collective-permute-start.7 = (bf16[64,512]{1,0:T(8,128)(2,1)}, bf16[64,512]{1,0:T(8,128)(2,1)}, u32[]{:S(2)}, u32[]{:S(2)}) collective-permute-start(bf16[64,512]{1,0:T(8,128)(2,1)} %get-tuple-element.70), channel_id=1, source_target_pairs={{0,1},{1,0},{2,3},{3,2},{4,5},{5,4},{6,7},{7,6},{8,9},{9,8},{10,11... | collective-permute-start | bytes 196616 | tf_op jit(solution)/shard_map/ppermute | solution.py:46
  34.8 5.7 %collective-permute-start.8 = (bf16[64,512]{1,0:T(8,128)(2,1)}, bf16[64,512]{1,0:T(8,128)(2,1)}, u32[]{:S(2)}, u32[]{:S(2)}) collective-permute-start(bf16[64,512]{1,0:T(8,128)(2,1)} %get-tuple-element.72), channel_id=1, source_target_pairs={{0,2},{1,3},{2,0},{3,1},{4,6},{5,7},{6,4},{7,5},{8,10},{9,11},{10,... | collective-permute-start | bytes 196616 | tf_op jit(solution)/shard_map/ppermute | solution.py:46
  54.7 2.9 %collective-permute-start.9 = (bf16[2,512,512]{2,1,0:T(8,128)(2,1)}, bf16[2,512,512]{2,1,0:T(8,128)(2,1)S(1)}, u32[]{:S(2)}, u32[]{:S(2)}) collective-permute-start(bf16[2,512,512]{2,1,0:T(8,128)(2,1)} %get-tuple-element.75), channel_id=1, source_target_pairs={{0,1},{1,0},{2,3},{3,2},{4,5},{5,4},{6,7},{7,6},{8,9},{9,8},{10,11... | collective-permute-start | bytes 3145736 | tf_op jit(solution)/shard_map/ppermute | solution.py:46
  57.7 3.0 %copy-start.3 = (bf16[64,2048]{1,0:T(8,128)(2,1)S(1)}, bf16[64,2048]{1,0:T(8,128)(2,1)}, u32[]{:S(2)}) copy-start(bf16[64,2048]{1,0:T(8,128)(2,1)} %get-tuple-element.76) | copy-start | bytes 786436
  57.7 5.0 %copy-start.2 = (bf16[64,2048]{1,0:T(8,128)(2,1)S(1)}, bf16[64,2048]{1,0:T(8,128)(2,1)}, u32[]{:S(2)}) copy-start(bf16[64,2048]{1,0:T(8,128)(2,1)} %get-tuple-element.77) | copy-start | bytes 786436
  57.7 6.5 %copy-start.1 = (bf16[64,2048]{1,0:T(8,128)(2,1)S(1)}, bf16[64,2048]{1,0:T(8,128)(2,1)}, u32[]{:S(2)}) copy-start(bf16[64,2048]{1,0:T(8,128)(2,1)} %get-tuple-element.78) | copy-start | bytes 786436
  60.1 33.2 %collective-permute-start.10 = (bf16[512,512]{1,0:T(8,128)(2,1)S(1)}, bf16[512,512]{1,0:T(8,128)(2,1)}, u32[]{:S(2)}, u32[]{:S(2)}) collective-permute-start(bf16[512,512]{1,0:T(8,128)(2,1)S(1)} %get-tuple-element.108), channel_id=1, source_target_pairs={{0,2},{1,3},{2,0},{3,1},{4,6},{5,7},{6,4},{7,5},{8,10},{9,11},{10,... | collective-permute-start | bytes 1572872 | tf_op jit(solution)/shard_map/ppermute | solution.py:46
  60.6 12.6 %collective-permute-start.11 = (bf16[64,2048]{1,0:T(8,128)(2,1)S(1)}, bf16[64,2048]{1,0:T(8,128)(2,1)}, u32[]{:S(2)}, u32[]{:S(2)}) collective-permute-start(bf16[64,2048]{1,0:T(8,128)(2,1)S(1)} %copy-done.3), channel_id=1, source_target_pairs={{0,4},{4,0},{8,12},{12,8},{16,20},{20,16},{24,28},{28,24},{1,5},{5... | collective-permute-start | bytes 786440 | tf_op jit(solution)/shard_map/ppermute | solution.py:46
  62.7 29.5 %collective-permute-start.12 = (bf16[64,2048]{1,0:T(8,128)(2,1)S(1)}, bf16[64,2048]{1,0:T(8,128)(2,1)}, u32[]{:S(2)}, u32[]{:S(2)}) collective-permute-start(bf16[64,2048]{1,0:T(8,128)(2,1)S(1)} %copy-done.2), channel_id=1, source_target_pairs={{0,8},{4,12},{8,0},{12,4},{16,24},{20,28},{24,16},{28,20},{1,9},{5... | collective-permute-start | bytes 786440 | tf_op jit(solution)/shard_map/ppermute | solution.py:46
  64.1 28.1 %collective-permute-start.13 = (bf16[64,2048]{1,0:T(8,128)(2,1)S(1)}, bf16[64,2048]{1,0:T(8,128)(2,1)}, u32[]{:S(2)}, u32[]{:S(2)}) collective-permute-start(bf16[64,2048]{1,0:T(8,128)(2,1)S(1)} %copy-done.1), channel_id=1, source_target_pairs={{0,12},{4,8},{8,4},{12,0},{16,28},{20,24},{24,20},{28,16},{1,13},{... | collective-permute-start | bytes 786440 | tf_op jit(solution)/shard_map/ppermute | solution.py:46
  64.2 45.9 %collective-permute-start.16 = (bf16[64,2048]{1,0:T(8,128)(2,1)}, bf16[64,2048]{1,0:T(8,128)(2,1)}, u32[]{:S(2)}, u32[]{:S(2)}) collective-permute-start(bf16[64,2048]{1,0:T(8,128)(2,1)} %get-tuple-element.84), channel_id=1, source_target_pairs={{0,16},{4,20},{8,24},{12,28},{16,0},{20,4},{24,8},{28,12},{1,17},{... | collective-permute-start | bytes 786440 | tf_op jit(solution)/shard_map/ppermute | solution.py:46
  73.3 38.7 %collective-permute-start.17 = (bf16[64,2048]{1,0:T(8,128)(2,1)}, bf16[64,2048]{1,0:T(8,128)(2,1)}, u32[]{:S(2)}, u32[]{:S(2)}) collective-permute-start(bf16[64,2048]{1,0:T(8,128)(2,1)} %get-tuple-element.85), channel_id=1, source_target_pairs={{0,20},{4,16},{8,28},{12,24},{16,4},{20,0},{24,12},{28,8},{1,21},{... | collective-permute-start | bytes 786440 | tf_op jit(solution)/shard_map/ppermute | solution.py:46
  92.2 26.7 %collective-permute-start.18 = (bf16[64,2048]{1,0:T(8,128)(2,1)}, bf16[64,2048]{1,0:T(8,128)(2,1)}, u32[]{:S(2)}, u32[]{:S(2)}) collective-permute-start(bf16[64,2048]{1,0:T(8,128)(2,1)} %get-tuple-element.87), channel_id=1, source_target_pairs={{0,24},{4,28},{8,16},{12,20},{16,8},{20,12},{24,0},{28,4},{1,25},{... | collective-permute-start | bytes 786440 | tf_op jit(solution)/shard_map/ppermute | solution.py:46
  92.2 27.9 %collective-permute-start.19 = (bf16[64,2048]{1,0:T(8,128)(2,1)}, bf16[64,2048]{1,0:T(8,128)(2,1)}, u32[]{:S(2)}, u32[]{:S(2)}) collective-permute-start(bf16[64,2048]{1,0:T(8,128)(2,1)} %get-tuple-element.89), channel_id=1, source_target_pairs={{0,28},{4,24},{8,20},{12,16},{16,12},{20,8},{24,4},{28,0},{1,29},{... | collective-permute-start | bytes 786440 | tf_op jit(solution)/shard_map/ppermute | solution.py:46
  97.5 1.6 %collective-permute-start.14 = (bf16[64,512]{1,0:T(8,128)(2,1)}, bf16[64,512]{1,0:T(8,128)(2,1)}, u32[]{:S(2)}, u32[]{:S(2)}) collective-permute-start(bf16[64,512]{1,0:T(8,128)(2,1)} %get-tuple-element.80), channel_id=1, source_target_pairs={{0,1},{1,0},{2,3},{3,2},{4,5},{5,4},{6,7},{7,6},{8,9},{9,8},{10,11... | collective-permute-start | bytes 196616 | tf_op jit(solution)/shard_map/ppermute | solution.py:46
  100.7 4.6 %collective-permute-start.15 = (bf16[64,512]{1,0:T(8,128)(2,1)}, bf16[64,512]{1,0:T(8,128)(2,1)}, u32[]{:S(2)}, u32[]{:S(2)}) collective-permute-start(bf16[64,512]{1,0:T(8,128)(2,1)} %get-tuple-element.82), channel_id=1, source_target_pairs={{0,2},{1,3},{2,0},{3,1},{4,6},{5,7},{6,4},{7,5},{8,10},{9,11},{10,... | collective-permute-start | bytes 196616 | tf_op jit(solution)/shard_map/ppermute | solution.py:46
  114.2 13.4 %collective-permute-start.24 = (bf16[64,512]{1,0:T(8,128)(2,1)}, bf16[64,512]{1,0:T(8,128)(2,1)}, u32[]{:S(2)}, u32[]{:S(2)}) collective-permute-start(bf16[64,512]{1,0:T(8,128)(2,1)} %get-tuple-element.101), channel_id=1, source_target_pairs={{0,20},{4,16},{8,28},{12,24},{16,4},{20,0},{24,12},{28,8},{1,21},{... | collective-permute-start | bytes 196616 | tf_op jit(solution)/shard_map/ppermute | solution.py:46
  114.2 14.4 %collective-permute-start.23 = (bf16[64,512]{1,0:T(8,128)(2,1)}, bf16[64,512]{1,0:T(8,128)(2,1)}, u32[]{:S(2)}, u32[]{:S(2)}) collective-permute-start(bf16[64,512]{1,0:T(8,128)(2,1)} %get-tuple-element.99), channel_id=1, source_target_pairs={{0,16},{4,20},{8,24},{12,28},{16,0},{20,4},{24,8},{28,12},{1,17},{... | collective-permute-start | bytes 196616 | tf_op jit(solution)/shard_map/ppermute | solution.py:46
  118.9 15.3 %collective-permute-start.22 = (bf16[64,512]{1,0:T(8,128)(2,1)}, bf16[64,512]{1,0:T(8,128)(2,1)}, u32[]{:S(2)}, u32[]{:S(2)}) collective-permute-start(bf16[64,512]{1,0:T(8,128)(2,1)} %get-tuple-element.97), channel_id=1, source_target_pairs={{0,12},{4,8},{8,4},{12,0},{16,28},{20,24},{24,20},{28,16},{1,13},{... | collective-permute-start | bytes 196616 | tf_op jit(solution)/shard_map/ppermute | solution.py:46
  118.9 15.3 %collective-permute-start.21 = (bf16[64,512]{1,0:T(8,128)(2,1)}, bf16[64,512]{1,0:T(8,128)(2,1)}, u32[]{:S(2)}, u32[]{:S(2)}) collective-permute-start(bf16[64,512]{1,0:T(8,128)(2,1)} %get-tuple-element.95), channel_id=1, source_target_pairs={{0,8},{4,12},{8,0},{12,4},{16,24},{20,28},{24,16},{28,20},{1,9},{5... | collective-permute-start | bytes 196616 | tf_op jit(solution)/shard_map/ppermute | solution.py:46
  120.1 14.1 %collective-permute-start.20 = (bf16[64,512]{1,0:T(8,128)(2,1)}, bf16[64,512]{1,0:T(8,128)(2,1)}, u32[]{:S(2)}, u32[]{:S(2)}) collective-permute-start(bf16[64,512]{1,0:T(8,128)(2,1)} %get-tuple-element.93), channel_id=1, source_target_pairs={{0,4},{4,0},{8,12},{12,8},{16,20},{20,16},{24,28},{28,24},{1,5},{5... | collective-permute-start | bytes 196616 | tf_op jit(solution)/shard_map/ppermute | solution.py:46
  127.7 7.6 %collective-permute-start.26 = (bf16[64,512]{1,0:T(8,128)(2,1)}, bf16[64,512]{1,0:T(8,128)(2,1)}, u32[]{:S(2)}, u32[]{:S(2)}) collective-permute-start(bf16[64,512]{1,0:T(8,128)(2,1)} %get-tuple-element.105), channel_id=1, source_target_pairs={{0,28},{4,24},{8,20},{12,16},{16,12},{20,8},{24,4},{28,0},{1,29},{... | collective-permute-start | bytes 196616 | tf_op jit(solution)/shard_map/ppermute | solution.py:46
  128.7 6.6 %collective-permute-start.25 = (bf16[64,512]{1,0:T(8,128)(2,1)}, bf16[64,512]{1,0:T(8,128)(2,1)}, u32[]{:S(2)}, u32[]{:S(2)}) collective-permute-start(bf16[64,512]{1,0:T(8,128)(2,1)} %get-tuple-element.103), channel_id=1, source_target_pairs={{0,24},{4,28},{8,16},{12,20},{16,8},{20,12},{24,0},{28,4},{1,25},{... | collective-permute-start | bytes 196616 | tf_op jit(solution)/shard_map/ppermute | solution.py:46

commit v6 on v5

--- a/solution.py
+++ b/solution.py
@@ -491,7 +491,8 @@
     adv, down_grad = down_grads(
         gst, place, slot_rows, score_rows, back, back_got, rows, up_got
     )
-    late = range(half + half // 2, groups)
+    late = list(range(half, half + half // 2))
+    soon = list(range(half + half // 2, groups))
     down_grad = list(down_grad)
     for k in late:
         down_grad[k] = lax.optimization_barrier((down_grad[k], down_got))[0]
@@ -513,7 +514,7 @@
     kv_new = adapted(place, ahead, ahead_got, base_mine, base_got, up_got, ())
     kv_out = kv_new.reshape(att, steps, cols)
     up_grad = up_grads(
-        place, adv, ahead, ahead_got, cot, groups, (kv_out, *down_grad_got[half : half + half // 2])
+        place, adv, ahead, ahead_got, cot, groups, (kv_out, *[down_grad_got[k] for k in soon])
     )
     up_grad_got = [up_grad[0]] + [None] * (groups - 1)
     for k in [*range(half, groups), *range(1, half)]:

time: 138 us -> 137 us (level)
  waiting for transfers between devices: 37.7 us -> 35.2 us
  starting transfers between devices: 48.9 us -> 50.8 us
    ppermute x27, waiting for transfers between devices: 27 us -> 24.6 us  [swap(): return lax.ppermute(x, axis, [(i, i ^ k) for i in range(n)])]
    ppermute x27, starting transfers between devices: 44.2 us -> 46.1 us  [swap(): return lax.ppermute(x, axis, [(i, i ^ k) for i in range(n)])]
where the time goes in v6:
time: 137 us; the launch traced here: 136 us
  starting transfers between devices  50.8 us (37%)
  Pallas kernels  40.1 us (29%)
  waiting for transfers between devices  35.2 us (26%)
  local copies, waits for them, and re-layouts  8.07 us (6%)
  other arithmetic  1.6 us (1%)
    ppermute x27, starting transfers between devices, swap(): return lax.ppermute(x, axis, [(i, i ^ k) for i in range(n)])  46.1 us
    pallas_call x9, Pallas kernels, call(): pl.pallas_call(run, out_shape=list(outs), in_specs=list(specs) + [ANY] *...  25.9 us
    ppermute x27, waiting for transfers between devices, swap(): return lax.ppermute(x, axis, [(i, i ^ k) for i in range(n)])  24.6 us
    all_to_all x1, waiting for transfers between devices, exchange(): return lax.all_to_all(x, 'dp', split_axis=0, concat_axis=0, tiled=True)  10.6 us
    pallas_call x1, Pallas kernels, base_parts(): pl.pallas_call(kernel, out_shape=[shaped((half, n, cols), bf)] * 2 + [sha...  9.83 us
    all_to_all x1, starting transfers between devices, exchange(): return lax.all_to_all(x, 'dp', split_axis=0, concat_axis=0, tiled=True)  4.68 us
    pallas_call x2, Pallas kernels, combine(): pl.pallas_call(kernel, out_shape=shaped(filled.shape, bf), in_specs=[ANY]...  4.35 us
    reshape x1, local copies, waits for them, and re-layouts, body(): rows = hidden.reshape(n, width)  4.13 us
  transfers between devices with their start and end apart: 28, of which 11 were waited for; matrix products, arithmetic and copies ran while one was open for 7% of the time, Pallas kernels for 26%

profile of v6, /device:TPU:0, one launch (start us, length us, event | category | flops | bytes accessed | tf_op | source)
XLA Modules:
  0.0 136.5 jit_solution(13401719955370986056)
XLA Ops:
  0.6 2.8 %shard_map.112 = (bf16[272,128]{1,0:T(8,128)(2,1)}, bf16[272,128]{1,0:T(8,128)(2,1)}, bf16[272,128]{1,0:T(8,128)(2,1)}, bf16[272,128]{1,0:T(8,128)(2,1)}, bf16[2...) custom-call(s32[8,8]{1,0:T(8,128)} %refs_0_.9, ...), custom_call_target="tpu_custom_call" | custom-call | tf_op jit(solution)/shard_map/pallas_call | solution.py:33
  3.5 3.0 %collective-permute-start = (bf16[272,128]{1,0:T(8,128)(2,1)}, bf16[272,128]{1,0:T(8,128)(2,1)}, u32[]{:S(2)}, u32[]{:S(2)}) collective-permute-start(bf16[272,128]{1,0:T(8,128)(2,1)} %get-tuple-element.57), channel_id=1, source_target_pairs={{0,4},{4,0},{8,12},{12,8},{16,20},{20,16},{24,28},{28,24},{1,5},{5... | collective-permute-start | bytes 208904 | tf_op jit(solution)/shard_map/ppermute | solution.py:46
  8.1 3.0 %collective-permute-start.3 = (bf16[272,128]{1,0:T(8,128)(2,1)}, bf16[272,128]{1,0:T(8,128)(2,1)}, u32[]{:S(2)}, u32[]{:S(2)}) collective-permute-start(bf16[272,128]{1,0:T(8,128)(2,1)} %get-tuple-element.60), channel_id=1, source_target_pairs={{0,16},{4,20},{8,24},{12,28},{16,0},{20,4},{24,8},{28,12},{1,17},{... | collective-permute-start | bytes 208904 | tf_op jit(solution)/shard_map/ppermute | solution.py:46
  12.3 3.6 %collective-permute-start.5 = (bf16[272,128]{1,0:T(8,128)(2,1)}, bf16[272,128]{1,0:T(8,128)(2,1)}, u32[]{:S(2)}, u32[]{:S(2)}) collective-permute-start(bf16[272,128]{1,0:T(8,128)(2,1)} %get-tuple-element.62), channel_id=1, source_target_pairs={{0,24},{4,28},{8,16},{12,20},{16,8},{20,12},{24,0},{28,4},{1,25},{... | collective-permute-start | bytes 208904 | tf_op jit(solution)/shard_map/ppermute | solution.py:46
  16.0 3.7 %shard_map.114 = bf16[8,64,2048]{2,1,0:T(8,128)(2,1)} custom-call(s32[8,8]{1,0:T(8,128)} %refs_0_.9, s32[128]{0:T(128)} %refs_1_.7, bf16[16,64,2048]{2,1,0:T(8,128)(2,1)} %bitcast.10, bf16[272,128]{1,0:T(8,128)(2,1)} %get-tuple-element.55.refs_3_.refs_7_.refs_5_), custom_call_target="tpu_custom_call" | custom-call | tf_op jit(solution)/shard_map/pallas_call | solution.py:33
  19.7 2.4 %collective-permute-done.4.refs_8_.refs_12_.refs_10_ = bf16[272,128]{1,0:T(8,128)(2,1)} collective-permute-done((bf16[272,128]{1,0:T(8,128)(2,1)}, bf16[272,128]{1,0:T(8,128)(2,1)}, u32[]{:S(2)}, u32[]{:S(2)}) %collective-permute-start.4) | collective-permute-done | bytes 69664 | tf_op jit(solution)/shard_map/ppermute | solution.py:46
  23.4 4.7 %all-to-all-start = ((bf16[8,64,2048]{2,1,0:T(8,128)(2,1)}), bf16[8,64,2048]{2,1,0:T(8,128)(2,1)}, u32[]{:S(2)}, u32[]{:S(2)}) async-start(bf16[8,64,2048]{2,1,0:T(8,128)(2,1)} %shard_map.114), calls=%async_computation | async-start | bytes 4194304 | tf_op jit(solution)/shard_map/all_to_all | solution.py:458
  29.1 2.5 %shard_map.113 = (f32[64,512]{1,0:T(8,128)}, bf16[64,512]{1,0:T(8,128)(2,1)}, s32[1,512]{1,0:T(1,128)}, s32[1,512]{1,0:T(1,128)}, f32[1,512]{1,0:T(1,128)}) custom-call(s32[1,256]{1,0:T(1,128)} %bitcast.12, s32[1,256]{1,0:T(1,128)} %bitcast.14, bf16[512,512]{1,0:T(8,128)(2,1)} %reshape.32.refs_2_.refs_4_, ...), custom_call_target="tpu_custom_call" | custom-call | tf_op jit(solution)/shard_map/pallas_call | solution.py:33
  36.3 4.1 %reshape.33.refs_6_.rows.refs_1_ = bf16[512,2048]{1,0:T(8,128)(2,1)} reshape(bf16[256,2,2048]{2,1,0:T(2,128)(2,1)} %param.9) | data formatting | bytes 4194304 | tf_op jit(solution)/shard_map/reshape | solution.py:485
  40.4 4.5 %shard_map.116 = (f32[1,512]{1,0:T(1,128)}, bf16[64,2048]{1,0:T(8,128)(2,1)}, bf16[64,2048]{1,0:T(8,128)(2,1)}, bf16[64,2048]{1,0:T(8,128)(2,1)}, bf16[64,2048]{...) custom-call(s32[8,8]{1,0:T(8,128)} %refs_0_.9, ...), custom_call_target="tpu_custom_call" | custom-call | tf_op jit(solution)/shard_map/pallas_call | solution.py:33
  44.9 9.8 %shard_map.117 = (bf16[2,512,512]{2,1,0:T(8,128)(2,1)}, bf16[2,512,512]{2,1,0:T(8,128)(2,1)}, bf16[16,64,2048]{2,1,0:T(8,128)(2,1)}, bf16[16,64,512]{2,1,0:T(8,128)(2,1)}) custom-call(s32[1]{0:T(128)} %bitcast.3.mine, bf16[512,2048]{1,0:T(8,128)(2,1)} %reshape.33.refs_6_.rows.refs_1_, bf16[2048,2048]{1,0:T(8,128)(2,1)} %weight.1, ...), custom_call_target="tpu_custom_call" | custom-call | tf_op jit(solution)/shard_map/pallas_call | solution.py:170
  54.8 2.9 %collective-permute-done.9 = bf16[2,512,512]{2,1,0:T(8,128)(2,1)S(1)} collective-permute-done((bf16[2,512,512]{2,1,0:T(8,128)(2,1)}, bf16[2,512,512]{2,1,0:T(8,128)(2,1)S(1)}, u32[]{:S(2)}, u32[]{:S(2)}) %collective-permute-start.9) | collective-permute-done | bytes 1048608 | tf_op jit(solution)/shard_map/ppermute | solution.py:46
  57.7 1.6 %add_convert_fusion = bf16[2,512,512]{2,1,0:T(8,128)(2,1)S(1)} fusion(bf16[2,512,512]{2,1,0:T(8,128)(2,1)S(1)} %collective-permute-done.9, bf16[2,512,512]{2,1,0:T(8,128)(2,1)} %get-tuple-element.74), kind=kLoop, calls=%fused_computation | loop fusion | flops 2097152 | bytes 3145728 | tf_op jit(solution)/shard_map/convert_element_type | solution.py:507
  60.6 2.0 %collective-permute-start.11 = (bf16[64,2048]{1,0:T(8,128)(2,1)S(1)}, bf16[64,2048]{1,0:T(8,128)(2,1)}, u32[]{:S(2)}, u32[]{:S(2)}) collective-permute-start(bf16[64,2048]{1,0:T(8,128)(2,1)S(1)} %copy-done.3), channel_id=1, source_target_pairs={{0,4},{4,0},{8,12},{12,8},{16,20},{20,16},{24,28},{28,24},{1,5},{5... | collective-permute-start | bytes 786440 | tf_op jit(solution)/shard_map/ppermute | solution.py:46
  64.2 3.8 %collective-permute-start.18 = (bf16[64,2048]{1,0:T(8,128)(2,1)}, bf16[64,2048]{1,0:T(8,128)(2,1)}, u32[]{:S(2)}, u32[]{:S(2)}) collective-permute-start(bf16[64,2048]{1,0:T(8,128)(2,1)} %get-tuple-element.88), channel_id=1, source_target_pairs={{0,24},{4,28},{8,16},{12,20},{16,8},{20,12},{24,0},{28,4},{1,25},{... | collective-permute-start | bytes 786440 | tf_op jit(solution)/shard_map/ppermute | solution.py:46
  68.0 5.3 %collective-permute-done.11.refs_4_.refs_3_ = bf16[64,2048]{1,0:T(8,128)(2,1)} collective-permute-done((bf16[64,2048]{1,0:T(8,128)(2,1)S(1)}, bf16[64,2048]{1,0:T(8,128)(2,1)}, u32[]{:S(2)}, u32[]{:S(2)}) %collective-permute-start.11) | collective-permute-done | bytes 262176 | tf_op jit(solution)/shard_map/ppermute | solution.py:46
  73.2 5.6 %collective-permute-start.19 = (bf16[64,2048]{1,0:T(8,128)(2,1)}, bf16[64,2048]{1,0:T(8,128)(2,1)}, u32[]{:S(2)}, u32[]{:S(2)}) collective-permute-start(bf16[64,2048]{1,0:T(8,128)(2,1)} %get-tuple-element.89), channel_id=1, source_target_pairs={{0,28},{4,24},{8,20},{12,16},{16,12},{20,8},{24,4},{28,0},{1,29},{... | collective-permute-start | bytes 786440 | tf_op jit(solution)/shard_map/ppermute | solution.py:46
  78.8 10.6 %all-to-all-done.refs_2_ = bf16[8,64,2048]{2,1,0:T(8,128)(2,1)} async-done(((bf16[8,64,2048]{2,1,0:T(8,128)(2,1)}), bf16[8,64,2048]{2,1,0:T(8,128)(2,1)}, u32[]{:S(2)}, u32[]{:S(2)}) %all-to-all-start) | async-done | bytes 2097184 | tf_op jit(solution)/shard_map/all_to_all | solution.py:458
  89.4 4.3 %collective-permute-done.12.refs_5_.refs_4_ = bf16[64,2048]{1,0:T(8,128)(2,1)} collective-permute-done((bf16[64,2048]{1,0:T(8,128)(2,1)S(1)}, bf16[64,2048]{1,0:T(8,128)(2,1)}, u32[]{:S(2)}, u32[]{:S(2)}) %collective-permute-start.12) | collective-permute-done | bytes 262176 | tf_op jit(solution)/shard_map/ppermute | solution.py:46
  95.2 4.2 %shard_map.118 = (f32[64,512]{1,0:T(8,128)}, bf16[64,512]{1,0:T(8,128)(2,1)}) custom-call(s32[1,512]{1,0:T(1,128)} %get-tuple-element.65.refs_2_.refs_0_, bf16[512,2048]{1,0:T(8,128)(2,1)} %reshape.33.refs_6_.rows.refs_1_, bf16[8,64,2048]{2,1,0:T(8,128)(2,1)} %all-to-all-done.refs_2_, bf16[512,512]{1,0:T(8,128)(2,1)} %collective-permute-done.10.refs_3_.refs_4_, ...), custom_call_target="tpu_custom_call" | custom-call | tf_op jit(solution)/shard_map/pallas_call | solution.py:33
  104.1 3.1 %collective-permute-done.15.refs_2_.refs_3_ = bf16[64,512]{1,0:T(8,128)(2,1)} collective-permute-done((bf16[64,512]{1,0:T(8,128)(2,1)}, bf16[64,512]{1,0:T(8,128)(2,1)}, u32[]{:S(2)}, u32[]{:S(2)}) %collective-permute-start.15) | collective-permute-done | bytes 65568 | tf_op jit(solution)/shard_map/ppermute | solution.py:46
  107.1 2.8 %shard_map.120 = bf16[512,512]{1,0:T(8,128)(2,1)} custom-call(s32[1,512]{1,0:T(1,128)} %get-tuple-element.64.refs_1_.refs_0_, f32[64,512]{1,0:T(8,128)} %get-tuple-element.81.refs_1_.refs_2_, bf16[64,512]{1,0:T(8,128)(2,1)} %collective-permute-done.15.refs_2_.refs_3_, bf16[512,512]{1,0:T(8,128)(2,1)} %get-tuple-element.107.refs_3_, ...), custom_call_target="tpu_custom_call" | custom-call | tf_op jit(solution)/shard_map/pallas_call | solution.py:33
  109.9 2.0 %reshape.37.refs_5_ = bf16[256,2,512]{2,1,0:T(2,128)(2,1)} reshape(bf16[512,512]{1,0:T(8,128)(2,1)} %shard_map.120) | data formatting | bytes 1048576 | tf_op jit(solution)/shard_map/reshape | solution.py:515
  111.9 2.3 %shard_map.122 = (bf16[64,512]{1,0:T(8,128)(2,1)}, bf16[64,512]{1,0:T(8,128)(2,1)}, bf16[64,512]{1,0:T(8,128)(2,1)}, bf16[64,512]{1,0:T(8,128)(2,1)}, bf16[64,51...) custom-call(s32[1,512]{1,0:T(1,128)} %get-tuple-element.64.refs_1_.refs_0_, ...), custom_call_target="tpu_custom_call" | custom-call | tf_op jit(solution)/shard_map/pallas_call | solution.py:33
  114.2 6.6 %collective-permute-start.26 = (bf16[64,512]{1,0:T(8,128)(2,1)}, bf16[64,512]{1,0:T(8,128)(2,1)}, u32[]{:S(2)}, u32[]{:S(2)}) collective-permute-start(bf16[64,512]{1,0:T(8,128)(2,1)} %get-tuple-element.105), channel_id=1, source_target_pairs={{0,28},{4,24},{8,20},{12,16},{16,12},{20,8},{24,4},{28,0},{1,29},{... | collective-permute-start | bytes 196616 | tf_op jit(solution)/shard_map/ppermute | solution.py:46
  120.9 1.8 %collective-permute-start.25 = (bf16[64,512]{1,0:T(8,128)(2,1)}, bf16[64,512]{1,0:T(8,128)(2,1)}, u32[]{:S(2)}, u32[]{:S(2)}) collective-permute-start(bf16[64,512]{1,0:T(8,128)(2,1)} %get-tuple-element.103), channel_id=1, source_target_pairs={{0,24},{4,28},{8,16},{12,20},{16,8},{20,12},{24,0},{28,4},{1,25},{... | collective-permute-start | bytes 196616 | tf_op jit(solution)/shard_map/ppermute | solution.py:46
  122.7 1.7 %collective-permute-start.22 = (bf16[64,512]{1,0:T(8,128)(2,1)}, bf16[64,512]{1,0:T(8,128)(2,1)}, u32[]{:S(2)}, u32[]{:S(2)}) collective-permute-start(bf16[64,512]{1,0:T(8,128)(2,1)} %get-tuple-element.97), channel_id=1, source_target_pairs={{0,12},{4,8},{8,4},{12,0},{16,28},{20,24},{24,20},{28,16},{1,13},{... | collective-permute-start | bytes 196616 | tf_op jit(solution)/shard_map/ppermute | solution.py:46
  124.4 1.8 %collective-permute-start.20 = (bf16[64,512]{1,0:T(8,128)(2,1)}, bf16[64,512]{1,0:T(8,128)(2,1)}, u32[]{:S(2)}, u32[]{:S(2)}) collective-permute-start(bf16[64,512]{1,0:T(8,128)(2,1)} %get-tuple-element.93), channel_id=1, source_target_pairs={{0,4},{4,0},{8,12},{12,8},{16,20},{20,16},{24,28},{28,24},{1,5},{5... | collective-permute-start | bytes 196616 | tf_op jit(solution)/shard_map/ppermute | solution.py:46
  126.2 2.6 %collective-permute-start.24 = (bf16[64,512]{1,0:T(8,128)(2,1)}, bf16[64,512]{1,0:T(8,128)(2,1)}, u32[]{:S(2)}, u32[]{:S(2)}) collective-permute-start(bf16[64,512]{1,0:T(8,128)(2,1)} %get-tuple-element.101), channel_id=1, source_target_pairs={{0,20},{4,16},{8,28},{12,24},{16,4},{20,0},{24,12},{28,8},{1,21},{... | collective-permute-start | bytes 196616 | tf_op jit(solution)/shard_map/ppermute | solution.py:46
  129.9 2.5 %shard_map.121.refs_11_ = bf16[16,64,2048]{2,1,0:T(8,128)(2,1)} custom-call(s32[8,8]{1,0:T(8,128)} %refs_0_.9, s32[128]{0:T(128)} %refs_1_.7, bf16[64,2048]{1,0:T(8,128)(2,1)} %get-tuple-element.83.refs_2_, bf16[64,2048]{1,0:T(8,128)(2,1)} %collective-permute-done.11.refs_4_.refs_3_, ...), custom_call_target="tpu_custom_call", output_to_operand_aliasing={{}: (10, {})} | custom-call | tf_op jit(solution)/shard_map/pallas_call | solution.py:437
  132.9 1.7 %collective-permute-done.23.refs_6_ = bf16[64,512]{1,0:T(8,128)(2,1)} collective-permute-done((bf16[64,512]{1,0:T(8,128)(2,1)}, bf16[64,512]{1,0:T(8,128)(2,1)}, u32[]{:S(2)}, u32[]{:S(2)}) %collective-permute-start.23) | collective-permute-done | bytes 65568 | tf_op jit(solution)/shard_map/ppermute | solution.py:46
  134.6 1.9 %shard_map.123 = bf16[16,64,512]{2,1,0:T(8,128)(2,1)} custom-call(s32[8,8]{1,0:T(8,128)} %refs_0_.9, s32[128]{0:T(128)} %refs_1_.7, bf16[64,512]{1,0:T(8,128)(2,1)} %get-tuple-element.91.refs_2_, bf16[64,512]{1,0:T(8,128)(2,1)} %collective-permute-done.20.refs_3_, bf16[64,512]{1,0:T(8,128)(2,1)} %collective-permute-done.21.refs_4_, ...), custom_call_target="tpu_custom_call", output_to_operand_aliasing={{}: (10, {})} | custom-call | tf_op jit(solution)/shard_map/pallas_call | solution.py:437
  (49 shorter events, 20.7 us)
Async XLA Ops:
  3.5 8.9 %collective-permute-start = (bf16[272,128]{1,0:T(8,128)(2,1)}, bf16[272,128]{1,0:T(8,128)(2,1)}, u32[]{:S(2)}, u32[]{:S(2)}) collective-permute-start(bf16[272,128]{1,0:T(8,128)(2,1)} %get-tuple-element.57), channel_id=1, source_target_pairs={{0,4},{4,0},{8,12},{12,8},{16,20},{20,16},{24,28},{28,24},{1,5},{5... | collective-permute-start | bytes 208904 | tf_op jit(solution)/shard_map/ppermute | solution.py:46
  6.5 9.5 %collective-permute-start.1 = (bf16[272,128]{1,0:T(8,128)(2,1)}, bf16[272,128]{1,0:T(8,128)(2,1)}, u32[]{:S(2)}, u32[]{:S(2)}) collective-permute-start(bf16[272,128]{1,0:T(8,128)(2,1)} %get-tuple-element.58), channel_id=1, source_target_pairs={{0,8},{4,12},{8,0},{12,4},{16,24},{20,28},{24,16},{28,20},{1,9},{5... | collective-permute-start | bytes 208904 | tf_op jit(solution)/shard_map/ppermute | solution.py:46
  8.1 11.6 %collective-permute-start.2 = (bf16[272,128]{1,0:T(8,128)(2,1)}, bf16[272,128]{1,0:T(8,128)(2,1)}, u32[]{:S(2)}, u32[]{:S(2)}) collective-permute-start(bf16[272,128]{1,0:T(8,128)(2,1)} %get-tuple-element.59), channel_id=1, source_target_pairs={{0,12},{4,8},{8,4},{12,0},{16,28},{20,24},{24,20},{28,16},{1,13},{... | collective-permute-start | bytes 208904 | tf_op jit(solution)/shard_map/ppermute | solution.py:46
  8.1 11.6 %collective-permute-start.3 = (bf16[272,128]{1,0:T(8,128)(2,1)}, bf16[272,128]{1,0:T(8,128)(2,1)}, u32[]{:S(2)}, u32[]{:S(2)}) collective-permute-start(bf16[272,128]{1,0:T(8,128)(2,1)} %get-tuple-element.60), channel_id=1, source_target_pairs={{0,16},{4,20},{8,24},{12,28},{16,0},{20,4},{24,8},{28,12},{1,17},{... | collective-permute-start | bytes 208904 | tf_op jit(solution)/shard_map/ppermute | solution.py:46
  11.1 11.0 %collective-permute-start.4 = (bf16[272,128]{1,0:T(8,128)(2,1)}, bf16[272,128]{1,0:T(8,128)(2,1)}, u32[]{:S(2)}, u32[]{:S(2)}) collective-permute-start(bf16[272,128]{1,0:T(8,128)(2,1)} %get-tuple-element.61), channel_id=1, source_target_pairs={{0,20},{4,16},{8,28},{12,24},{16,4},{20,0},{24,12},{28,8},{1,21},{... | collective-permute-start | bytes 208904 | tf_op jit(solution)/shard_map/ppermute | solution.py:46
  12.3 9.8 %collective-permute-start.5 = (bf16[272,128]{1,0:T(8,128)(2,1)}, bf16[272,128]{1,0:T(8,128)(2,1)}, u32[]{:S(2)}, u32[]{:S(2)}) collective-permute-start(bf16[272,128]{1,0:T(8,128)(2,1)} %get-tuple-element.62), channel_id=1, source_target_pairs={{0,24},{4,28},{8,16},{12,20},{16,8},{20,12},{24,0},{28,4},{1,25},{... | collective-permute-start | bytes 208904 | tf_op jit(solution)/shard_map/ppermute | solution.py:46
  15.9 7.4 %collective-permute-start.6 = (bf16[272,128]{1,0:T(8,128)(2,1)}, bf16[272,128]{1,0:T(8,128)(2,1)}, u32[]{:S(2)}, u32[]{:S(2)}) collective-permute-start(bf16[272,128]{1,0:T(8,128)(2,1)} %get-tuple-element.63), channel_id=1, source_target_pairs={{0,28},{4,24},{8,20},{12,16},{16,12},{20,8},{24,4},{28,0},{1,29},{... | collective-permute-start | bytes 208904 | tf_op jit(solution)/shard_map/ppermute | solution.py:46
  19.7 8.4 %copy-start = (bf16[256,2,512]{2,1,0:T(2,128)(2,1)S(1)}, bf16[256,2,512]{2,1,0:T(2,128)(2,1)}, u32[]{:S(2)}) copy-start(bf16[256,2,512]{2,1,0:T(2,128)(2,1)} %param.17) | copy-start | bytes 1572868
  23.4 66.0 %all-to-all-start = ((bf16[8,64,2048]{2,1,0:T(8,128)(2,1)}), bf16[8,64,2048]{2,1,0:T(8,128)(2,1)}, u32[]{:S(2)}, u32[]{:S(2)}) async-start(bf16[8,64,2048]{2,1,0:T(8,128)(2,1)} %shard_map.114), calls=%async_computation | async-start | bytes 4194304 | tf_op jit(solution)/shard_map/all_to_all | solution.py:458
  31.6 1.6 %collective-permute-start.7 = (bf16[64,512]{1,0:T(8,128)(2,1)}, bf16[64,512]{1,0:T(8,128)(2,1)}, u32[]{:S(2)}, u32[]{:S(2)}) collective-permute-start(bf16[64,512]{1,0:T(8,128)(2,1)} %get-tuple-element.70), channel_id=1, source_target_pairs={{0,1},{1,0},{2,3},{3,2},{4,5},{5,4},{6,7},{7,6},{8,9},{9,8},{10,11... | collective-permute-start | bytes 196616 | tf_op jit(solution)/shard_map/ppermute | solution.py:46
  34.8 5.7 %collective-permute-start.8 = (bf16[64,512]{1,0:T(8,128)(2,1)}, bf16[64,512]{1,0:T(8,128)(2,1)}, u32[]{:S(2)}, u32[]{:S(2)}) collective-permute-start(bf16[64,512]{1,0:T(8,128)(2,1)} %get-tuple-element.72), channel_id=1, source_target_pairs={{0,2},{1,3},{2,0},{3,1},{4,6},{5,7},{6,4},{7,5},{8,10},{9,11},{10,... | collective-permute-start | bytes 196616 | tf_op jit(solution)/shard_map/ppermute | solution.py:46
  54.7 2.9 %collective-permute-start.9 = (bf16[2,512,512]{2,1,0:T(8,128)(2,1)}, bf16[2,512,512]{2,1,0:T(8,128)(2,1)S(1)}, u32[]{:S(2)}, u32[]{:S(2)}) collective-permute-start(bf16[2,512,512]{2,1,0:T(8,128)(2,1)} %get-tuple-element.75), channel_id=1, source_target_pairs={{0,1},{1,0},{2,3},{3,2},{4,5},{5,4},{6,7},{7,6},{8,9},{9,8},{10,11... | collective-permute-start | bytes 3145736 | tf_op jit(solution)/shard_map/ppermute | solution.py:46
  57.7 3.0 %copy-start.3 = (bf16[64,2048]{1,0:T(8,128)(2,1)S(1)}, bf16[64,2048]{1,0:T(8,128)(2,1)}, u32[]{:S(2)}) copy-start(bf16[64,2048]{1,0:T(8,128)(2,1)} %get-tuple-element.76) | copy-start | bytes 786436
  57.7 5.0 %copy-start.2 = (bf16[64,2048]{1,0:T(8,128)(2,1)S(1)}, bf16[64,2048]{1,0:T(8,128)(2,1)}, u32[]{:S(2)}) copy-start(bf16[64,2048]{1,0:T(8,128)(2,1)} %get-tuple-element.77) | copy-start | bytes 786436
  57.7 6.5 %copy-start.1 = (bf16[64,2048]{1,0:T(8,128)(2,1)S(1)}, bf16[64,2048]{1,0:T(8,128)(2,1)}, u32[]{:S(2)}) copy-start(bf16[64,2048]{1,0:T(8,128)(2,1)} %get-tuple-element.78) | copy-start | bytes 786436
  60.1 35.1 %collective-permute-start.10 = (bf16[512,512]{1,0:T(8,128)(2,1)S(1)}, bf16[512,512]{1,0:T(8,128)(2,1)}, u32[]{:S(2)}, u32[]{:S(2)}) collective-permute-start(bf16[512,512]{1,0:T(8,128)(2,1)S(1)} %get-tuple-element.108), channel_id=1, source_target_pairs={{0,2},{1,3},{2,0},{3,1},{4,6},{5,7},{6,4},{7,5},{8,10},{9,11},{10,... | collective-permute-start | bytes 1572872 | tf_op jit(solution)/shard_map/ppermute | solution.py:46
  60.6 12.6 %collective-permute-start.11 = (bf16[64,2048]{1,0:T(8,128)(2,1)S(1)}, bf16[64,2048]{1,0:T(8,128)(2,1)}, u32[]{:S(2)}, u32[]{:S(2)}) collective-permute-start(bf16[64,2048]{1,0:T(8,128)(2,1)S(1)} %copy-done.3), channel_id=1, source_target_pairs={{0,4},{4,0},{8,12},{12,8},{16,20},{20,16},{24,28},{28,24},{1,5},{5... | collective-permute-start | bytes 786440 | tf_op jit(solution)/shard_map/ppermute | solution.py:46
  62.7 31.0 %collective-permute-start.12 = (bf16[64,2048]{1,0:T(8,128)(2,1)S(1)}, bf16[64,2048]{1,0:T(8,128)(2,1)}, u32[]{:S(2)}, u32[]{:S(2)}) collective-permute-start(bf16[64,2048]{1,0:T(8,128)(2,1)S(1)} %copy-done.2), channel_id=1, source_target_pairs={{0,8},{4,12},{8,0},{12,4},{16,24},{20,28},{24,16},{28,20},{1,9},{5... | collective-permute-start | bytes 786440 | tf_op jit(solution)/shard_map/ppermute | solution.py:46
  64.1 29.6 %collective-permute-start.13 = (bf16[64,2048]{1,0:T(8,128)(2,1)S(1)}, bf16[64,2048]{1,0:T(8,128)(2,1)}, u32[]{:S(2)}, u32[]{:S(2)}) collective-permute-start(bf16[64,2048]{1,0:T(8,128)(2,1)S(1)} %copy-done.1), channel_id=1, source_target_pairs={{0,12},{4,8},{8,4},{12,0},{16,28},{20,24},{24,20},{28,16},{1,13},{... | collective-permute-start | bytes 786440 | tf_op jit(solution)/shard_map/ppermute | solution.py:46
  64.2 47.7 %collective-permute-start.18 = (bf16[64,2048]{1,0:T(8,128)(2,1)}, bf16[64,2048]{1,0:T(8,128)(2,1)}, u32[]{:S(2)}, u32[]{:S(2)}) collective-permute-start(bf16[64,2048]{1,0:T(8,128)(2,1)} %get-tuple-element.88), channel_id=1, source_target_pairs={{0,24},{4,28},{8,16},{12,20},{16,8},{20,12},{24,0},{28,4},{1,25},{... | collective-permute-start | bytes 786440 | tf_op jit(solution)/shard_map/ppermute | solution.py:46
  73.2 38.7 %collective-permute-start.19 = (bf16[64,2048]{1,0:T(8,128)(2,1)}, bf16[64,2048]{1,0:T(8,128)(2,1)}, u32[]{:S(2)}, u32[]{:S(2)}) collective-permute-start(bf16[64,2048]{1,0:T(8,128)(2,1)} %get-tuple-element.89), channel_id=1, source_target_pairs={{0,28},{4,24},{8,20},{12,16},{16,12},{20,8},{24,4},{28,0},{1,29},{... | collective-permute-start | bytes 786440 | tf_op jit(solution)/shard_map/ppermute | solution.py:46
  93.7 30.7 %collective-permute-start.16 = (bf16[64,2048]{1,0:T(8,128)(2,1)}, bf16[64,2048]{1,0:T(8,128)(2,1)}, u32[]{:S(2)}, u32[]{:S(2)}) collective-permute-start(bf16[64,2048]{1,0:T(8,128)(2,1)} %get-tuple-element.85), channel_id=1, source_target_pairs={{0,16},{4,20},{8,24},{12,28},{16,0},{20,4},{24,8},{28,12},{1,17},{... | collective-permute-start | bytes 786440 | tf_op jit(solution)/shard_map/ppermute | solution.py:46
  93.7 30.7 %collective-permute-start.17 = (bf16[64,2048]{1,0:T(8,128)(2,1)}, bf16[64,2048]{1,0:T(8,128)(2,1)}, u32[]{:S(2)}, u32[]{:S(2)}) collective-permute-start(bf16[64,2048]{1,0:T(8,128)(2,1)} %get-tuple-element.87), channel_id=1, source_target_pairs={{0,20},{4,16},{8,28},{12,24},{16,4},{20,0},{24,12},{28,8},{1,21},{... | collective-permute-start | bytes 786440 | tf_op jit(solution)/shard_map/ppermute | solution.py:46
  99.4 1.6 %collective-permute-start.14 = (bf16[64,512]{1,0:T(8,128)(2,1)}, bf16[64,512]{1,0:T(8,128)(2,1)}, u32[]{:S(2)}, u32[]{:S(2)}) collective-permute-start(bf16[64,512]{1,0:T(8,128)(2,1)} %get-tuple-element.80), channel_id=1, source_target_pairs={{0,1},{1,0},{2,3},{3,2},{4,5},{5,4},{6,7},{7,6},{8,9},{9,8},{10,11... | collective-permute-start | bytes 196616 | tf_op jit(solution)/shard_map/ppermute | solution.py:46
  102.6 4.6 %collective-permute-start.15 = (bf16[64,512]{1,0:T(8,128)(2,1)}, bf16[64,512]{1,0:T(8,128)(2,1)}, u32[]{:S(2)}, u32[]{:S(2)}) collective-permute-start(bf16[64,512]{1,0:T(8,128)(2,1)} %get-tuple-element.82), channel_id=1, source_target_pairs={{0,2},{1,3},{2,0},{3,1},{4,6},{5,7},{6,4},{7,5},{8,10},{9,11},{10,... | collective-permute-start | bytes 196616 | tf_op jit(solution)/shard_map/ppermute | solution.py:46
  114.2 11.9 %collective-permute-start.26 = (bf16[64,512]{1,0:T(8,128)(2,1)}, bf16[64,512]{1,0:T(8,128)(2,1)}, u32[]{:S(2)}, u32[]{:S(2)}) collective-permute-start(bf16[64,512]{1,0:T(8,128)(2,1)} %get-tuple-element.105), channel_id=1, source_target_pairs={{0,28},{4,24},{8,20},{12,16},{16,12},{20,8},{24,4},{28,0},{1,29},{... | collective-permute-start | bytes 196616 | tf_op jit(solution)/shard_map/ppermute | solution.py:46
  120.9 7.9 %collective-permute-start.25 = (bf16[64,512]{1,0:T(8,128)(2,1)}, bf16[64,512]{1,0:T(8,128)(2,1)}, u32[]{:S(2)}, u32[]{:S(2)}) collective-permute-start(bf16[64,512]{1,0:T(8,128)(2,1)} %get-tuple-element.103), channel_id=1, source_target_pairs={{0,24},{4,28},{8,16},{12,20},{16,8},{20,12},{24,0},{28,4},{1,25},{... | collective-permute-start | bytes 196616 | tf_op jit(solution)/shard_map/ppermute | solution.py:46
  122.7 9.7 %collective-permute-start.22 = (bf16[64,512]{1,0:T(8,128)(2,1)}, bf16[64,512]{1,0:T(8,128)(2,1)}, u32[]{:S(2)}, u32[]{:S(2)}) collective-permute-start(bf16[64,512]{1,0:T(8,128)(2,1)} %get-tuple-element.97), channel_id=1, source_target_pairs={{0,12},{4,8},{8,4},{12,0},{16,28},{20,24},{24,20},{28,16},{1,13},{... | collective-permute-start | bytes 196616 | tf_op jit(solution)/shard_map/ppermute | solution.py:46
  124.4 8.0 %collective-permute-start.21 = (bf16[64,512]{1,0:T(8,128)(2,1)}, bf16[64,512]{1,0:T(8,128)(2,1)}, u32[]{:S(2)}, u32[]{:S(2)}) collective-permute-start(bf16[64,512]{1,0:T(8,128)(2,1)} %get-tuple-element.95), channel_id=1, source_target_pairs={{0,8},{4,12},{8,0},{12,4},{16,24},{20,28},{24,16},{28,20},{1,9},{5... | collective-permute-start | bytes 196616 | tf_op jit(solution)/shard_map/ppermute | solution.py:46
  124.4 8.0 %collective-permute-start.20 = (bf16[64,512]{1,0:T(8,128)(2,1)}, bf16[64,512]{1,0:T(8,128)(2,1)}, u32[]{:S(2)}, u32[]{:S(2)}) collective-permute-start(bf16[64,512]{1,0:T(8,128)(2,1)} %get-tuple-element.93), channel_id=1, source_target_pairs={{0,4},{4,0},{8,12},{12,8},{16,20},{20,16},{24,28},{28,24},{1,5},{5... | collective-permute-start | bytes 196616 | tf_op jit(solution)/shard_map/ppermute | solution.py:46
  126.2 6.7 %collective-permute-start.24 = (bf16[64,512]{1,0:T(8,128)(2,1)}, bf16[64,512]{1,0:T(8,128)(2,1)}, u32[]{:S(2)}, u32[]{:S(2)}) collective-permute-start(bf16[64,512]{1,0:T(8,128)(2,1)} %get-tuple-element.101), channel_id=1, source_target_pairs={{0,20},{4,16},{8,28},{12,24},{16,4},{20,0},{24,12},{28,8},{1,21},{... | collective-permute-start | bytes 196616 | tf_op jit(solution)/shard_map/ppermute | solution.py:46
  128.8 5.8 %collective-permute-start.23 = (bf16[64,512]{1,0:T(8,128)(2,1)}, bf16[64,512]{1,0:T(8,128)(2,1)}, u32[]{:S(2)}, u32[]{:S(2)}) collective-permute-start(bf16[64,512]{1,0:T(8,128)(2,1)} %get-tuple-element.99), channel_id=1, source_target_pairs={{0,16},{4,20},{8,24},{12,28},{16,0},{20,4},{24,8},{28,12},{1,17},{... | collective-permute-start | bytes 196616 | tf_op jit(solution)/shard_map/ppermute | solution.py:46

commit v7 on v6

--- a/solution.py
+++ b/solution.py
@@ -514,7 +514,7 @@
     kv_new = adapted(place, ahead, ahead_got, base_mine, base_got, up_got, ())
     kv_out = kv_new.reshape(att, steps, cols)
     up_grad = up_grads(
-        place, adv, ahead, ahead_got, cot, groups, (kv_out, *[down_grad_got[k] for k in soon])
+        place, adv, ahead, ahead_got, cot, groups, (kv_out, down_grad_got[soon[-1]])
     )
     up_grad_got = [up_grad[0]] + [None] * (groups - 1)
     for k in [*range(half, groups), *range(1, half)]:

time: 137 us -> 137 us (level)
    all_to_all x1, waiting for transfers between devices: 10.6 us -> 12.6 us  [exchange(): return lax.all_to_all(x, 'dp', split_axis=0, concat_axis=0, tiled=True)]
where the time goes in v7:
time: 137 us; the launch traced here: 136 us
  starting transfers between devices  49.7 us (36%)
  Pallas kernels  40.1 us (29%)
  waiting for transfers between devices  36.3 us (26%)
  local copies, waits for them, and re-layouts  8.07 us (6%)
  other arithmetic  1.6 us (1%)
    ppermute x27, starting transfers between devices, swap(): return lax.ppermute(x, axis, [(i, i ^ k) for i in range(n)])  45 us
    pallas_call x9, Pallas kernels, call(): pl.pallas_call(run, out_shape=list(outs), in_specs=list(specs) + [ANY] *...  25.9 us
    ppermute x27, waiting for transfers between devices, swap(): return lax.ppermute(x, axis, [(i, i ^ k) for i in range(n)])  23.7 us
    all_to_all x1, waiting for transfers between devices, exchange(): return lax.all_to_all(x, 'dp', split_axis=0, concat_axis=0, tiled=True)  12.6 us
    pallas_call x1, Pallas kernels, base_parts(): pl.pallas_call(kernel, out_shape=[shaped((half, n, cols), bf)] * 2 + [sha...  9.83 us
    all_to_all x1, starting transfers between devices, exchange(): return lax.all_to_all(x, 'dp', split_axis=0, concat_axis=0, tiled=True)  4.68 us
    pallas_call x2, Pallas kernels, combine(): pl.pallas_call(kernel, out_shape=shaped(filled.shape, bf), in_specs=[ANY]...  4.36 us
    reshape x1, local copies, waits for them, and re-layouts, body(): rows = hidden.reshape(n, width)  4.13 us
  transfers between devices with their start and end apart: 28, of which 11 were waited for; matrix products, arithmetic and copies ran while one was open for 7% of the time, Pallas kernels for 26%

profile of v7, /device:TPU:0, one launch (start us, length us, event | category | flops | bytes accessed | tf_op | source)
XLA Modules:
  0.0 136.5 jit_solution(8024817598901790636)
XLA Ops:
  0.6 2.8 %shard_map.112 = (bf16[272,128]{1,0:T(8,128)(2,1)}, bf16[272,128]{1,0:T(8,128)(2,1)}, bf16[272,128]{1,0:T(8,128)(2,1)}, bf16[272,128]{1,0:T(8,128)(2,1)}, bf16[2...) custom-call(s32[8,8]{1,0:T(8,128)} %refs_0_.9, ...), custom_call_target="tpu_custom_call" | custom-call | tf_op jit(solution)/shard_map/pallas_call | solution.py:33
  3.5 3.0 %collective-permute-start = (bf16[272,128]{1,0:T(8,128)(2,1)}, bf16[272,128]{1,0:T(8,128)(2,1)}, u32[]{:S(2)}, u32[]{:S(2)}) collective-permute-start(bf16[272,128]{1,0:T(8,128)(2,1)} %get-tuple-element.57), channel_id=1, source_target_pairs={{0,4},{4,0},{8,12},{12,8},{16,20},{20,16},{24,28},{28,24},{1,5},{5... | collective-permute-start | bytes 208904 | tf_op jit(solution)/shard_map/ppermute | solution.py:46
  8.1 3.0 %collective-permute-start.3 = (bf16[272,128]{1,0:T(8,128)(2,1)}, bf16[272,128]{1,0:T(8,128)(2,1)}, u32[]{:S(2)}, u32[]{:S(2)}) collective-permute-start(bf16[272,128]{1,0:T(8,128)(2,1)} %get-tuple-element.60), channel_id=1, source_target_pairs={{0,16},{4,20},{8,24},{12,28},{16,0},{20,4},{24,8},{28,12},{1,17},{... | collective-permute-start | bytes 208904 | tf_op jit(solution)/shard_map/ppermute | solution.py:46
  12.3 3.6 %collective-permute-start.5 = (bf16[272,128]{1,0:T(8,128)(2,1)}, bf16[272,128]{1,0:T(8,128)(2,1)}, u32[]{:S(2)}, u32[]{:S(2)}) collective-permute-start(bf16[272,128]{1,0:T(8,128)(2,1)} %get-tuple-element.62), channel_id=1, source_target_pairs={{0,24},{4,28},{8,16},{12,20},{16,8},{20,12},{24,0},{28,4},{1,25},{... | collective-permute-start | bytes 208904 | tf_op jit(solution)/shard_map/ppermute | solution.py:46
  16.0 3.7 %shard_map.114 = bf16[8,64,2048]{2,1,0:T(8,128)(2,1)} custom-call(s32[8,8]{1,0:T(8,128)} %refs_0_.9, s32[128]{0:T(128)} %refs_1_.7, bf16[16,64,2048]{2,1,0:T(8,128)(2,1)} %bitcast.10, bf16[272,128]{1,0:T(8,128)(2,1)} %get-tuple-element.55.refs_3_.refs_7_.refs_5_), custom_call_target="tpu_custom_call" | custom-call | tf_op jit(solution)/shard_map/pallas_call | solution.py:33
  19.7 2.4 %collective-permute-done.4.refs_8_.refs_12_.refs_10_ = bf16[272,128]{1,0:T(8,128)(2,1)} collective-permute-done((bf16[272,128]{1,0:T(8,128)(2,1)}, bf16[272,128]{1,0:T(8,128)(2,1)}, u32[]{:S(2)}, u32[]{:S(2)}) %collective-permute-start.4) | collective-permute-done | bytes 69664 | tf_op jit(solution)/shard_map/ppermute | solution.py:46
  23.4 4.7 %all-to-all-start = ((bf16[8,64,2048]{2,1,0:T(8,128)(2,1)}), bf16[8,64,2048]{2,1,0:T(8,128)(2,1)}, u32[]{:S(2)}, u32[]{:S(2)}) async-start(bf16[8,64,2048]{2,1,0:T(8,128)(2,1)} %shard_map.114), calls=%async_computation | async-start | bytes 4194304 | tf_op jit(solution)/shard_map/all_to_all | solution.py:458
  29.1 2.5 %shard_map.113 = (f32[64,512]{1,0:T(8,128)}, bf16[64,512]{1,0:T(8,128)(2,1)}, s32[1,512]{1,0:T(1,128)}, s32[1,512]{1,0:T(1,128)}, f32[1,512]{1,0:T(1,128)}) custom-call(s32[1,256]{1,0:T(1,128)} %bitcast.12, s32[1,256]{1,0:T(1,128)} %bitcast.14, bf16[512,512]{1,0:T(8,128)(2,1)} %reshape.32.refs_2_.refs_4_, ...), custom_call_target="tpu_custom_call" | custom-call | tf_op jit(solution)/shard_map/pallas_call | solution.py:33
  36.3 4.1 %reshape.33.refs_6_.rows.refs_1_ = bf16[512,2048]{1,0:T(8,128)(2,1)} reshape(bf16[256,2,2048]{2,1,0:T(2,128)(2,1)} %param.9) | data formatting | bytes 4194304 | tf_op jit(solution)/shard_map/reshape | solution.py:485
  40.4 4.5 %shard_map.116 = (f32[1,512]{1,0:T(1,128)}, bf16[64,2048]{1,0:T(8,128)(2,1)}, bf16[64,2048]{1,0:T(8,128)(2,1)}, bf16[64,2048]{1,0:T(8,128)(2,1)}, bf16[64,2048]{...) custom-call(s32[8,8]{1,0:T(8,128)} %refs_0_.9, ...), custom_call_target="tpu_custom_call" | custom-call | tf_op jit(solution)/shard_map/pallas_call | solution.py:33
  44.9 9.8 %shard_map.117 = (bf16[2,512,512]{2,1,0:T(8,128)(2,1)}, bf16[2,512,512]{2,1,0:T(8,128)(2,1)}, bf16[16,64,2048]{2,1,0:T(8,128)(2,1)}, bf16[16,64,512]{2,1,0:T(8,128)(2,1)}) custom-call(s32[1]{0:T(128)} %bitcast.3.mine, bf16[512,2048]{1,0:T(8,128)(2,1)} %reshape.33.refs_6_.rows.refs_1_, bf16[2048,2048]{1,0:T(8,128)(2,1)} %weight.1, ...), custom_call_target="tpu_custom_call" | custom-call | tf_op jit(solution)/shard_map/pallas_call | solution.py:170
  54.8 2.9 %collective-permute-done.9 = bf16[2,512,512]{2,1,0:T(8,128)(2,1)S(1)} collective-permute-done((bf16[2,512,512]{2,1,0:T(8,128)(2,1)}, bf16[2,512,512]{2,1,0:T(8,128)(2,1)S(1)}, u32[]{:S(2)}, u32[]{:S(2)}) %collective-permute-start.9) | collective-permute-done | bytes 1048608 | tf_op jit(solution)/shard_map/ppermute | solution.py:46
  57.7 1.6 %add_convert_fusion = bf16[2,512,512]{2,1,0:T(8,128)(2,1)S(1)} fusion(bf16[2,512,512]{2,1,0:T(8,128)(2,1)S(1)} %collective-permute-done.9, bf16[2,512,512]{2,1,0:T(8,128)(2,1)} %get-tuple-element.74), kind=kLoop, calls=%fused_computation | loop fusion | flops 2097152 | bytes 3145728 | tf_op jit(solution)/shard_map/convert_element_type | solution.py:507
  60.6 2.0 %collective-permute-start.11 = (bf16[64,2048]{1,0:T(8,128)(2,1)S(1)}, bf16[64,2048]{1,0:T(8,128)(2,1)}, u32[]{:S(2)}, u32[]{:S(2)}) collective-permute-start(bf16[64,2048]{1,0:T(8,128)(2,1)S(1)} %copy-done.3), channel_id=1, source_target_pairs={{0,4},{4,0},{8,12},{12,8},{16,20},{20,16},{24,28},{28,24},{1,5},{5... | collective-permute-start | bytes 786440 | tf_op jit(solution)/shard_map/ppermute | solution.py:46
  64.2 4.7 %collective-permute-start.19 = (bf16[64,2048]{1,0:T(8,128)(2,1)}, bf16[64,2048]{1,0:T(8,128)(2,1)}, u32[]{:S(2)}, u32[]{:S(2)}) collective-permute-start(bf16[64,2048]{1,0:T(8,128)(2,1)} %get-tuple-element.89), channel_id=1, source_target_pairs={{0,28},{4,24},{8,20},{12,16},{16,12},{20,8},{24,4},{28,0},{1,29},{... | collective-permute-start | bytes 786440 | tf_op jit(solution)/shard_map/ppermute | solution.py:46
  68.9 4.4 %collective-permute-done.11.refs_4_.refs_3_ = bf16[64,2048]{1,0:T(8,128)(2,1)} collective-permute-done((bf16[64,2048]{1,0:T(8,128)(2,1)S(1)}, bf16[64,2048]{1,0:T(8,128)(2,1)}, u32[]{:S(2)}, u32[]{:S(2)}) %collective-permute-start.11) | collective-permute-done | bytes 262176 | tf_op jit(solution)/shard_map/ppermute | solution.py:46
  73.2 3.6 %collective-permute-start.18 = (bf16[64,2048]{1,0:T(8,128)(2,1)}, bf16[64,2048]{1,0:T(8,128)(2,1)}, u32[]{:S(2)}, u32[]{:S(2)}) collective-permute-start(bf16[64,2048]{1,0:T(8,128)(2,1)} %get-tuple-element.88), channel_id=1, source_target_pairs={{0,24},{4,28},{8,16},{12,20},{16,8},{20,12},{24,0},{28,4},{1,25},{... | collective-permute-start | bytes 786440 | tf_op jit(solution)/shard_map/ppermute | solution.py:46
  76.8 12.6 %all-to-all-done.refs_2_ = bf16[8,64,2048]{2,1,0:T(8,128)(2,1)} async-done(((bf16[8,64,2048]{2,1,0:T(8,128)(2,1)}), bf16[8,64,2048]{2,1,0:T(8,128)(2,1)}, u32[]{:S(2)}, u32[]{:S(2)}) %all-to-all-start) | async-done | bytes 2097184 | tf_op jit(solution)/shard_map/all_to_all | solution.py:458
  89.4 4.3 %collective-permute-done.12.refs_5_.refs_4_ = bf16[64,2048]{1,0:T(8,128)(2,1)} collective-permute-done((bf16[64,2048]{1,0:T(8,128)(2,1)S(1)}, bf16[64,2048]{1,0:T(8,128)(2,1)}, u32[]{:S(2)}, u32[]{:S(2)}) %collective-permute-start.12) | collective-permute-done | bytes 262176 | tf_op jit(solution)/shard_map/ppermute | solution.py:46
  95.2 4.2 %shard_map.118 = (f32[64,512]{1,0:T(8,128)}, bf16[64,512]{1,0:T(8,128)(2,1)}) custom-call(s32[1,512]{1,0:T(1,128)} %get-tuple-element.65.refs_2_.refs_0_, bf16[512,2048]{1,0:T(8,128)(2,1)} %reshape.33.refs_6_.rows.refs_1_, bf16[8,64,2048]{2,1,0:T(8,128)(2,1)} %all-to-all-done.refs_2_, bf16[512,512]{1,0:T(8,128)(2,1)} %collective-permute-done.10.refs_3_.refs_4_, ...), custom_call_target="tpu_custom_call" | custom-call | tf_op jit(solution)/shard_map/pallas_call | solution.py:33
  104.1 3.1 %collective-permute-done.15.refs_2_.refs_3_ = bf16[64,512]{1,0:T(8,128)(2,1)} collective-permute-done((bf16[64,512]{1,0:T(8,128)(2,1)}, bf16[64,512]{1,0:T(8,128)(2,1)}, u32[]{:S(2)}, u32[]{:S(2)}) %collective-permute-start.15) | collective-permute-done | bytes 65568 | tf_op jit(solution)/shard_map/ppermute | solution.py:46
  107.1 2.8 %shard_map.120 = bf16[512,512]{1,0:T(8,128)(2,1)} custom-call(s32[1,512]{1,0:T(1,128)} %get-tuple-element.64.refs_1_.refs_0_, f32[64,512]{1,0:T(8,128)} %get-tuple-element.81.refs_1_.refs_2_, bf16[64,512]{1,0:T(8,128)(2,1)} %collective-permute-done.15.refs_2_.refs_3_, bf16[512,512]{1,0:T(8,128)(2,1)} %get-tuple-element.107.refs_3_, ...), custom_call_target="tpu_custom_call" | custom-call | tf_op jit(solution)/shard_map/pallas_call | solution.py:33
  109.9 2.0 %reshape.37.refs_5_ = bf16[256,2,512]{2,1,0:T(2,128)(2,1)} reshape(bf16[512,512]{1,0:T(8,128)(2,1)} %shard_map.120) | data formatting | bytes 1048576 | tf_op jit(solution)/shard_map/reshape | solution.py:515
  111.9 2.3 %shard_map.122 = (bf16[64,512]{1,0:T(8,128)(2,1)}, bf16[64,512]{1,0:T(8,128)(2,1)}, bf16[64,512]{1,0:T(8,128)(2,1)}, bf16[64,512]{1,0:T(8,128)(2,1)}, bf16[64,51...) custom-call(s32[1,512]{1,0:T(1,128)} %get-tuple-element.64.refs_1_.refs_0_, ...), custom_call_target="tpu_custom_call" | custom-call | tf_op jit(solution)/shard_map/pallas_call | solution.py:33
  114.2 6.6 %collective-permute-start.26 = (bf16[64,512]{1,0:T(8,128)(2,1)}, bf16[64,512]{1,0:T(8,128)(2,1)}, u32[]{:S(2)}, u32[]{:S(2)}) collective-permute-start(bf16[64,512]{1,0:T(8,128)(2,1)} %get-tuple-element.105), channel_id=1, source_target_pairs={{0,28},{4,24},{8,20},{12,16},{16,12},{20,8},{24,4},{28,0},{1,29},{... | collective-permute-start | bytes 196616 | tf_op jit(solution)/shard_map/ppermute | solution.py:46
  120.9 1.8 %collective-permute-start.25 = (bf16[64,512]{1,0:T(8,128)(2,1)}, bf16[64,512]{1,0:T(8,128)(2,1)}, u32[]{:S(2)}, u32[]{:S(2)}) collective-permute-start(bf16[64,512]{1,0:T(8,128)(2,1)} %get-tuple-element.103), channel_id=1, source_target_pairs={{0,24},{4,28},{8,16},{12,20},{16,8},{20,12},{24,0},{28,4},{1,25},{... | collective-permute-start | bytes 196616 | tf_op jit(solution)/shard_map/ppermute | solution.py:46
  122.7 1.7 %collective-permute-start.22 = (bf16[64,512]{1,0:T(8,128)(2,1)}, bf16[64,512]{1,0:T(8,128)(2,1)}, u32[]{:S(2)}, u32[]{:S(2)}) collective-permute-start(bf16[64,512]{1,0:T(8,128)(2,1)} %get-tuple-element.97), channel_id=1, source_target_pairs={{0,12},{4,8},{8,4},{12,0},{16,28},{20,24},{24,20},{28,16},{1,13},{... | collective-permute-start | bytes 196616 | tf_op jit(solution)/shard_map/ppermute | solution.py:46
  124.4 1.8 %collective-permute-start.20 = (bf16[64,512]{1,0:T(8,128)(2,1)}, bf16[64,512]{1,0:T(8,128)(2,1)}, u32[]{:S(2)}, u32[]{:S(2)}) collective-permute-start(bf16[64,512]{1,0:T(8,128)(2,1)} %get-tuple-element.93), channel_id=1, source_target_pairs={{0,4},{4,0},{8,12},{12,8},{16,20},{20,16},{24,28},{28,24},{1,5},{5... | collective-permute-start | bytes 196616 | tf_op jit(solution)/shard_map/ppermute | solution.py:46
  126.2 2.6 %collective-permute-start.24 = (bf16[64,512]{1,0:T(8,128)(2,1)}, bf16[64,512]{1,0:T(8,128)(2,1)}, u32[]{:S(2)}, u32[]{:S(2)}) collective-permute-start(bf16[64,512]{1,0:T(8,128)(2,1)} %get-tuple-element.101), channel_id=1, source_target_pairs={{0,20},{4,16},{8,28},{12,24},{16,4},{20,0},{24,12},{28,8},{1,21},{... | collective-permute-start | bytes 196616 | tf_op jit(solution)/shard_map/ppermute | solution.py:46
  129.9 2.5 %shard_map.121.refs_11_ = bf16[16,64,2048]{2,1,0:T(8,128)(2,1)} custom-call(s32[8,8]{1,0:T(8,128)} %refs_0_.9, s32[128]{0:T(128)} %refs_1_.7, bf16[64,2048]{1,0:T(8,128)(2,1)} %get-tuple-element.83.refs_2_, bf16[64,2048]{1,0:T(8,128)(2,1)} %collective-permute-done.11.refs_4_.refs_3_, ...), custom_call_target="tpu_custom_call", output_to_operand_aliasing={{}: (10, {})} | custom-call | tf_op jit(solution)/shard_map/pallas_call | solution.py:437
  132.8 1.8 %collective-permute-done.23.refs_6_ = bf16[64,512]{1,0:T(8,128)(2,1)} collective-permute-done((bf16[64,512]{1,0:T(8,128)(2,1)}, bf16[64,512]{1,0:T(8,128)(2,1)}, u32[]{:S(2)}, u32[]{:S(2)}) %collective-permute-start.23) | collective-permute-done | bytes 65568 | tf_op jit(solution)/shard_map/ppermute | solution.py:46
  134.6 1.9 %shard_map.123 = bf16[16,64,512]{2,1,0:T(8,128)(2,1)} custom-call(s32[8,8]{1,0:T(8,128)} %refs_0_.9, s32[128]{0:T(128)} %refs_1_.7, bf16[64,512]{1,0:T(8,128)(2,1)} %get-tuple-element.91.refs_2_, bf16[64,512]{1,0:T(8,128)(2,1)} %collective-permute-done.20.refs_3_, bf16[64,512]{1,0:T(8,128)(2,1)} %collective-permute-done.21.refs_4_, ...), custom_call_target="tpu_custom_call", output_to_operand_aliasing={{}: (10, {})} | custom-call | tf_op jit(solution)/shard_map/pallas_call | solution.py:437
  (49 shorter events, 20.7 us)
Async XLA Ops:
  3.5 8.9 %collective-permute-start = (bf16[272,128]{1,0:T(8,128)(2,1)}, bf16[272,128]{1,0:T(8,128)(2,1)}, u32[]{:S(2)}, u32[]{:S(2)}) collective-permute-start(bf16[272,128]{1,0:T(8,128)(2,1)} %get-tuple-element.57), channel_id=1, source_target_pairs={{0,4},{4,0},{8,12},{12,8},{16,20},{20,16},{24,28},{28,24},{1,5},{5... | collective-permute-start | bytes 208904 | tf_op jit(solution)/shard_map/ppermute | solution.py:46
  6.5 9.5 %collective-permute-start.1 = (bf16[272,128]{1,0:T(8,128)(2,1)}, bf16[272,128]{1,0:T(8,128)(2,1)}, u32[]{:S(2)}, u32[]{:S(2)}) collective-permute-start(bf16[272,128]{1,0:T(8,128)(2,1)} %get-tuple-element.58), channel_id=1, source_target_pairs={{0,8},{4,12},{8,0},{12,4},{16,24},{20,28},{24,16},{28,20},{1,9},{5... | collective-permute-start | bytes 208904 | tf_op jit(solution)/shard_map/ppermute | solution.py:46
  8.1 11.6 %collective-permute-start.2 = (bf16[272,128]{1,0:T(8,128)(2,1)}, bf16[272,128]{1,0:T(8,128)(2,1)}, u32[]{:S(2)}, u32[]{:S(2)}) collective-permute-start(bf16[272,128]{1,0:T(8,128)(2,1)} %get-tuple-element.59), channel_id=1, source_target_pairs={{0,12},{4,8},{8,4},{12,0},{16,28},{20,24},{24,20},{28,16},{1,13},{... | collective-permute-start | bytes 208904 | tf_op jit(solution)/shard_map/ppermute | solution.py:46
  8.1 11.6 %collective-permute-start.3 = (bf16[272,128]{1,0:T(8,128)(2,1)}, bf16[272,128]{1,0:T(8,128)(2,1)}, u32[]{:S(2)}, u32[]{:S(2)}) collective-permute-start(bf16[272,128]{1,0:T(8,128)(2,1)} %get-tuple-element.60), channel_id=1, source_target_pairs={{0,16},{4,20},{8,24},{12,28},{16,0},{20,4},{24,8},{28,12},{1,17},{... | collective-permute-start | bytes 208904 | tf_op jit(solution)/shard_map/ppermute | solution.py:46
  11.1 11.0 %collective-permute-start.4 = (bf16[272,128]{1,0:T(8,128)(2,1)}, bf16[272,128]{1,0:T(8,128)(2,1)}, u32[]{:S(2)}, u32[]{:S(2)}) collective-permute-start(bf16[272,128]{1,0:T(8,128)(2,1)} %get-tuple-element.61), channel_id=1, source_target_pairs={{0,20},{4,16},{8,28},{12,24},{16,4},{20,0},{24,12},{28,8},{1,21},{... | collective-permute-start | bytes 208904 | tf_op jit(solution)/shard_map/ppermute | solution.py:46
  12.3 9.8 %collective-permute-start.5 = (bf16[272,128]{1,0:T(8,128)(2,1)}, bf16[272,128]{1,0:T(8,128)(2,1)}, u32[]{:S(2)}, u32[]{:S(2)}) collective-permute-start(bf16[272,128]{1,0:T(8,128)(2,1)} %get-tuple-element.62), channel_id=1, source_target_pairs={{0,24},{4,28},{8,16},{12,20},{16,8},{20,12},{24,0},{28,4},{1,25},{... | collective-permute-start | bytes 208904 | tf_op jit(solution)/shard_map/ppermute | solution.py:46
  15.9 7.4 %collective-permute-start.6 = (bf16[272,128]{1,0:T(8,128)(2,1)}, bf16[272,128]{1,0:T(8,128)(2,1)}, u32[]{:S(2)}, u32[]{:S(2)}) collective-permute-start(bf16[272,128]{1,0:T(8,128)(2,1)} %get-tuple-element.63), channel_id=1, source_target_pairs={{0,28},{4,24},{8,20},{12,16},{16,12},{20,8},{24,4},{28,0},{1,29},{... | collective-permute-start | bytes 208904 | tf_op jit(solution)/shard_map/ppermute | solution.py:46
  19.7 8.4 %copy-start = (bf16[256,2,512]{2,1,0:T(2,128)(2,1)S(1)}, bf16[256,2,512]{2,1,0:T(2,128)(2,1)}, u32[]{:S(2)}) copy-start(bf16[256,2,512]{2,1,0:T(2,128)(2,1)} %param.17) | copy-start | bytes 1572868
  23.4 66.0 %all-to-all-start = ((bf16[8,64,2048]{2,1,0:T(8,128)(2,1)}), bf16[8,64,2048]{2,1,0:T(8,128)(2,1)}, u32[]{:S(2)}, u32[]{:S(2)}) async-start(bf16[8,64,2048]{2,1,0:T(8,128)(2,1)} %shard_map.114), calls=%async_computation | async-start | bytes 4194304 | tf_op jit(solution)/shard_map/all_to_all | solution.py:458
  31.6 1.6 %collective-permute-start.7 = (bf16[64,512]{1,0:T(8,128)(2,1)}, bf16[64,512]{1,0:T(8,128)(2,1)}, u32[]{:S(2)}, u32[]{:S(2)}) collective-permute-start(bf16[64,512]{1,0:T(8,128)(2,1)} %get-tuple-element.70), channel_id=1, source_target_pairs={{0,1},{1,0},{2,3},{3,2},{4,5},{5,4},{6,7},{7,6},{8,9},{9,8},{10,11... | collective-permute-start | bytes 196616 | tf_op jit(solution)/shard_map/ppermute | solution.py:46
  34.8 5.7 %collective-permute-start.8 = (bf16[64,512]{1,0:T(8,128)(2,1)}, bf16[64,512]{1,0:T(8,128)(2,1)}, u32[]{:S(2)}, u32[]{:S(2)}) collective-permute-start(bf16[64,512]{1,0:T(8,128)(2,1)} %get-tuple-element.72), channel_id=1, source_target_pairs={{0,2},{1,3},{2,0},{3,1},{4,6},{5,7},{6,4},{7,5},{8,10},{9,11},{10,... | collective-permute-start | bytes 196616 | tf_op jit(solution)/shard_map/ppermute | solution.py:46
  54.7 2.9 %collective-permute-start.9 = (bf16[2,512,512]{2,1,0:T(8,128)(2,1)}, bf16[2,512,512]{2,1,0:T(8,128)(2,1)S(1)}, u32[]{:S(2)}, u32[]{:S(2)}) collective-permute-start(bf16[2,512,512]{2,1,0:T(8,128)(2,1)} %get-tuple-element.75), channel_id=1, source_target_pairs={{0,1},{1,0},{2,3},{3,2},{4,5},{5,4},{6,7},{7,6},{8,9},{9,8},{10,11... | collective-permute-start | bytes 3145736 | tf_op jit(solution)/shard_map/ppermute | solution.py:46
  57.7 3.0 %copy-start.3 = (bf16[64,2048]{1,0:T(8,128)(2,1)S(1)}, bf16[64,2048]{1,0:T(8,128)(2,1)}, u32[]{:S(2)}) copy-start(bf16[64,2048]{1,0:T(8,128)(2,1)} %get-tuple-element.76) | copy-start | bytes 786436
  57.7 5.0 %copy-start.2 = (bf16[64,2048]{1,0:T(8,128)(2,1)S(1)}, bf16[64,2048]{1,0:T(8,128)(2,1)}, u32[]{:S(2)}) copy-start(bf16[64,2048]{1,0:T(8,128)(2,1)} %get-tuple-element.77) | copy-start | bytes 786436
  57.7 6.5 %copy-start.1 = (bf16[64,2048]{1,0:T(8,128)(2,1)S(1)}, bf16[64,2048]{1,0:T(8,128)(2,1)}, u32[]{:S(2)}) copy-start(bf16[64,2048]{1,0:T(8,128)(2,1)} %get-tuple-element.78) | copy-start | bytes 786436
  60.1 35.0 %collective-permute-start.10 = (bf16[512,512]{1,0:T(8,128)(2,1)S(1)}, bf16[512,512]{1,0:T(8,128)(2,1)}, u32[]{:S(2)}, u32[]{:S(2)}) collective-permute-start(bf16[512,512]{1,0:T(8,128)(2,1)S(1)} %get-tuple-element.108), channel_id=1, source_target_pairs={{0,2},{1,3},{2,0},{3,1},{4,6},{5,7},{6,4},{7,5},{8,10},{9,11},{10,... | collective-permute-start | bytes 1572872 | tf_op jit(solution)/shard_map/ppermute | solution.py:46
  60.6 12.6 %collective-permute-start.11 = (bf16[64,2048]{1,0:T(8,128)(2,1)S(1)}, bf16[64,2048]{1,0:T(8,128)(2,1)}, u32[]{:S(2)}, u32[]{:S(2)}) collective-permute-start(bf16[64,2048]{1,0:T(8,128)(2,1)S(1)} %copy-done.3), channel_id=1, source_target_pairs={{0,4},{4,0},{8,12},{12,8},{16,20},{20,16},{24,28},{28,24},{1,5},{5... | collective-permute-start | bytes 786440 | tf_op jit(solution)/shard_map/ppermute | solution.py:46
  62.7 31.0 %collective-permute-start.12 = (bf16[64,2048]{1,0:T(8,128)(2,1)S(1)}, bf16[64,2048]{1,0:T(8,128)(2,1)}, u32[]{:S(2)}, u32[]{:S(2)}) collective-permute-start(bf16[64,2048]{1,0:T(8,128)(2,1)S(1)} %copy-done.2), channel_id=1, source_target_pairs={{0,8},{4,12},{8,0},{12,4},{16,24},{20,28},{24,16},{28,20},{1,9},{5... | collective-permute-start | bytes 786440 | tf_op jit(solution)/shard_map/ppermute | solution.py:46
  64.1 29.5 %collective-permute-start.13 = (bf16[64,2048]{1,0:T(8,128)(2,1)S(1)}, bf16[64,2048]{1,0:T(8,128)(2,1)}, u32[]{:S(2)}, u32[]{:S(2)}) collective-permute-start(bf16[64,2048]{1,0:T(8,128)(2,1)S(1)} %copy-done.1), channel_id=1, source_target_pairs={{0,12},{4,8},{8,4},{12,0},{16,28},{20,24},{24,20},{28,16},{1,13},{... | collective-permute-start | bytes 786440 | tf_op jit(solution)/shard_map/ppermute | solution.py:46
  64.2 47.7 %collective-permute-start.19 = (bf16[64,2048]{1,0:T(8,128)(2,1)}, bf16[64,2048]{1,0:T(8,128)(2,1)}, u32[]{:S(2)}, u32[]{:S(2)}) collective-permute-start(bf16[64,2048]{1,0:T(8,128)(2,1)} %get-tuple-element.89), channel_id=1, source_target_pairs={{0,28},{4,24},{8,20},{12,16},{16,12},{20,8},{24,4},{28,0},{1,29},{... | collective-permute-start | bytes 786440 | tf_op jit(solution)/shard_map/ppermute | solution.py:46
  73.2 47.6 %collective-permute-start.18 = (bf16[64,2048]{1,0:T(8,128)(2,1)}, bf16[64,2048]{1,0:T(8,128)(2,1)}, u32[]{:S(2)}, u32[]{:S(2)}) collective-permute-start(bf16[64,2048]{1,0:T(8,128)(2,1)} %get-tuple-element.88), channel_id=1, source_target_pairs={{0,24},{4,28},{8,16},{12,20},{16,8},{20,12},{24,0},{28,4},{1,25},{... | collective-permute-start | bytes 786440 | tf_op jit(solution)/shard_map/ppermute | solution.py:46
  93.7 30.7 %collective-permute-start.16 = (bf16[64,2048]{1,0:T(8,128)(2,1)}, bf16[64,2048]{1,0:T(8,128)(2,1)}, u32[]{:S(2)}, u32[]{:S(2)}) collective-permute-start(bf16[64,2048]{1,0:T(8,128)(2,1)} %get-tuple-element.85), channel_id=1, source_target_pairs={{0,16},{4,20},{8,24},{12,28},{16,0},{20,4},{24,8},{28,12},{1,17},{... | collective-permute-start | bytes 786440 | tf_op jit(solution)/shard_map/ppermute | solution.py:46
  93.7 30.7 %collective-permute-start.17 = (bf16[64,2048]{1,0:T(8,128)(2,1)}, bf16[64,2048]{1,0:T(8,128)(2,1)}, u32[]{:S(2)}, u32[]{:S(2)}) collective-permute-start(bf16[64,2048]{1,0:T(8,128)(2,1)} %get-tuple-element.87), channel_id=1, source_target_pairs={{0,20},{4,16},{8,28},{12,24},{16,4},{20,0},{24,12},{28,8},{1,21},{... | collective-permute-start | bytes 786440 | tf_op jit(solution)/shard_map/ppermute | solution.py:46
  99.4 1.6 %collective-permute-start.14 = (bf16[64,512]{1,0:T(8,128)(2,1)}, bf16[64,512]{1,0:T(8,128)(2,1)}, u32[]{:S(2)}, u32[]{:S(2)}) collective-permute-start(bf16[64,512]{1,0:T(8,128)(2,1)} %get-tuple-element.80), channel_id=1, source_target_pairs={{0,1},{1,0},{2,3},{3,2},{4,5},{5,4},{6,7},{7,6},{8,9},{9,8},{10,11... | collective-permute-start | bytes 196616 | tf_op jit(solution)/shard_map/ppermute | solution.py:46
  102.5 4.6 %collective-permute-start.15 = (bf16[64,512]{1,0:T(8,128)(2,1)}, bf16[64,512]{1,0:T(8,128)(2,1)}, u32[]{:S(2)}, u32[]{:S(2)}) collective-permute-start(bf16[64,512]{1,0:T(8,128)(2,1)} %get-tuple-element.82), channel_id=1, source_target_pairs={{0,2},{1,3},{2,0},{3,1},{4,6},{5,7},{6,4},{7,5},{8,10},{9,11},{10,... | collective-permute-start | bytes 196616 | tf_op jit(solution)/shard_map/ppermute | solution.py:46
  114.2 11.9 %collective-permute-start.26 = (bf16[64,512]{1,0:T(8,128)(2,1)}, bf16[64,512]{1,0:T(8,128)(2,1)}, u32[]{:S(2)}, u32[]{:S(2)}) collective-permute-start(bf16[64,512]{1,0:T(8,128)(2,1)} %get-tuple-element.105), channel_id=1, source_target_pairs={{0,28},{4,24},{8,20},{12,16},{16,12},{20,8},{24,4},{28,0},{1,29},{... | collective-permute-start | bytes 196616 | tf_op jit(solution)/shard_map/ppermute | solution.py:46
  120.9 7.9 %collective-permute-start.25 = (bf16[64,512]{1,0:T(8,128)(2,1)}, bf16[64,512]{1,0:T(8,128)(2,1)}, u32[]{:S(2)}, u32[]{:S(2)}) collective-permute-start(bf16[64,512]{1,0:T(8,128)(2,1)} %get-tuple-element.103), channel_id=1, source_target_pairs={{0,24},{4,28},{8,16},{12,20},{16,8},{20,12},{24,0},{28,4},{1,25},{... | collective-permute-start | bytes 196616 | tf_op jit(solution)/shard_map/ppermute | solution.py:46
  122.7 9.7 %collective-permute-start.22 = (bf16[64,512]{1,0:T(8,128)(2,1)}, bf16[64,512]{1,0:T(8,128)(2,1)}, u32[]{:S(2)}, u32[]{:S(2)}) collective-permute-start(bf16[64,512]{1,0:T(8,128)(2,1)} %get-tuple-element.97), channel_id=1, source_target_pairs={{0,12},{4,8},{8,4},{12,0},{16,28},{20,24},{24,20},{28,16},{1,13},{... | collective-permute-start | bytes 196616 | tf_op jit(solution)/shard_map/ppermute | solution.py:46
  124.4 8.0 %collective-permute-start.21 = (bf16[64,512]{1,0:T(8,128)(2,1)}, bf16[64,512]{1,0:T(8,128)(2,1)}, u32[]{:S(2)}, u32[]{:S(2)}) collective-permute-start(bf16[64,512]{1,0:T(8,128)(2,1)} %get-tuple-element.95), channel_id=1, source_target_pairs={{0,8},{4,12},{8,0},{12,4},{16,24},{20,28},{24,16},{28,20},{1,9},{5... | collective-permute-start | bytes 196616 | tf_op jit(solution)/shard_map/ppermute | solution.py:46
  124.4 8.0 %collective-permute-start.20 = (bf16[64,512]{1,0:T(8,128)(2,1)}, bf16[64,512]{1,0:T(8,128)(2,1)}, u32[]{:S(2)}, u32[]{:S(2)}) collective-permute-start(bf16[64,512]{1,0:T(8,128)(2,1)} %get-tuple-element.93), channel_id=1, source_target_pairs={{0,4},{4,0},{8,12},{12,8},{16,20},{20,16},{24,28},{28,24},{1,5},{5... | collective-permute-start | bytes 196616 | tf_op jit(solution)/shard_map/ppermute | solution.py:46
  126.2 6.7 %collective-permute-start.24 = (bf16[64,512]{1,0:T(8,128)(2,1)}, bf16[64,512]{1,0:T(8,128)(2,1)}, u32[]{:S(2)}, u32[]{:S(2)}) collective-permute-start(bf16[64,512]{1,0:T(8,128)(2,1)} %get-tuple-element.101), channel_id=1, source_target_pairs={{0,20},{4,16},{8,28},{12,24},{16,4},{20,0},{24,12},{28,8},{1,21},{... | collective-permute-start | bytes 196616 | tf_op jit(solution)/shard_map/ppermute | solution.py:46
  128.7 5.8 %collective-permute-start.23 = (bf16[64,512]{1,0:T(8,128)(2,1)}, bf16[64,512]{1,0:T(8,128)(2,1)}, u32[]{:S(2)}, u32[]{:S(2)}) collective-permute-start(bf16[64,512]{1,0:T(8,128)(2,1)} %get-tuple-element.99), channel_id=1, source_target_pairs={{0,16},{4,20},{8,24},{12,28},{16,0},{20,4},{24,8},{28,12},{1,17},{... | collective-permute-start | bytes 196616 | tf_op jit(solution)/shard_map/ppermute | solution.py:46
